TPU v7x, 32 devices: a whole 2x2x4 slice. The times are simulated.
32 devices in a mesh: ctx: 8 (over z, x), wshard: 4 (over y, core).
Axes of the slice: x: 2, y: 2, z: 4, core: 2. Of those that a mesh axis runs over, the one named last changes fastest.
Arguments:
- inputs: bfloat16 [4096, 2048], P(('ctx', 'wshard')), may hold values from -6 to 6
- span_order: int32 [64], replicated, may hold values from 0 to 63, each once
- attn_gain: bfloat16 [2048], P('wshard'), may hold values from 0.5 to 1.5
- query_weight: bfloat16 [2048, 2048], P('wshard'), may hold values from -0.125 to 0.125
- key_weight: bfloat16 [2048, 512], P('wshard'), may hold values from -0.125 to 0.125
- value_weight: bfloat16 [2048, 512], P('wshard'), may hold values from -0.125 to 0.125
- output_weight: bfloat16 [2048, 2048], P('wshard'), as said below
- ffn_gain: bfloat16 [2048], P('wshard'), may hold values from 0.5 to 1.5
- gate_weight: bfloat16 [2048, 8192], P('wshard'), may hold values from -0.125 to 0.125
- up_weight: bfloat16 [2048, 8192], P('wshard'), may hold values from -0.125 to 0.125
- down_weight: bfloat16 [8192, 2048], P('wshard'), may hold values from -0.0625 to 0.0625
- cotangent: bfloat16 [4096, 2048], P(('ctx', 'wshard')), may hold values from -6 to 6
Outputs:
- outputs: bfloat16 [4096, 2048], P(('ctx', 'wshard'))
- input_grad: float32 [4096, 2048], P(('ctx', 'wshard'))
- attn_gain_grad: float32 [2048], P('wshard')
- query_grad: float32 [2048, 2048], P('wshard')
- key_grad: float32 [2048, 512], P('wshard')
- value_grad: float32 [2048, 512], P('wshard')
- output_grad: float32 [2048, 2048], P('wshard')
- ffn_gain_grad: float32 [2048], P('wshard')
- gate_grad: float32 [2048, 8192], P('wshard')
- up_grad: float32 [2048, 8192], P('wshard')
- down_grad: float32 [8192, 2048], P('wshard')
Inputs may be any that keep to these rules, and one draw needn't show every extreme that they name: `span_order`: every number of 0 to 63 appears once. `output_weight`: independent entries of mean zero.
All inputs are finite; a program needn't handle non-finite values.
Results may differ from a plain program's by a relative error of at most 0.02.
Values may be sent and summed in bfloat16 or wider, within the bound.
No kernel may reach another device: no remote copies, remote signals or barrier semaphores. Data moves between devices by JAX's collectives and lax.ppermute only.
A program may use at most 448 MiB of HBM per device.

v0:
```python
import math

import jax
import jax.numpy as jnp
from jax import lax
from jax.sharding import PartitionSpec as P

H = 32
KVH = 8
HD = 64


epsilon = 1e-05
rope_base = 500000.0
masked_score = -1e30


def rms_scale(vector, scale_gain):
    return (
        vector * lax.rsqrt(jnp.mean(vector * vector, axis=-1, keepdims=True) + epsilon) * scale_gain
    )


def rms_back(vector, scale_gain, gradient):
    inverse = lax.rsqrt(jnp.mean(vector * vector, axis=-1, keepdims=True) + epsilon)
    normed = vector * inverse
    gain_term = jnp.sum(gradient * normed, axis=0)
    scaled = gradient * scale_gain
    return (
        inverse * (scaled - normed * jnp.mean(scaled * normed, axis=-1, keepdims=True)),
        gain_term,
    )


def rotary_tables(positions, width):
    half_width = width // 2
    frequency = jnp.power(rope_base, -jnp.arange(half_width, dtype=jnp.float32) * 2.0 / width)
    angles = positions.astype(jnp.float32)[:, None] * frequency[None, :]
    return (jnp.cos(angles), jnp.sin(angles))


def rotate(vector, cosine, sine):
    half_width = vector.shape[-1] // 2
    first = vector[..., :half_width]
    second = vector[..., half_width:]
    cos_part = cosine[:, None, :]
    sin_part = sine[:, None, :]
    return jnp.concatenate(
        [first * cos_part - second * sin_part, second * cos_part + first * sin_part], axis=-1
    )


def rotate_back(gradient, cosine, sine):
    half_width = gradient.shape[-1] // 2
    first = gradient[..., :half_width]
    second = gradient[..., half_width:]
    cos_part = cosine[:, None, :]
    sin_part = sine[:, None, :]
    return jnp.concatenate(
        [first * cos_part + second * sin_part, second * cos_part - first * sin_part], axis=-1
    )


def span_positions(order_table, offset, amount, tok_dev):
    span_len = tok_dev // 2
    row_ids = offset + jnp.arange(amount, dtype=jnp.int32)
    slot_ids = 2 * (row_ids // tok_dev) + row_ids % tok_dev // span_len
    matches = slot_ids[:, None] == jnp.arange(order_table.shape[0], dtype=jnp.int32)[None, :]
    span_ids = jnp.sum(jnp.where(matches, order_table[None, :], 0), axis=1)
    return span_ids * span_len + row_ids % span_len


def dot_left(left, right):
    return lax.dot_general(
        left, right, (((0,), (0,)), ((), ())), preferred_element_type=jnp.float32
    )


def dot_right(left, right):
    return lax.dot_general(
        left, right, (((1,), (1,)), ((), ())), preferred_element_type=jnp.float32
    )


def local(
    inputs,
    span_order,
    attn_gain,
    query_weight,
    key_weight,
    value_weight,
    output_weight,
    ffn_gain,
    gate_weight,
    up_weight,
    down_weight,
    cotangent,
):
    tok_dev = inputs.shape[0]
    group = H // KVH
    scale = HD ** (-0.5)
    all_tokens = tok_dev * lax.axis_size(("ctx", "wshard"))
    own_index = lax.axis_index(("ctx", "wshard"))
    own_positions = span_positions(span_order, own_index * tok_dev, tok_dev, tok_dev)
    cosine, sine = rotary_tables(own_positions, HD)
    gathered = (
        lax.all_gather(attn_gain, "wshard", axis=0, tiled=True),
        lax.all_gather(ffn_gain, "wshard", axis=0, tiled=True),
        lax.all_gather(query_weight, "wshard", axis=0, tiled=True),
        lax.all_gather(key_weight, "wshard", axis=0, tiled=True),
        lax.all_gather(value_weight, "wshard", axis=0, tiled=True),
        lax.all_gather(output_weight, "wshard", axis=0, tiled=True),
    )
    gain_one = gathered[0].astype(jnp.float32)
    gain_two = gathered[1].astype(jnp.float32)
    query_full, key_full, value_full, output_full = (
        gathered[2],
        gathered[3],
        gathered[4],
        gathered[5],
    )
    floats_in = inputs.astype(jnp.float32)
    normed_one = rms_scale(floats_in, gain_one).astype(jnp.bfloat16)
    query_rows = rotate(
        jnp.dot(normed_one, query_full, preferred_element_type=jnp.float32).reshape(tok_dev, H, HD),
        cosine,
        sine,
    ).astype(jnp.bfloat16)
    key_rows = (
        rotate(
            jnp.dot(normed_one, key_full, preferred_element_type=jnp.float32).reshape(
                tok_dev, KVH, HD
            ),
            cosine,
            sine,
        )
        .astype(jnp.bfloat16)
        .reshape(tok_dev, KVH * HD)
    )
    value_rows = jnp.dot(normed_one, value_full, preferred_element_type=jnp.float32).astype(
        jnp.bfloat16
    )
    queries = query_rows.reshape(tok_dev, KVH, group, HD).transpose(1, 2, 0, 3)
    start_state = (
        jnp.zeros((KVH, group, tok_dev, HD), jnp.float32),
        jnp.full((KVH, group, tok_dev), masked_score, jnp.float32),
        jnp.zeros((KVH, group, tok_dev), jnp.float32),
    )
    carried = start_state
    key_part = lax.all_gather(key_rows, ("ctx", "wshard"), axis=0, tiled=True)
    value_part = lax.all_gather(value_rows, ("ctx", "wshard"), axis=0, tiled=True)
    amount = key_part.shape[0]
    stride = math.gcd(amount, 1024)

    def attend_block(running, counter):
        accum, running_max, running_sum = running
        local_start = counter * stride
        key_block = lax.dynamic_slice_in_dim(key_part, local_start, stride, 0).reshape(
            stride, KVH, HD
        )
        value_block = lax.dynamic_slice_in_dim(value_part, local_start, stride, 0).reshape(
            stride, KVH, HD
        )
        key_pos = span_positions(span_order, local_start, stride, tok_dev)
        scores = (
            jnp.einsum("hgqd,khd->hgqk", queries, key_block, preferred_element_type=jnp.float32)
            * scale
        )
        allowed = key_pos[None, :] <= own_positions[:, None]
        new_max = jnp.maximum(
            running_max, jnp.max(jnp.where(allowed, scores, masked_score), axis=-1)
        )
        shrink = jnp.exp(running_max - new_max)
        weights = jnp.where(allowed, jnp.exp(scores - new_max[..., None]), 0.0)
        running_sum = running_sum * shrink + jnp.sum(weights, axis=-1)
        accum = accum * shrink[..., None] + jnp.einsum(
            "hgqk,khd->hgqd",
            weights.astype(jnp.bfloat16),
            value_block,
            preferred_element_type=jnp.float32,
        )
        return ((accum, new_max, running_sum), None)

    carried, unused = lax.scan(attend_block, carried, jnp.arange(amount // stride, dtype=jnp.int32))
    accum, running_max, running_sum = carried
    attn_float = accum / running_sum[..., None]
    log_total = running_max + jnp.log(running_sum)
    attended = attn_float.transpose(2, 0, 1, 3).reshape(tok_dev, H * HD).astype(jnp.bfloat16)
    residual = floats_in + jnp.dot(attended, output_full, preferred_element_type=jnp.float32)
    gate_full, up_full, down_full = (
        lax.all_gather(gate_weight, "wshard", axis=0, tiled=True),
        lax.all_gather(up_weight, "wshard", axis=0, tiled=True),
        lax.all_gather(down_weight, "wshard", axis=0, tiled=True),
    )
    normed_two = rms_scale(residual, gain_two).astype(jnp.bfloat16)
    gate_pre = jnp.dot(normed_two, gate_full, preferred_element_type=jnp.float32)
    up_pre = jnp.dot(normed_two, up_full, preferred_element_type=jnp.float32)
    hidden = (jax.nn.silu(gate_pre) * up_pre).astype(jnp.bfloat16)
    outputs = (residual + jnp.dot(hidden, down_full, preferred_element_type=jnp.float32)).astype(
        jnp.bfloat16
    )
    grad_out = cotangent.astype(jnp.float32)
    gate_back, up_back, down_back = (
        lax.all_gather(gate_weight, "wshard", axis=0, tiled=True),
        lax.all_gather(up_weight, "wshard", axis=0, tiled=True),
        lax.all_gather(down_weight, "wshard", axis=0, tiled=True),
    )
    hidden_grad = dot_right(cotangent, down_back)
    sigmoid_gate = jax.nn.sigmoid(gate_pre)
    gate_low = (
        hidden_grad * up_pre * sigmoid_gate * (1.0 + gate_pre * (1.0 - sigmoid_gate))
    ).astype(jnp.bfloat16)
    up_low = (hidden_grad * gate_pre * sigmoid_gate).astype(jnp.bfloat16)
    normed_two_grad = dot_right(gate_low, gate_back) + dot_right(up_low, up_back)
    normed_cols, hidden_cols = (
        lax.all_to_all(normed_two, "wshard", split_axis=1, concat_axis=0, tiled=True),
        lax.all_to_all(hidden, "wshard", split_axis=1, concat_axis=0, tiled=True),
    )
    pieces = (
        lax.all_gather(gate_low, "wshard", axis=0, tiled=True),
        lax.all_gather(up_low, "wshard", axis=0, tiled=True),
        lax.all_gather(cotangent, "wshard", axis=0, tiled=True),
    )
    gate_share = dot_left(normed_cols, pieces[0])
    up_share = dot_left(normed_cols, pieces[1])
    down_share = dot_left(hidden_cols, pieces[2])
    residual_part, ffn_gain_term = rms_back(residual, gain_two, normed_two_grad)
    residual_grad = grad_out + residual_part
    gate_share, up_share, down_share = (
        lax.psum(gate_share.astype(jnp.bfloat16), "ctx").astype(jnp.float32),
        lax.psum(up_share.astype(jnp.bfloat16), "ctx").astype(jnp.float32),
        lax.psum(down_share.astype(jnp.bfloat16), "ctx").astype(jnp.float32),
    )
    query_back, key_back, value_back, output_back = (
        lax.all_gather(query_weight, "wshard", axis=0, tiled=True),
        lax.all_gather(key_weight, "wshard", axis=0, tiled=True),
        lax.all_gather(value_weight, "wshard", axis=0, tiled=True),
        lax.all_gather(output_weight, "wshard", axis=0, tiled=True),
    )
    branch_low = residual_grad.astype(jnp.bfloat16)
    attended_grad = dot_right(branch_low, output_back).astype(jnp.bfloat16)
    out_grad = attended_grad.reshape(tok_dev, KVH, group, HD).transpose(1, 2, 0, 3)
    delta = jnp.sum(out_grad.astype(jnp.float32) * attn_float, axis=-1)
    back_state = (
        jnp.zeros((KVH, group, tok_dev, HD), jnp.float32),
        jnp.zeros((all_tokens, KVH * HD), jnp.float32),
        jnp.zeros((all_tokens, KVH * HD), jnp.float32),
    )
    carried = back_state
    back_key_part = lax.all_gather(key_rows, ("ctx", "wshard"), axis=0, tiled=True)
    back_value_part = lax.all_gather(value_rows, ("ctx", "wshard"), axis=0, tiled=True)
    amount = back_key_part.shape[0]
    back_stride = math.gcd(amount, 1024)

    def back_block(running, counter):
        query_acc, key_acc, value_acc = running
        local_start = counter * back_stride
        key_block = lax.dynamic_slice_in_dim(back_key_part, local_start, back_stride, 0).reshape(
            back_stride, KVH, HD
        )
        value_block = lax.dynamic_slice_in_dim(
            back_value_part, local_start, back_stride, 0
        ).reshape(back_stride, KVH, HD)
        key_pos = span_positions(span_order, local_start, back_stride, tok_dev)
        scores = (
            jnp.einsum("hgqd,khd->hgqk", queries, key_block, preferred_element_type=jnp.float32)
            * scale
        )
        allowed = key_pos[None, :] <= own_positions[:, None]
        probs = jnp.where(allowed, jnp.exp(scores - log_total[..., None]), 0.0)
        value_block_grad = jnp.einsum(
            "hgqk,hgqd->khd",
            probs.astype(jnp.bfloat16),
            out_grad,
            preferred_element_type=jnp.float32,
        )
        probs_grad = jnp.einsum(
            "hgqd,khd->hgqk", out_grad, value_block, preferred_element_type=jnp.float32
        )
        score_low = (probs * (probs_grad - delta[..., None])).astype(jnp.bfloat16)
        query_acc = (
            query_acc
            + jnp.einsum("hgqk,khd->hgqd", score_low, key_block, preferred_element_type=jnp.float32)
            * scale
        )
        key_block_grad = (
            jnp.einsum("hgqk,hgqd->khd", score_low, queries, preferred_element_type=jnp.float32)
            * scale
        )
        key_acc = lax.dynamic_update_slice_in_dim(
            key_acc, key_block_grad.reshape(back_stride, KVH * HD), local_start, 0
        )
        value_acc = lax.dynamic_update_slice_in_dim(
            value_acc, value_block_grad.reshape(back_stride, KVH * HD), local_start, 0
        )
        return ((query_acc, key_acc, value_acc), None)

    carried, unused = lax.scan(
        back_block, carried, jnp.arange(amount // back_stride, dtype=jnp.int32)
    )
    query_acc, key_all_grad, value_all_grad = carried
    key_own_grad, value_own_grad = (
        lax.psum_scatter(key_all_grad, ("ctx", "wshard"), scatter_dimension=0, tiled=True),
        lax.psum_scatter(value_all_grad, ("ctx", "wshard"), scatter_dimension=0, tiled=True),
    )
    query_low = (
        rotate_back(query_acc.transpose(2, 0, 1, 3).reshape(tok_dev, H, HD), cosine, sine)
        .reshape(tok_dev, H * HD)
        .astype(jnp.bfloat16)
    )
    key_low = (
        rotate_back(key_own_grad.reshape(tok_dev, KVH, HD), cosine, sine)
        .reshape(tok_dev, KVH * HD)
        .astype(jnp.bfloat16)
    )
    value_low = value_own_grad.astype(jnp.bfloat16)
    normed_one_grad = (
        dot_right(query_low, query_back)
        + dot_right(key_low, key_back)
        + dot_right(value_low, value_back)
    )
    input_part, attn_gain_term = rms_back(floats_in, gain_one, normed_one_grad)
    input_grad = residual_grad + input_part
    first_cols, attended_cols = (
        lax.all_to_all(normed_one, "wshard", split_axis=1, concat_axis=0, tiled=True),
        lax.all_to_all(attended, "wshard", split_axis=1, concat_axis=0, tiled=True),
    )
    pieces = (
        lax.all_gather(query_low, "wshard", axis=0, tiled=True),
        lax.all_gather(key_low, "wshard", axis=0, tiled=True),
        lax.all_gather(value_low, "wshard", axis=0, tiled=True),
        lax.all_gather(branch_low, "wshard", axis=0, tiled=True),
    )
    query_share = dot_left(first_cols, pieces[0])
    key_share = dot_left(first_cols, pieces[1])
    value_share = dot_left(first_cols, pieces[2])
    output_share = dot_left(attended_cols, pieces[3])
    gain_shares = lax.psum_scatter(
        jnp.stack([attn_gain_term, ffn_gain_term]), "wshard", scatter_dimension=1, tiled=True
    )
    attn_shares = (
        gain_shares[0],
        gain_shares[1],
        query_share,
        key_share,
        value_share,
        output_share,
    )
    attn_shares = (
        lax.psum(attn_shares[0].astype(jnp.bfloat16), "ctx").astype(jnp.float32),
        lax.psum(attn_shares[1].astype(jnp.bfloat16), "ctx").astype(jnp.float32),
        lax.psum(attn_shares[2].astype(jnp.bfloat16), "ctx").astype(jnp.float32),
        lax.psum(attn_shares[3].astype(jnp.bfloat16), "ctx").astype(jnp.float32),
        lax.psum(attn_shares[4].astype(jnp.bfloat16), "ctx").astype(jnp.float32),
        lax.psum(attn_shares[5].astype(jnp.bfloat16), "ctx").astype(jnp.float32),
    )
    gain_one_grad, gain_two_grad, query_grad, key_grad, value_grad, output_grad = attn_shares
    return (
        outputs,
        input_grad,
        gain_one_grad,
        query_grad,
        key_grad,
        value_grad,
        output_grad,
        gain_two_grad,
        gate_share,
        up_share,
        down_share,
    )


def solution(mesh):
    in_specs = (
        P(("ctx", "wshard"), None),
        P(),
        P("wshard"),
        P("wshard", None),
        P("wshard", None),
        P("wshard", None),
        P("wshard", None),
        P("wshard"),
        P("wshard", None),
        P("wshard", None),
        P("wshard", None),
        P(("ctx", "wshard"), None),
    )
    out_specs = (
        P(("ctx", "wshard"), None),
        P(("ctx", "wshard"), None),
        P("wshard"),
        P("wshard", None),
        P("wshard", None),
        P("wshard", None),
        P("wshard", None),
        P("wshard"),
        P("wshard", None),
        P("wshard", None),
        P("wshard", None),
    )
    return jax.shard_map(local, mesh=mesh, in_specs=in_specs, out_specs=out_specs, check_vma=False)
```

profile of v0, /device:TPU:0, one launch (start us, length us, event | category | flops | bytes accessed | tf_op | source)
XLA Modules:
  0.0 2674.6 jit_solution(3032577523685150928)
XLA Ops:
  18.6 16.3 all-gather.23.cloned.1.call-done
  39.2 19.9 all-gather.17.cloned.1.call-done
  71.6 53.0 %all-gather.25.cloned.1.call-done = bf16[4096,512]{1,0:T(8,128)(2,1)} async-done(((bf16[128,512]{1,0:T(8,128)(2,1)}), bf16[4096,512]{1,0:T(8,128)(2,1)}) %all-gather.25.cloned.1.call-update) | async-done | bytes 4194320 | tf_op jit(solution)/shard_map/all_gather | solution.py:151
  130.9 52.0 %all-gather.21.cloned.1.call-done = bf16[2048,2048]{1,0:T(8,128)(2,1)} async-done(((bf16[512,2048]{1,0:T(8,128)(2,1)}), bf16[2048,2048]{1,0:T(8,128)(2,1)}) %all-gather.21.cloned.1.call-update) | async-done | bytes 8388624 | tf_op jit(solution)/shard_map/all_gather | solution.py:109
  189.9 61.6 %all-gather.19.cloned.1.call-done = bf16[4096,512]{0,1:T(8,128)(2,1)} async-done(((bf16[128,512]{0,1:T(8,128)(2,1)}), bf16[4096,512]{0,1:T(8,128)(2,1)}) %all-gather.19.cloned.1.call-update) | async-done | bytes 4194320 | tf_op jit(solution)/shard_map/all_gather | solution.py:150
  251.6 118.8 %while.36 = (s32[]{:T(128)}, f32[8,4,128,64]{2,3,1,0:T(8,128)S(1)}, f32[8,4,128]{2,1,0:T(4,128)S(1)}, f32[8,4,128]{2,1,0:T(4,128)S(1)}, s32[4]{0:T(128)S(1)}, /*...) while((s32[]{:T(128)}, f32[8,4,128,64]{2,3,1,0:T(8,128)S(1)}, ...), condition=%wide.region_6.7_spmd.clone, body=%wide.region_2.6_spmd.clone.sunk | while | flops 1121064960 | bytes 60056532 | solution.py:184
  254.9 9.4 fusion.159
  264.3 9.1 fusion.160
  273.4 7.5 fusion.162
  284.3 7.5 fusion.159
  291.8 9.1 fusion.160
  300.9 7.5 fusion.162
  311.8 9.0 fusion.159
  320.8 12.8 fusion.160
  333.6 8.9 fusion.162
  353.4 9.4 fusion.160
  378.6 134.0 %all-gather.29.cloned.1.call-done = bf16[2048,8192]{1,0:T(8,128)(2,1)} async-done(((bf16[512,8192]{1,0:T(8,128)(2,1)}), bf16[2048,8192]{1,0:T(8,128)(2,1)}) %all-gather.29.cloned.1.call-update) | async-done | bytes 33554448 | tf_op jit(solution)/shard_map/all_gather | solution.py:191
  512.6 20.5 fusion.69
  533.1 182.6 %all-gather.31.cloned.1.call-done = bf16[2048,8192]{1,0:T(8,128)(2,1)} async-done(((bf16[512,8192]{1,0:T(8,128)(2,1)}), bf16[2048,8192]{1,0:T(8,128)(2,1)}) %all-gather.31.cloned.1.call-update) | async-done | bytes 33554448 | tf_op jit(solution)/shard_map/all_gather | solution.py:192
  715.7 20.5 fusion.70
  736.2 182.6 %all-gather.33.cloned.1.call-done = bf16[8192,2048]{1,0:T(8,128)(2,1)} async-done(((bf16[2048,2048]{1,0:T(8,128)(2,1)}), bf16[8192,2048]{1,0:T(8,128)(2,1)}) %all-gather.33.cloned.1.call-update) | async-done | bytes 33554448 | tf_op jit(solution)/shard_map/all_gather | solution.py:193
  918.8 20.6 multiply_convert_fusion
  939.4 17.3 fusion.71
  956.7 17.5 multiply_reduce_fusion
  993.7 192.1 %while.37 = (s32[]{:T(128)}, f32[8,4,128,64]{2,3,1,0:T(8,128)S(1)}, f32[4096,512]{0,1:T(8,128)}, f32[4096,512]{0,1:T(8,128)}, s32[4]{0:T(128)}, /*index=5*/s32[6...) while((s32[]{:T(128)}, f32[8,4,128,64]{2,3,1,0:T(8,128)S(1)}, ...), condition=%wide.region_12.13_spmd.clone, body=%wide.region_10.12_spmd.clone.sunk | while | flops 2727987200 | bytes 171385936 | solution.py:298
  1005.2 9.2 fusion.176
  1021.8 10.3 fusion.178
  1053.2 9.2 fusion.176
  1069.7 10.3 fusion.178
  1101.1 9.2 fusion.176
  1117.7 10.3 fusion.178
  1149.0 9.2 fusion.176
  1165.6 10.3 fusion.178
  1197.3 13.0 all-to-all-done
  1223.3 28.6 %all-to-all-done.3 = bf16[128,4,2048]{2,0,1:T(8,128)(2,1)} async-done(((bf16[128,4,2048]{2,0,1:T(8,128)(2,1)}), bf16[128,4,2048]{2,0,1:T(8,128)(2,1)}, u32[]{:S(2)}, u32[]{:S(2)}) %all-to-all-start.3) | async-done | bytes 2097184 | tf_op jit(solution)/shard_map/all_to_all | solution.py:217
  1255.5 11.4 convolution_convert_fusion.2
  1285.1 33.2 %all-gather.41.cloned.1.call-done = bf16[512,8192]{1,0:T(8,128)(2,1)} async-done(((bf16[128,8192]{1,0:T(8,128)(2,1)}), bf16[512,8192]{1,0:T(8,128)(2,1)}) %all-gather.41.cloned.1.call-update) | async-done | bytes 8388624 | tf_op jit(solution)/shard_map/all_gather | solution.py:221
  1318.3 10.4 convolution_convert_fusion
  1328.7 49.3 %all-gather.39.cloned.1.call-done = bf16[512,8192]{1,0:T(8,128)(2,1)} async-done(((bf16[128,8192]{1,0:T(8,128)(2,1)}), bf16[512,8192]{1,0:T(8,128)(2,1)}) %all-gather.39.cloned.1.call-update) | async-done | bytes 8388624 | tf_op jit(solution)/shard_map/all_gather | solution.py:220
  1378.0 10.2 convolution_convert_fusion.1
  1388.2 141.6 %reduce-scatter.6.cloned.1.call-done = f32[128,512]{0,1:T(8,128)} async-done(((f32[4096,512]{0,1:T(8,128)}), f32[128,512]{0,1:T(8,128)}) %reduce-scatter.6.cloned.1.call-update) | async-done | bytes 262160 | tf_op jit(solution)/shard_map/reduce_scatter | solution.py:303
  1539.7 137.7 %reduce-scatter.8.cloned.1.call-done = f32[128,512]{0,1:T(8,128)} async-done(((f32[4096,512]{0,1:T(8,128)}), f32[128,512]{0,1:T(8,128)}) %reduce-scatter.8.cloned.1.call-update) | async-done | bytes 262160 | tf_op jit(solution)/shard_map/reduce_scatter | solution.py:304
  1695.2 17.0 fusion.48
  1714.9 21.3 all-reduce
  1737.3 887.6 %all-reduce.4.cloned.1.call-done = (bf16[512,2048]{1,0:T(8,128)(2,1)}, bf16[512,512]{1,0:T(8,128)(2,1)}, bf16[512,512]{1,0:T(8,128)(2,1)}, bf16[512,2048]{1,0:T(...) async-done(((bf16[512,2048]{1,0:T(8,128)(2,1)}, bf16[512,512]{1,0:T(8,128)(2,1)}, bf16[512,512]{1,0:T(8,128)(2,1)}, ...) | async-done | bytes 30408720 | tf_op jit(solution)/shard_map/psum | solution.py:352
  2624.9 11.7 convert_element_type.194
  2636.7 11.7 convert_element_type.196
  2648.4 11.8 convert_element_type.198
  (301 shorter events, 289.9 us)
Async XLA Ops:
  7.2 27.7 %all-gather.23.cloned.1.call-start = ((), (), s32[]{:S(2)}) async-start(), calls=%async_computation.10 | async-start | bytes 2621440 | tf_op jit(solution)/shard_map/all_gather | solution.py:111
  7.9 51.2 %all-gather.17.cloned.1.call-start = ((), (), s32[]{:S(2)}) async-start(), calls=%async_computation.7 | async-start | bytes 2621440 | tf_op jit(solution)/shard_map/all_gather | solution.py:110
  8.7 115.9 %all-gather.25.cloned.1.call-start = ((), (), s32[]{:S(2)}) async-start(), calls=%async_computation.11 | async-start | bytes 4325376 | tf_op jit(solution)/shard_map/all_gather | solution.py:151
  18.6 164.3 %copy-start.6 = (bf16[128,2048]{1,0:T(8,128)(2,1)}, bf16[128,2048]{1,0:T(8,128)(2,1)S(1)}, u32[]{:S(2)}) copy-start(bf16[128,2048]{1,0:T(8,128)(2,1)S(1)} %fusion.53) | copy-start | bytes 1572868
  37.6 145.3 %all-gather.21.cloned.1.call-start = ((), (), s32[]{:S(2)}) async-start(), calls=%async_computation.9 | async-start | bytes 10485760 | tf_op jit(solution)/shard_map/all_gather | solution.py:109
  38.2 213.4 %all-gather.19.cloned.1.call-start = ((), (), s32[]{:S(2)}) async-start(), calls=%async_computation.8 | async-start | bytes 4325376 | tf_op jit(solution)/shard_map/all_gather | solution.py:150
  39.2 150.5 %copy-start.25 = (f32[128,32]{0,1:T(8,128)}, f32[128,32]{0,1:T(8,128)S(1)}, u32[]{:S(2)}) copy-start(f32[128,32]{0,1:T(8,128)S(1)} %get-tuple-element.650) | copy-start | bytes 49156
  39.2 150.5 %copy-start.27 = (f32[128,32]{0,1:T(8,128)}, f32[128,32]{0,1:T(8,128)S(1)}, u32[]{:S(2)}) copy-start(f32[128,32]{0,1:T(8,128)S(1)} %get-tuple-element.651) | copy-start | bytes 49156
  62.3 310.4 %all-gather.27.cloned.1.call-start = ((), (), s32[]{:S(2)}) async-start(), calls=%async_computation.12 | async-start | bytes 10485760 | tf_op jit(solution)/shard_map/all_gather | solution.py:112
  62.9 449.7 %all-gather.29.cloned.1.call-start = ((), (), s32[]{:S(2)}) async-start(), calls=%async_computation.13 | async-start | bytes 41943040 | tf_op jit(solution)/shard_map/all_gather | solution.py:191
  63.7 652.0 %all-gather.31.cloned.1.call-start = ((), (), s32[]{:S(2)}) async-start(), calls=%async_computation.14 | async-start | bytes 41943040 | tf_op jit(solution)/shard_map/all_gather | solution.py:192
  64.4 854.4 %all-gather.33.cloned.1.call-start = ((), (), s32[]{:S(2)}) async-start(), calls=%async_computation.15 | async-start | bytes 41943040 | tf_op jit(solution)/shard_map/all_gather | solution.py:193
  65.2 1190.3 %all-gather.43.cloned.1.call-start = ((), (), s32[]{:S(2)}) async-start(), calls=%async_computation.22 | async-start | bytes 2621440 | tf_op jit(solution)/shard_map/all_gather | solution.py:222
  65.7 1204.6 %all-gather.35.cloned.1.call-start = ((), (), s32[]{:S(2)}) async-start(), calls=%async_computation.18 | async-start | bytes 2621440 | tf_op jit(solution)/shard_map/all_gather | solution.py:329
  71.6 902.7 %copy-start.29 = (f32[4,1,512]{2,1,0:T(1,128)}, f32[4,1,512]{2,1,0:T(1,128)S(1)}, u32[]{:S(2)}) copy-start(f32[4,1,512]{2,1,0:T(1,128)S(1)} %convert_element_type.200) | copy-start | bytes 24580
  130.9 120.6 %copy-start.33 = (s32[64]{0:T(128)S(1)}, s32[64]{0:T(128)}, u32[]{:S(2)}) copy-start(s32[64]{0:T(128)} %param.17) | copy-start | bytes 772
  251.6 121.2 %copy-start.4 = (bf16[128,2048]{1,0:T(8,128)(2,1)S(1)}, bf16[128,2048]{1,0:T(8,128)(2,1)}, u32[]{:S(2)}) copy-start(bf16[128,2048]{1,0:T(8,128)(2,1)} %param.16) | copy-start | bytes 1572868
  377.6 596.6 %copy-start.2 = (f32[128,2048]{1,0:T(8,128)}, f32[128,2048]{1,0:T(8,128)S(1)}, u32[]{:S(2)}) copy-start(f32[128,2048]{1,0:T(8,128)S(1)} %get-tuple-element.653) | copy-start | bytes 3145732
  377.7 596.6 %copy-start.35 = (f32[128]{0:T(128)}, f32[128]{0:T(128)S(1)}, u32[]{:S(2)}) copy-start(f32[128]{0:T(128)S(1)} %add_rsqrt_fusion) | copy-start | bytes 1540
  378.5 337.2 %copy-start.11 = (bf16[128,2048]{1,0:T(8,128)(2,1)}, bf16[128,2048]{1,0:T(8,128)(2,1)S(1)}, u32[]{:S(2)}) copy-start(bf16[128,2048]{1,0:T(8,128)(2,1)S(1)} %multiply_convert_fusion.3) | copy-start | bytes 1572868
  533.1 385.7 %copy-start.15 = (bf16[128,2048]{1,0:T(8,128)(2,1)S(1)}, bf16[128,2048]{1,0:T(8,128)(2,1)}, u32[]{:S(2)}) copy-start(bf16[128,2048]{1,0:T(8,128)(2,1)} %param.27) | copy-start | bytes 1572868
  974.3 15.1 copy-start.39
  993.7 192.1 %copy-start.26 = (f32[128,32]{0,1:T(8,128)S(1)}, f32[128,32]{0,1:T(8,128)}, u32[]{:S(2)}) copy-start(f32[128,32]{0,1:T(8,128)} %copy-done.25) | copy-start | bytes 49156
  1047.7 14.7 copy-start
  1143.6 14.7 copy-start
  1187.7 87.1 %all-gather.37.cloned.1.call-start = ((), (), s32[]{:S(2)}) async-start(), calls=%async_computation.19 | async-start | bytes 2621440 | tf_op jit(solution)/shard_map/all_gather | solution.py:332
  1188.2 130.0 %all-gather.41.cloned.1.call-start = ((), (), s32[]{:S(2)}) async-start(), calls=%async_computation.21 | async-start | bytes 10485760 | tf_op jit(solution)/shard_map/all_gather | solution.py:221
  1189.0 189.0 %all-gather.39.cloned.1.call-start = ((), (), s32[]{:S(2)}) async-start(), calls=%async_computation.20 | async-start | bytes 10485760 | tf_op jit(solution)/shard_map/all_gather | solution.py:220
  1189.6 340.3 %reduce-scatter.6.cloned.1.call-start = ((), (), s32[]{:S(2)}) async-start(), calls=%async_computation.16 | async-start | bytes 8650752 | tf_op jit(solution)/shard_map/reduce_scatter | solution.py:303
  1190.1 487.2 %reduce-scatter.8.cloned.1.call-start = ((), (), s32[]{:S(2)}) async-start(), calls=%async_computation.17 | async-start | bytes 8650752 | tf_op jit(solution)/shard_map/reduce_scatter | solution.py:304
  1190.2 25.8 copy-start.12
  1191.6 23.4 copy-start.14
  1191.6 18.8 all-to-all-start
  1210.3 41.6 %all-to-all-start.3 = ((bf16[128,4,2048]{2,0,1:T(8,128)(2,1)}), bf16[128,4,2048]{2,0,1:T(8,128)(2,1)}, u32[]{:S(2)}, u32[]{:S(2)}) async-start(bf16[128,4,2048]{2,0,1:T(8,128)(2,1)} %bitcast.235), calls=%async_computation.5 | async-start | bytes 4194304 | tf_op jit(solution)/shard_map/all_to_all | solution.py:217
  1252.0 14.9 all-to-all-start.1
  1266.8 18.2 all-to-all-start.2
  1270.3 443.5 %reduce-scatter.10.cloned.1.call-start = ((), (), s32[]{:S(2)}) async-start(), calls=%async_computation.23 | async-start | bytes 1310720
  1328.7 201.1 %copy-start.28 = (f32[128,32]{0,1:T(8,128)S(1)}, f32[128,32]{0,1:T(8,128)}, u32[]{:S(2)}) copy-start(f32[128,32]{0,1:T(8,128)} %copy-done.27) | copy-start | bytes 49156
  1328.7 358.6 %copy-start.32 = (f32[4,1,512]{2,1,0:T(1,128)S(1)}, f32[4,1,512]{2,1,0:T(1,128)}, u32[]{:S(2)}) copy-start(f32[4,1,512]{2,1,0:T(1,128)} %copy-done.31) | copy-start | bytes 24580
  1328.7 358.6 %copy-start.38 = (f32[128]{0:T(128)S(1)}, f32[128]{0:T(128)}, u32[]{:S(2)}) copy-start(f32[128]{0:T(128)} %copy-done.37) | copy-start | bytes 1540
  1388.2 299.1 %copy-start.5 = (bf16[128,2048]{1,0:T(8,128)(2,1)S(1)}, bf16[128,2048]{1,0:T(8,128)(2,1)}, u32[]{:S(2)}) copy-start(bf16[128,2048]{1,0:T(8,128)(2,1)} %param.16) | copy-start | bytes 1572868
  1388.2 301.7 %copy-start.34 = (f32[2048]{0:T(1024)S(1)}, f32[2048]{0:T(1024)}, u32[]{:S(2)}) copy-start(f32[2048]{0:T(1024)} %get-tuple-element.568) | copy-start | bytes 24580
  1691.3 933.6 %all-reduce.4.cloned.1.call-start = ((), (), s32[]{:S(2)}) async-start(), calls=%async_computation.24 | async-start | bytes 60817408 | tf_op jit(solution)/shard_map/psum | solution.py:352
  1695.1 17.0 copy-start.10
  1695.1 17.0 copy-start.16
  1695.1 17.0 copy-start.30
  1695.1 17.0 copy-start.36
  1695.2 17.0 copy-start.40
  (25 other events, 142.6 us)
Sparse Core Ops, SparseCore 0:
  9.6 25.2 all-gather.22
  36.5 22.5 all-gather.16
  62.5 62.0 all-gather.24
  126.0 56.8 all-gather.20
  186.1 65.3 all-gather.18
  253.0 56.4 all-gather.26
  311.0 201.5 all-gather.28
  514.1 201.5 all-gather.30
  717.3 201.5 all-gather.32
  920.3 22.5 all-gather.42
  1187.8 29.4 all-gather.34
  1218.7 33.9 all-gather.36
  1254.3 63.8 all-gather.40
  1319.7 58.2 all-gather.38
  1380.7 149.0 reduce-scatter.5
  1532.5 144.7 reduce-scatter.7
  1691.4 21.8 reduce-scatter.9
  1721.3 903.5 all-reduce.3
where the time goes:
time: 2680 us; the launch traced here: 2670 us
  waiting for transfers between devices  2010 us (75%)
  matrix products  396 us (15%)
  other arithmetic  107 us (4%)
  local copies, waits for them, and re-layouts  80.5 us (3%)
  blocking collectives  46.1 us (2%)
    psum x1, waiting for transfers between devices, local(): lax.psum(attn_shares[2].astype(jnp.bfloat16), 'ctx').astype(jnp.float32)  888 us
    all_gather x1, waiting for transfers between devices, local(): lax.all_gather(down_weight, 'wshard', axis=0, tiled=True)  183 us
    all_gather x1, waiting for transfers between devices, local(): lax.all_gather(up_weight, 'wshard', axis=0, tiled=True)  183 us
    reduce_scatter x1, waiting for transfers between devices, local(): lax.psum_scatter(key_all_grad, ('ctx', 'wshard'), scatter_dimension=0, ti...  142 us
    reduce_scatter x1, waiting for transfers between devices, local(): lax.psum_scatter(value_all_grad, ('ctx', 'wshard'), scatter_dimension=0,...  138 us
    all_gather x1, waiting for transfers between devices, local(): lax.all_gather(gate_weight, 'wshard', axis=0, tiled=True)  134 us
    dot_general x7, matrix products, dot_right(): lax.dot_general(left, right, (((1,), (1,)), ((), ())), preferred_element_...  73.3 us
    all_gather x1, waiting for transfers between devices, local(): key_part = lax.all_gather(key_rows, ('ctx', 'wshard'), axis=0, tiled=True)  61.6 us
  transfers between devices with their start and end apart: 22, of which 16 were waited for; matrix products, arithmetic and copies ran while one was open for 20% of the time, Pallas kernels for 0%

commit v1 on v0

v1 whole, which is shorter than its diff:
```python
import functools

import jax
import jax.numpy as jnp
from jax import lax
from jax.experimental import pallas as pl
from jax.experimental.pallas import tpu as pltpu
from jax.sharding import Mesh
from jax.sharding import PartitionSpec as P

H = 32
KVH = 8
HD = 64
GROUP = H // KVH

epsilon = 1e-05
rope_base = 500000.0
masked_score = -1e30
f32 = jnp.float32
bf16 = jnp.bfloat16


def rotary_tables(positions, width):
    half_width = width // 2
    frequency = jnp.power(rope_base, -jnp.arange(half_width, dtype=f32) * 2.0 / width)
    angles = frequency[:, None] * positions.astype(f32)[None, :]
    return (jnp.cos(angles), jnp.sin(angles))


def rotate(vector, cosine, sine):
    half_width = vector.shape[-2] // 2
    first = vector[..., :half_width, :]
    second = vector[..., half_width:, :]
    return jnp.concatenate(
        [first * cosine - second * sine, second * cosine + first * sine], axis=-2
    )


def contract(left, right, left_dim, right_dim):
    return lax.dot_general(
        left, right, (((left_dim,), (right_dim,)), ((), ())), preferred_element_type=f32
    )


SLAB = ("xpart", "wshard")


def swap(value, flip):
    return lax.ppermute(value, SLAB, [(i, i ^ flip) for i in range(KVH)])


FLIPS = (0, 2, 4, 6, 1, 3, 5, 7)


def slab_gather(block):
    half = block.shape[0] // 2
    row = swap(block, 2)
    column = swap(block, 4)
    far = jnp.concatenate([swap(row[:half], 4), swap(column[half:], 2)], axis=0)
    near = [block, row, column, far]
    return jnp.concatenate(near + [swap(v, 1) for v in near], axis=0)


def slab_reduce(partial):
    rows = partial.shape[0] // KVH
    half = partial.shape[1] // 2
    partial = partial.reshape(KVH, rows, 2 * half)
    own = partial[:4] + swap(partial[4:].astype(bf16), 1).astype(f32)
    left, right = own[..., :half], own[..., half:]
    left = left[:2] + swap(left[2:].astype(bf16), 4).astype(f32)
    right = right[0::2] + swap(right[1::2].astype(bf16), 2).astype(f32)
    left = left[0] + swap(left[1].astype(bf16), 2).astype(f32)
    right = right[0] + swap(right[1].astype(bf16), 4).astype(f32)
    return jnp.concatenate([left, right], axis=1)


def line_reduce(parts):
    count = parts.shape[0]
    place = lax.axis_index("line")

    def pick(index):
        return lax.dynamic_index_in_dim(
            parts, jnp.clip(index, 0, count - 1), 0, keepdims=False
        )

    up = pick(place * 0 + count - 1)
    down = pick(place * 0)
    for step in range(1, count):
        up_got = lax.ppermute(up, "line", [(i, i + 1) for i in range(step)])
        down_got = lax.ppermute(
            down, "line", [(count - 1 - i, count - 2 - i) for i in range(step)]
        )
        if step < count - 1:
            up = (pick(count - 1 - step + place).astype(f32) + up_got.astype(f32)).astype(bf16)
            down = (pick(place - (count - 1 - step)).astype(f32) + down_got.astype(f32)).astype(
                bf16
            )
    return pick(place).astype(f32) + (up_got.astype(f32) + down_got.astype(f32))


def line_gather(own):
    count = lax.axis_size("line")
    place = lax.axis_index("line")
    ups, downs = [own], [own]
    for step in range(1, count):
        ups.append(lax.ppermute(ups[-1], "line", [(i, i + 1) for i in range(step - 1, count - 1)]))
        downs.append(
            lax.ppermute(downs[-1], "line", [(i + 1, i) for i in range(0, count - step)])
        )
    return [own] + [
        jnp.where(place + k < count, downs[k], ups[count - k]) for k in range(1, count)
    ]


def place_kernel(spots_ref, *refs):
    out_ref = refs[-1]
    halves = spots_ref.shape[0] - 1
    columns = refs[0].shape[-1]
    for turn in range(halves):
        for spot in range(halves):

            @pl.when(spots_ref[1 + turn] == spot)
            def put(turn=turn, spot=spot):
                out_ref[:, spot * columns : (spot + 1) * columns] = refs[turn][0].astype(f32)


def place_columns(total, pieces, spot, sides, count):
    shards, rows, columns = pieces[0].shape
    halves = len(pieces)
    operands = [jnp.stack([spot] + sides).astype(jnp.int32)] + list(pieces)
    specs = [pl.BlockSpec((1, rows, columns), lambda w, spots: (w, 0, 0))] * halves
    aliases = {}
    if total is not None:
        aliases = {len(operands): 0}
        operands.append(total)
        specs.append(pl.BlockSpec(memory_space=pl.ANY))
    return pl.pallas_call(
        place_kernel,
        grid_spec=pltpu.PrefetchScalarGridSpec(
            num_scalar_prefetch=1,
            grid=(shards,),
            in_specs=specs,
            out_specs=pl.BlockSpec((rows, halves * columns), lambda w, spots: (spots[0], w)),
        ),
        out_shape=jax.ShapeDtypeStruct((count * rows, shards * halves * columns), f32),
        input_output_aliases=aliases,
        compiler_params=pltpu.CompilerParams(vmem_limit_bytes=32 * 1024 * 1024),
        cost_estimate=pl.CostEstimate(
            flops=0, transcendentals=0, bytes_accessed=6 * halves * shards * rows * columns
        ),
        name="place_columns",
    )(*operands)


def place_rows(total, pieces, spot, sides, count):
    rows, columns = pieces[0].shape
    halves = len(pieces)
    for piece, side in zip(pieces, sides):
        operands = [jnp.stack([side * count + spot, side * 0]).astype(jnp.int32), piece[None]]
        width = min(columns, 1024)
        specs = [pl.BlockSpec((1, rows, width), lambda w, spots: (0, 0, w))]
        aliases = {}
        if total is not None:
            aliases = {2: 0}
            operands.append(total)
            specs.append(pl.BlockSpec(memory_space=pl.ANY))
        total = pl.pallas_call(
            place_kernel,
            grid_spec=pltpu.PrefetchScalarGridSpec(
                num_scalar_prefetch=1,
                grid=(columns // width,),
                in_specs=specs,
                out_specs=pl.BlockSpec((rows, width), lambda w, spots: (spots[0], w)),
            ),
            out_shape=jax.ShapeDtypeStruct((halves * count * rows, columns), f32),
            input_output_aliases=aliases,
            compiler_params=pltpu.CompilerParams(vmem_limit_bytes=32 * 1024 * 1024),
            cost_estimate=pl.CostEstimate(
                flops=0, transcendentals=0, bytes_accessed=6 * rows * columns
            ),
            name="place_rows",
        )(*operands)
    return total


def place_narrow(total, pieces, spot, sides, count):
    shards, rows, columns = pieces[0].shape
    halves = len(pieces)
    ordered = [pieces[0]]
    if halves == 2:
        ordered = [jnp.where(sides[0] == t, pieces[0], pieces[1]) for t in range(2)]
    block = jnp.concatenate(
        [ordered[t][w] for w in range(shards) for t in range(halves)], axis=1
    ).astype(f32)
    if total is None:
        total = jnp.zeros((count * rows, block.shape[1]), f32)
    return lax.dynamic_update_slice(total, block, (spot * rows, 0))


def spread(own, places):
    count, halves = lax.axis_size("line"), lax.axis_size("xpart")
    place, side = lax.axis_index("line"), lax.axis_index("xpart")
    totals = [None] * len(places)
    sides = [lax.rem(side + halves - turn, halves) for turn in range(halves)]
    for k, block in enumerate(line_gather(own)):
        spot = lax.rem(place + k, count)
        pieces = [block] + [
            lax.ppermute(block, "xpart", [(i, (i + turn) % halves) for i in range(halves)])
            for turn in range(1, halves)
        ]
        totals = [
            put(total, [part(piece) for piece in pieces], spot, sides, count)
            for total, (put, part) in zip(totals, places)
        ]
    return totals


def whole_block(block):
    return block


def spread_rows(reduced):
    return spread(reduced.astype(bf16), [(place_rows, whole_block)])[0]


def spread_columns(reduced, places):
    return spread(lax.all_to_all(reduced.astype(bf16), "wshard", 0, 0, tiled=True), places)


def line_parts(partial):
    count = lax.axis_size("line")
    *lead, rows, columns = partial.shape
    cut = partial.astype(bf16).reshape(*lead, count, rows // count, columns)
    return jnp.moveaxis(cut, -3, 0)


def move_spans(load, store, order_ref, tiles, span):
    lane = lax.broadcasted_iota(jnp.int32, (1, 2 * span), 1)

    def step(t, unused):
        first, second = order_ref[2 * t], order_ref[2 * t + 1]
        left = load(first // 2).astype(f32)
        right = load(second // 2).astype(f32)
        left = jnp.where(first % 2 == 1, pltpu.roll(left, span, 1), left)
        right = jnp.where(second % 2 == 0, pltpu.roll(right, span, 1), right)
        store(t, jnp.where(lane < span, left, right))
        return unused

    lax.fori_loop(0, tiles, step, 0)


def tile_at(index, tile):
    return pl.ds(pl.multiple_of(index * tile, tile), tile)


def block_mask(size):
    return lax.broadcasted_iota(jnp.int32, (size, size), 0) <= lax.broadcasted_iota(
        jnp.int32, (size, size), 1
    )


def forward_kernel(
    size, span, sort_ref, back_ref, range_ref, blocks_ref, out_ref, sorted_ref, float_ref, log_ref, keys_ref
):
    count, unused, width = blocks_ref.shape
    tile = 2 * span
    per = width // tile
    tiles = count * per

    def load(t):
        return blocks_ref[t // per, :, tile_at(t % per, tile)]

    def store(t, value):
        sorted_ref[:, tile_at(t, tile)] = value.astype(bf16)
        keys_ref[tile_at(t, tile), :] = jnp.transpose(value[HD : 2 * HD, :]).astype(bf16)

    move_spans(load, store, sort_ref, tiles, span)
    allowed = block_mask(size)

    def query_block(i, unused):
        here = tile_at(i, size)
        queries = sorted_ref[0:HD, here]

        def part(j, carried, masked):
            accum, running_max, running_sum = carried
            there = tile_at(j, size)
            scores = jnp.dot(keys_ref[there, :], queries, preferred_element_type=f32)
            if masked:
                scores = jnp.where(allowed, scores, masked_score)
            new_max = jnp.maximum(running_max, jnp.max(scores, axis=0, keepdims=True))
            weights = jnp.exp(scores - new_max)
            shrink = jnp.exp(running_max - new_max)
            running_sum = running_sum * shrink + jnp.sum(weights, axis=0, keepdims=True)
            accum = accum * shrink + jnp.dot(
                sorted_ref[2 * HD : 3 * HD, there],
                weights.astype(bf16),
                preferred_element_type=f32,
            )
            return (accum, new_max, running_sum)

        carried = (
            jnp.zeros((HD, size), f32),
            jnp.full((1, size), masked_score, f32),
            jnp.zeros((1, size), f32),
        )
        carried = lax.fori_loop(0, i, functools.partial(part, masked=False), carried)
        accum, running_max, running_sum = part(i, carried, True)
        float_ref[:, here] = accum / running_sum
        log_ref[:, here] = running_max + jnp.log(running_sum)
        return unused

    float_ref[...] = jnp.zeros_like(float_ref)
    log_ref[...] = jnp.zeros_like(log_ref)
    lax.fori_loop(range_ref[0], range_ref[1], query_block, 0)

    def store_back(t, value):
        out_ref[t // per, :, tile_at(t % per, tile)] = value.astype(bf16)

    move_spans(lambda t: float_ref[:, tile_at(t, tile)], store_back, back_ref, tiles, span)


def backward_kernel(
    size,
    span,
    sort_ref,
    back_ref,
    range_ref,
    sorted_ref,
    float_ref,
    log_ref,
    blocks_ref,
    out_ref,
    keys_ref,
    values_ref,
    given_ref,
    delta_ref,
    grads_ref,
):
    count, unused, width = blocks_ref.shape
    tile = 2 * span
    per = width // tile
    tiles = count * per

    def load(t):
        return blocks_ref[t // per, :, tile_at(t % per, tile)]

    def store(t, value):
        here = tile_at(t, tile)
        given_ref[:, here] = value.astype(bf16)
        delta_ref[:, here] = jnp.sum(value * float_ref[:, here], axis=0, keepdims=True)
        keys_ref[here, :] = jnp.transpose(sorted_ref[HD : 2 * HD, here].astype(f32)).astype(bf16)
        values_ref[here, :] = jnp.transpose(sorted_ref[2 * HD :, here].astype(f32)).astype(bf16)

    move_spans(load, store, sort_ref, tiles, span)
    allowed = block_mask(size)
    grads_ref[...] = jnp.zeros_like(grads_ref)

    def key_block(j, unused):
        there = tile_at(j, size)
        keys = keys_ref[there, :]
        values = values_ref[there, :]
        keys_across = sorted_ref[HD : 2 * HD, there]

        def part(i, carried, masked):
            key_acc, value_acc = carried
            here = tile_at(i, size)
            queries = sorted_ref[0:HD, here]
            given = given_ref[:, here]
            scores = jnp.dot(keys, queries, preferred_element_type=f32)
            probs = jnp.exp(scores - log_ref[:, here])
            if masked:
                probs = jnp.where(allowed, probs, 0.0)
            probs_grad = jnp.dot(values, given, preferred_element_type=f32)
            score_low = (probs * (probs_grad - delta_ref[:, here])).astype(bf16)
            value_acc = value_acc + contract(given, probs.astype(bf16), 1, 1)
            key_acc = key_acc + contract(queries, score_low, 1, 1)
            grads_ref[0:HD, here] += jnp.dot(
                keys_across, score_low, preferred_element_type=f32
            ) * (HD**-0.5)
            return (key_acc, value_acc)

        carried = (jnp.zeros((HD, size), f32), jnp.zeros((HD, size), f32))
        first, last = range_ref[0], range_ref[1]
        carried = lax.cond(
            jnp.logical_and(j >= first, j < last),
            lambda c: part(j, c, True),
            lambda c: c,
            carried,
        )
        carried = lax.fori_loop(
            jnp.maximum(j + 1, first), last, functools.partial(part, masked=False), carried
        )
        grads_ref[HD : 2 * HD, there] = carried[0]
        grads_ref[2 * HD :, there] = carried[1]
        return unused

    lax.fori_loop(0, range_ref[1], key_block, 0)

    def store_back(t, value):
        out_ref[t // per, :, tile_at(t % per, tile)] = value.astype(bf16)

    move_spans(lambda t: grads_ref[:, tile_at(t, tile)], store_back, back_ref, tiles, span)


def attend_forward(blocks, sort_order, back_order, query_range, span, size):
    count, unused, width = blocks.shape
    total = count * width
    smem = pl.BlockSpec(memory_space=pltpu.SMEM)
    vmem = pl.BlockSpec(memory_space=pltpu.VMEM)
    return pl.pallas_call(
        functools.partial(forward_kernel, size, span),
        out_shape=(
            jax.ShapeDtypeStruct((count, HD, width), bf16),
            jax.ShapeDtypeStruct((3 * HD, total), bf16),
            jax.ShapeDtypeStruct((HD, total), f32),
            jax.ShapeDtypeStruct((1, total), f32),
        ),
        in_specs=[smem, smem, smem, vmem],
        out_specs=(vmem, vmem, vmem, vmem),
        scratch_shapes=[pltpu.VMEM((total, HD), bf16)],
        compiler_params=pltpu.CompilerParams(vmem_limit_bytes=56 * 1024 * 1024),
        cost_estimate=pl.CostEstimate(
            flops=30 * 10**9, transcendentals=0, bytes_accessed=8 * 10**6
        ),
        name="attend_forward",
    )(sort_order, back_order, query_range, blocks)


def attend_backward(
    ordered, floats, logs, blocks, sort_order, back_order, query_range, span, size
):
    count, unused, width = blocks.shape
    total = count * width
    smem = pl.BlockSpec(memory_space=pltpu.SMEM)
    vmem = pl.BlockSpec(memory_space=pltpu.VMEM)
    return pl.pallas_call(
        functools.partial(backward_kernel, size, span),
        out_shape=jax.ShapeDtypeStruct((count, 3 * HD, width), bf16),
        in_specs=[smem, smem, smem, vmem, vmem, vmem, vmem],
        out_specs=vmem,
        scratch_shapes=[
            pltpu.VMEM((total, HD), bf16),
            pltpu.VMEM((total, HD), bf16),
            pltpu.VMEM((HD, total), bf16),
            pltpu.VMEM((1, total), f32),
            pltpu.VMEM((3 * HD, total), f32),
        ],
        compiler_params=pltpu.CompilerParams(vmem_limit_bytes=56 * 1024 * 1024),
        cost_estimate=pl.CostEstimate(
            flops=36 * 10**9, transcendentals=0, bytes_accessed=8 * 10**6
        ),
        name="attend_backward",
    )(sort_order, back_order, query_range, ordered, floats, logs, blocks)


def norm_parts(vector):
    inverse = lax.rsqrt(jnp.mean(vector * vector, axis=-1, keepdims=True) + epsilon)
    return inverse, vector * inverse


def norm_back(vector, scale_gain, gradient):
    inverse, normed = norm_parts(vector)
    gain_term = jnp.sum(gradient * normed, axis=0)
    scaled = gradient * scale_gain
    return (
        inverse * (scaled - normed * jnp.mean(scaled * normed, axis=-1, keepdims=True)),
        gain_term,
    )


def local(
    inputs,
    span_order,
    attn_gain,
    query_weight,
    key_weight,
    value_weight,
    output_weight,
    ffn_gain,
    gate_weight,
    up_weight,
    down_weight,
    cotangent,
):
    tok_dev, width = inputs.shape
    span = tok_dev // 2
    tokens = KVH * tok_dev
    line = lax.axis_size("line")
    halves = lax.axis_size("xpart")
    shards = lax.axis_size("wshard")
    place = lax.axis_index("line")
    side = lax.axis_index("xpart")
    slab_place = side * shards + lax.axis_index("wshard")
    copies = line // GROUP
    rows = width // shards

    flips = jnp.array(FLIPS, jnp.int32)
    devices = jnp.arange(line, dtype=jnp.int32)[:, None] * KVH + (flips ^ slab_place)[None, :]
    slots = (2 * devices[..., None] + jnp.arange(2, dtype=jnp.int32)).reshape(-1)
    spans = span_order.shape[0]
    numbers = jnp.arange(spans, dtype=jnp.int32)
    back_order = jnp.sum(
        jnp.where(slots[:, None] == numbers[None, :], span_order[None, :], 0), axis=1
    )
    sort_order = jnp.sum(
        jnp.where(back_order[None, :] == numbers[:, None], numbers[None, :], 0), axis=1
    )
    total = line * tokens
    size = min(512, total // copies)
    blocks_each = total // size // copies
    first_block = (place // GROUP) * blocks_each
    query_range = jnp.stack([first_block, first_block + blocks_each]).astype(jnp.int32)
    slab_spans = lax.dynamic_slice_in_dim(back_order, place * 2 * KVH, 2 * KVH, 0)
    positions = (slab_spans[:, None] * span + jnp.arange(span, dtype=jnp.int32)).reshape(-1)
    cosine, sine = rotary_tables(positions, HD)

    def own_columns(weight):
        units = weight.shape[1] // KVH
        if units % 128 == 0 or halves == 1:
            cuts = [
                lax.dynamic_slice_in_dim(weight, (w * halves + side) * units, units, 1)
                for w in range(shards)
            ]
        else:
            cuts = [
                jnp.where(
                    side == 0,
                    weight[:, 2 * w * units : (2 * w + 1) * units],
                    weight[:, (2 * w + 1) * units : (2 * w + 2) * units],
                )
                for w in range(shards)
            ]
        return jnp.stack(cuts)

    def gather_rows(columns):
        return lax.all_to_all(columns, "wshard", 0, 0, tiled=True).reshape(width, -1)

    gains = jnp.broadcast_to(jnp.stack([attn_gain, ffn_gain])[None], (shards, 2, rows))
    gains = lax.all_to_all(gains, "wshard", 0, 0, tiled=True).astype(f32)
    gain_one = gains[:, 0].reshape(width)
    gain_two = gains[:, 1].reshape(width)
    attn_weight = gather_rows(
        jnp.concatenate(
            [own_columns(query_weight), own_columns(key_weight), own_columns(value_weight)], axis=-1
        )
    )
    heads = query_weight.shape[1] // KVH
    slab_inputs = slab_gather(inputs)
    normed_one = (norm_parts(slab_inputs.astype(f32))[1] * gain_one).astype(bf16)
    slab_cotangent = slab_gather(cotangent)

    projected = contract(attn_weight, normed_one, 0, 1)
    queries = rotate(projected[:heads].reshape(GROUP, HD, tokens), cosine, sine).astype(bf16)
    queries = queries * jnp.asarray(HD**-0.5, bf16)
    keys = rotate(projected[heads : heads + HD], cosine, sine).astype(bf16)
    values = projected[heads + HD :].astype(bf16)
    blocks = jnp.concatenate(
        [queries, jnp.broadcast_to(jnp.concatenate([keys, values]), (GROUP, 2 * HD, tokens))],
        axis=1,
    )
    blocks = lax.all_to_all(jnp.tile(blocks, (copies, 1, 1)), "line", 0, 0, tiled=True)
    attended, ordered, floats, logs = attend_forward(
        blocks, sort_order, back_order, query_range, span, size
    )

    def from_heads(blocks):
        got = lax.all_to_all(blocks, "line", 0, 0, tiled=True)
        return got.reshape((copies, GROUP) + got.shape[1:])

    def add_copies(got):
        return got[0] if copies == 1 else jnp.sum(got.astype(f32), axis=0).astype(bf16)

    attended = add_copies(from_heads(attended)).reshape(heads, tokens)
    own_output = lax.dynamic_slice_in_dim(output_weight, side * heads, heads, 0)
    residual = inputs.astype(f32) + slab_reduce(contract(attended, own_output, 0, 0))

    gate_full = gather_rows(own_columns(gate_weight))
    up_full = gather_rows(own_columns(up_weight))
    units = gate_full.shape[1]
    own_down = lax.dynamic_slice_in_dim(down_weight, side * units, units, 0)
    normed_two = slab_gather((norm_parts(residual)[1] * gain_two).astype(bf16))
    gate_pre = contract(normed_two, gate_full, 1, 0)
    up_pre = contract(normed_two, up_full, 1, 0)
    sigmoid_gate = jax.nn.sigmoid(gate_pre)
    hidden = (gate_pre * sigmoid_gate * up_pre).astype(bf16)
    hidden_grad = contract(slab_cotangent, own_down, 1, 1)
    gate_low = (
        hidden_grad * up_pre * sigmoid_gate * (1.0 + gate_pre * (1.0 - sigmoid_gate))
    ).astype(bf16)
    up_low = (hidden_grad * gate_pre * sigmoid_gate).astype(bf16)
    normed_two_grad = slab_reduce(
        contract(gate_low, gate_full, 1, 1) + contract(up_low, up_full, 1, 1)
    )
    down_share = line_reduce(line_parts(contract(hidden, slab_cotangent, 0, 0)))
    gate_share = line_reduce(
        line_parts(contract(normed_two, gate_low, 0, 0).reshape(shards, rows, units))
    )
    up_share = line_reduce(
        line_parts(contract(normed_two, up_low, 0, 0).reshape(shards, rows, units))
    )
    residual_part, ffn_gain_term = norm_back(residual, gain_two, normed_two_grad)
    residual_grad = cotangent.astype(f32) + residual_part
    branch_low = slab_gather(residual_grad.astype(bf16))

    attended_grad = contract(own_output, branch_low, 1, 1).astype(bf16)
    given = jnp.tile(attended_grad.reshape(GROUP, HD, tokens), (copies, 1, 1))
    given = lax.all_to_all(given, "line", 0, 0, tiled=True)
    raw = attend_backward(
        ordered, floats, logs, given, sort_order, back_order, query_range, span, size
    )
    raw = from_heads(raw)
    query_low = rotate(add_copies(raw[:, :, :HD]).astype(f32), cosine, -sine).astype(bf16)
    pair_raw = jnp.sum(raw[:, :, HD:].astype(f32), axis=(0, 1))
    key_low = rotate(pair_raw[:HD], cosine, -sine).astype(bf16)
    value_low = pair_raw[HD:].astype(bf16)
    low = jnp.concatenate([query_low.reshape(heads, tokens), key_low, value_low], axis=0)
    normed_one_grad = slab_reduce(contract(low, attn_weight, 0, 1))
    input_part, attn_gain_term = norm_back(inputs.astype(f32), gain_one, normed_one_grad)
    input_grad = residual_grad + input_part

    output_share = line_reduce(line_parts(contract(attended, branch_low, 1, 0)))
    attn_share = line_reduce(
        line_parts(contract(normed_one, low, 0, 1).reshape(shards, rows, heads + 2 * HD))
    )

    outputs = (residual + slab_reduce(contract(hidden, own_down, 1, 0))).astype(bf16)

    down_grad = spread_rows(down_share)
    (gate_grad,) = spread_columns(gate_share, [(place_columns, whole_block)])
    (up_grad,) = spread_columns(up_share, [(place_columns, whole_block)])
    output_grad = spread_rows(output_share)
    query_grad, key_grad, value_grad = spread_columns(
        attn_share,
        [
            (place_columns, lambda block: block[..., :heads]),
            (place_narrow, lambda block: block[..., heads : heads + HD]),
            (place_narrow, lambda block: block[..., heads + HD :]),
        ],
    )
    gain_terms = lax.psum(jnp.stack([attn_gain_term, ffn_gain_term]), ("line",) + SLAB)
    gain_terms = lax.dynamic_slice_in_dim(
        gain_terms, lax.axis_index("wshard") * rows, rows, 1
    )
    return (
        outputs,
        input_grad,
        gain_terms[0],
        query_grad,
        key_grad,
        value_grad,
        output_grad,
        gain_terms[1],
        gate_grad,
        up_grad,
        down_grad,
    )


def solution(mesh):
    shards = mesh.shape["wshard"]
    halves = KVH // shards
    fine = Mesh(
        mesh.devices.reshape(mesh.shape["ctx"] // halves, halves, shards),
        ("line", "xpart", "wshard"),
    )
    every = ("line", "xpart", "wshard")
    in_specs = (
        P(every, None),
        P(),
        P("wshard"),
        P("wshard", None),
        P("wshard", None),
        P("wshard", None),
        P("wshard", None),
        P("wshard"),
        P("wshard", None),
        P("wshard", None),
        P("wshard", None),
        P(every, None),
    )
    out_specs = (
        P(every, None),
        P(every, None),
        P("wshard"),
        P("wshard", None),
        P("wshard", None),
        P("wshard", None),
        P("wshard", None),
        P("wshard"),
        P("wshard", None),
        P("wshard", None),
        P("wshard", None),
    )
    return jax.shard_map(local, mesh=fine, in_specs=in_specs, out_specs=out_specs, check_vma=False)
```

time: 2680 us -> 1350 us (0.50)
  waiting for transfers between devices: 2010 us -> 551 us
  matrix products: 396 us -> 94.2 us
  starting transfers between devices: 16.8 us -> 310 us
  Pallas kernels: 0 us -> 146 us
    psum x1 -> x0, waiting for transfers between devices: 888 us -> none  [local(): lax.psum(attn_shares[2].astype(jnp.bfloat16), 'ctx').astype(jnp.float32)]
    all_gather x14 -> x0, waiting for transfers between devices: 785 us -> none  [the longest x1 183 us: local(): lax.all_gather(down_weight, 'wshard', axis=0, tiled=True)]
    ppermute x0 -> x132, waiting for transfers between devices: none -> 457 us  [the longest x52 136 us: swap(): return lax.ppermute(value, SLAB, [(i, i ^ flip) for i in range(KVH)])]
    dot_general x49 -> x15, matrix products: 396 us -> 94.2 us  [contract(): lax.dot_general(left, right, (((left_dim,), (right_dim,)), ((), ())), pre...]
    reduce_scatter x2 -> x0, waiting for transfers between devices: 279 us -> none  [the longest x1 142 us: local(): lax.psum_scatter(key_all_grad, ('ctx', 'wshard'), scatter_dimension=0, ti...]
    ppermute x0 -> x132, starting transfers between devices: none -> 250 us  [the longest x15 86.8 us: line_reduce(): up_got = lax.ppermute(up, 'line', [(i, i + 1) for i in range(step)])]
    pallas_call x0 -> x30, Pallas kernels: none -> 146 us  [the longest x12 42.7 us: place_columns(): pl.pallas_call(place_kernel, grid_spec=pltpu.PrefetchScalarGridSpec(num_s...]
    all_to_all x4 -> x11, waiting for transfers between devices: 47.7 us -> 94.2 us  [the longest x1 36.5 us: local(): lax.all_to_all(jnp.tile(blocks, (copies, 1, 1)), 'line', 0, 0, tiled=True)]
  transfers between devices with their start and end apart: 22 -> 143, of which waited for: 16 -> 55; matrix products, arithmetic and copies ran while one was open for 20% -> 16% of each run, Pallas kernels for 0% -> 8%
where the time goes in v1:
time: 1350 us; the launch traced here: 1340 us
  waiting for transfers between devices  551 us (41%)
  starting transfers between devices  310 us (23%)
  Pallas kernels  146 us (11%)
  other arithmetic  105 us (8%)
  matrix products  94.2 us (7%)
  local copies, waits for them, and re-layouts  88.1 us (7%)
  blocking collectives  41.7 us (3%)
    ppermute x52, waiting for transfers between devices, swap(): return lax.ppermute(value, SLAB, [(i, i ^ flip) for i in range(KVH)])  136 us
    ppermute x15, waiting for transfers between devices, line_gather(): lax.ppermute(downs[-1], 'line', [(i + 1, i) for i in range(0, count - ste...  133 us
    dot_general x15, matrix products, contract(): lax.dot_general(left, right, (((left_dim,), (right_dim,)), ((), ())), pre...  94.2 us
    ppermute x20, waiting for transfers between devices, spread(): lax.ppermute(block, 'xpart', [(i, (i + turn) % halves) for i in range(hal...  89.3 us
    ppermute x15, starting transfers between devices, line_reduce(): up_got = lax.ppermute(up, 'line', [(i, i + 1) for i in range(step)])  86.8 us
    ppermute x15, waiting for transfers between devices, line_reduce(): up_got = lax.ppermute(up, 'line', [(i, i + 1) for i in range(step)])  68.1 us
    ppermute x15, starting transfers between devices, line_gather(): lax.ppermute(ups[-1], 'line', [(i, i + 1) for i in range(step - 1, count...  54.8 us
    pallas_call x12, Pallas kernels, place_columns(): pl.pallas_call(place_kernel, grid_spec=pltpu.PrefetchScalarGridSpec(num_s...  42.7 us
  transfers between devices with their start and end apart: 143, of which 55 were waited for; matrix products, arithmetic and copies ran while one was open for 16% of the time, Pallas kernels for 8%

profile of v1, /device:TPU:0, one launch (start us, length us, event | category | flops | bytes accessed | tf_op | source)
XLA Modules:
  0.0 1339.5 jit_solution(18102662622489478796)
XLA Ops:
  29.4 20.8 %collective-permute-done.3 = bf16[64,2048]{1,0:T(8,128)(2,1)S(1)} collective-permute-done((bf16[64,2048]{1,0:T(8,128)(2,1)S(1)}, bf16[64,2048]{1,0:T(8,128)(2,1)S(1)}, u32[]{:S(2)}, u32[]{:S(2)}) %collective-permute-start.3) | collective-permute-done | bytes 262176 | tf_op jit(solution)/shard_map/ppermute | solution.py:49
  73.4 36.5 %all-to-all-done.2.blocks_ref = bf16[4,192,1024]{2,1,0:T(8,128)(2,1)} async-done(((bf16[4,192,1024]{2,1,0:T(8,128)(2,1)}), bf16[4,192,1024]{2,1,0:T(8,128)(2,1)}, u32[]{:S(2)}, u32[]{:S(2)}) %all-to-all-start.2) | async-done | bytes 1572896 | tf_op jit(solution)/shard_map/all_to_all | solution.py:561
  109.9 34.6 %attend_forward.1 = (bf16[4,64,1024]{2,1,0:T(8,128)(2,1)}, bf16[192,4096]{1,0:T(8,128)(2,1)}, f32[64,4096]{1,0:T(8,128)}, f32[1,4096]{1,0:T(1,128)}) custom-call(s32[64]{0:T(128)} %select_reduce_fusion.sort_ref, s32[64]{0:T(128)} %copy-done.88, s32[2]{0:T(128)} %pad_add_fusion.8.range_ref, bf16[4,192,1024]{2,1,0:T(8,128)(2,1)} %all-to-all-done.2.blocks_ref), custom_call_target="tpu_custom_call" | custom-call | flops 30000001024 | bytes 8000000 | tf_op jit(solution)/shard_map/attend_forward/pallas_call | solution.py:410
  148.0 14.3 %all-to-all-done.3 = bf16[4,64,1024]{2,1,0:T(8,128)(2,1)S(1)} async-done(((bf16[4,64,1024]{2,1,0:T(8,128)(2,1)}), bf16[4,64,1024]{2,1,0:T(8,128)(2,1)S(1)}, u32[]{:S(2)}, u32[]{:S(2)}) %all-to-all-start.3) | async-done | bytes 524320 | tf_op jit(solution)/shard_map/all_to_all | solution.py:567
  179.7 16.0 %all-to-all-start.5 = ((bf16[4,512,1024]{2,1,0:T(8,128)(2,1)}), bf16[4,512,1024]{2,1,0:T(8,128)(2,1)}, u32[]{:S(2)}, u32[]{:S(2)}) async-start(bf16[4,512,1024]{2,1,0:T(8,128)(2,1)} %pad_maximum_fusion.1), calls=%async_computation.5 | async-start | bytes 8388608 | tf_op jit(solution)/shard_map/all_to_all | solution.py:536
  216.6 32.7 %collective-permute-done.29 = bf16[64,2048]{1,0:T(8,128)(2,1)S(1)} collective-permute-done((bf16[64,2048]{1,0:T(8,128)(2,1)S(1)}, bf16[64,2048]{1,0:T(8,128)(2,1)S(1)}, u32[]{:S(2)}, u32[]{:S(2)}) %collective-permute-start.29) | collective-permute-done | bytes 262176 | tf_op jit(solution)/shard_map/ppermute | solution.py:49
  251.3 11.6 collective-permute-done.9
  263.6 12.2 collective-permute-done.11
  288.3 7.7 collective-permute-done.14
  322.0 10.0 fusion.92
  332.0 24.1 %all-to-all-done.4 = bf16[4,512,1024]{2,1,0:T(8,128)(2,1)} async-done(((bf16[4,512,1024]{2,1,0:T(8,128)(2,1)}), bf16[4,512,1024]{2,1,0:T(8,128)(2,1)}, u32[]{:S(2)}, u32[]{:S(2)}) %all-to-all-start.4) | async-done | bytes 4194336 | tf_op jit(solution)/shard_map/all_to_all | solution.py:536
  356.1 10.1 fusion.91
  366.2 10.8 multiply_convert_fusion
  381.9 10.4 fusion.93
  409.9 9.8 convolution_add_fusion
  425.9 20.2 %collective-permute-done.84 = bf16[4,128,1024]{2,1,0:T(8,128)(2,1)S(1)} collective-permute-done((bf16[4,128,1024]{2,1,0:T(8,128)(2,1)}, bf16[4,128,1024]{2,1,0:T(8,128)(2,1)S(1)}, u32[]{:S(2)}, u32[]{:S(2)}) %collective-permute-start.84) | collective-permute-done | bytes 1048608 | tf_op jit(solution)/shard_map/ppermute | solution.py:89
  450.6 6.9 fusion.5
  476.9 14.0 %collective-permute-done.117 = bf16[256,2048]{1,0:T(8,128)(2,1)S(1)} collective-permute-done((bf16[256,2048]{1,0:T(8,128)(2,1)S(1)}, bf16[256,2048]{1,0:T(8,128)(2,1)S(1)}, u32[]{:S(2)}, u32[]{:S(2)}) %collective-permute-start.117) | collective-permute-done | bytes 1048608 | tf_op jit(solution)/shard_map/ppermute | solution.py:89
  502.7 10.9 collective-permute-done.85
  522.9 13.1 collective-permute-done.101
  552.7 7.8 collective-permute-done.35
  618.7 36.8 %collective-permute-start.102 = (bf16[4,128,1024]{2,1,0:T(8,128)(2,1)}, bf16[4,128,1024]{2,1,0:T(8,128)(2,1)}, u32[]{:S(2)}, u32[]{:S(2)}) collective-permute-start(bf16[4,128,1024]{2,1,0:T(8,128)(2,1)} %get-tuple-element.45), channel_id=1, source_target_pairs={{0,8},{8,16},{16,24},{1,9},{9,17},{17,25},{2,10},{10,18},{18,26},{... | collective-permute-start | bytes 3145736 | tf_op jit(solution)/shard_map/ppermute | solution.py:89
  666.4 17.1 %collective-permute-done.89 = bf16[4,128,1024]{2,1,0:T(8,128)(2,1)S(1)} collective-permute-done((bf16[4,128,1024]{2,1,0:T(8,128)(2,1)S(1)}, bf16[4,128,1024]{2,1,0:T(8,128)(2,1)S(1)}, u32[]{:S(2)}, u32[]{:S(2)}) %collective-permute-start.89) | collective-permute-done | bytes 1048608 | tf_op jit(solution)/shard_map/ppermute | solution.py:90
  698.3 13.0 collective-permute-start.121
  711.3 6.6 all-to-all-start.6
  730.7 19.3 %all-to-all-done.6.blocks_ref = bf16[4,64,1024]{2,1,0:T(8,128)(2,1)S(1)} async-done(((bf16[4,64,1024]{2,1,0:T(8,128)(2,1)}), bf16[4,64,1024]{2,1,0:T(8,128)(2,1)S(1)}, u32[]{:S(2)}, u32[]{:S(2)}) %all-to-all-start.6) | async-done | bytes 524320 | tf_op jit(solution)/shard_map/all_to_all | solution.py:607
  754.4 39.9 %attend_backward.1 = bf16[4,192,1024]{2,1,0:T(8,128)(2,1)} custom-call(s32[64]{0:T(128)} %select_reduce_fusion.sort_ref, s32[64]{0:T(128)} %copy-done.88, s32[2]{0:T(128)} %pad_add_fusion.8.range_ref, bf16[192,4096]{1,0:T(8,128)(2,1)} %get-tuple-element.16.sorted_ref, f32[64,4096]{1,0:T(8,128)} %get-tuple-element.17.float_ref, ...), custom_call_target="tpu_custom_call" | custom-call | flops 35999997952 | bytes 8000000 | tf_op jit(solution)/shard_map/attend_backward/pallas_call | solution.py:436
  795.4 11.0 collective-permute-start.77
  814.3 10.8 collective-permute-done.74
  845.8 9.3 collective-permute-done.131
  855.1 11.5 collective-permute-start.93
  868.3 7.5 collective-permute-done.76
  878.5 6.5 collective-permute-done.83
  885.7 9.5 collective-permute-start.109
  917.8 13.3 collective-permute-done.106
  932.6 21.0 %collective-permute-done.123 = bf16[256,2048]{1,0:T(8,128)(2,1)S(1)} collective-permute-done((bf16[256,2048]{1,0:T(8,128)(2,1)S(1)}, bf16[256,2048]{1,0:T(8,128)(2,1)S(1)}, u32[]{:S(2)}, u32[]{:S(2)}) %collective-permute-start.123) | collective-permute-done | bytes 1048608 | tf_op jit(solution)/shard_map/ppermute | solution.py:108
  960.4 12.4 collective-permute-done.91
  976.5 6.9 collective-permute-done.82
  997.7 18.7 %collective-permute-done.124 = bf16[256,2048]{1,0:T(8,128)(2,1)S(1)} collective-permute-done((bf16[256,2048]{1,0:T(8,128)(2,1)S(1)}, bf16[256,2048]{1,0:T(8,128)(2,1)S(1)}, u32[]{:S(2)}, u32[]{:S(2)}) %collective-permute-start.124) | collective-permute-done | bytes 1048608 | tf_op jit(solution)/shard_map/ppermute | solution.py:108
  1035.0 16.7 %collective-permute-done.92 = bf16[4,128,1024]{2,1,0:T(8,128)(2,1)S(1)} collective-permute-done((bf16[4,128,1024]{2,1,0:T(8,128)(2,1)S(1)}, bf16[4,128,1024]{2,1,0:T(8,128)(2,1)S(1)}, u32[]{:S(2)}, u32[]{:S(2)}) %collective-permute-start.92) | collective-permute-done | bytes 1048608 | tf_op jit(solution)/shard_map/ppermute | solution.py:108
  1051.7 17.5 %collective-permute-done.108 = bf16[4,128,1024]{2,1,0:T(8,128)(2,1)S(1)} collective-permute-done((bf16[4,128,1024]{2,1,0:T(8,128)(2,1)S(1)}, bf16[4,128,1024]{2,1,0:T(8,128)(2,1)S(1)}, u32[]{:S(2)}, u32[]{:S(2)}) %collective-permute-start.108) | collective-permute-done | bytes 1048608 | tf_op jit(solution)/shard_map/ppermute | solution.py:108
  1084.6 9.3 collective-permute-done.57
  1095.3 6.6 collective-permute-done.98.refs_1_
  1104.3 20.0 %collective-permute-done.114.refs_1_ = bf16[4,128,1024]{2,1,0:T(8,128)(2,1)S(1)} collective-permute-done((bf16[4,128,1024]{2,1,0:T(8,128)(2,1)S(1)}, bf16[4,128,1024]{2,1,0:T(8,128)(2,1)S(1)}, u32[]{:S(2)}, u32[]{:S(2)}) %collective-permute-start.114) | collective-permute-done | bytes 1048608 | tf_op jit(solution)/shard_map/ppermute | solution.py:208
  1191.0 18.5 %collective-permute-done.110.refs_1_ = bf16[4,128,1024]{2,1,0:T(8,128)(2,1)} collective-permute-done((bf16[4,128,1024]{2,1,0:T(8,128)(2,1)}, bf16[4,128,1024]{2,1,0:T(8,128)(2,1)}, u32[]{:S(2)}, u32[]{:S(2)}) %collective-permute-start.110) | collective-permute-done | bytes 1048608 | tf_op jit(solution)/shard_map/ppermute | solution.py:208
  1221.5 8.4 collective-permute-start.61
  1263.4 41.7 %psum.7 = f32[2,2048]{1,0:T(2,128)S(1)} all-reduce(f32[2,2048]{1,0:T(2,128)S(1)} %pad_maximum_fusion.14), channel_id=1, replica_groups=mesh['line'=4,'xpart'=2,'wshard'=4] {'line','xpart','wshard'}, use_global_device_ids=true, to_apply=%region_10.11 | all-reduce | flops 4096 | bytes 32768 | tf_op jit(solution)/shard_map/psum | solution.py:640
  1311.8 7.4 collective-permute-done.66
  (721 shorter events, 584.9 us)
Async XLA Ops:
  5.2 46.5 %collective-permute-start.4 = (bf16[128,2048]{1,0:T(8,128)(2,1)}, bf16[128,2048]{1,0:T(8,128)(2,1)}, u32[]{:S(2)}, u32[]{:S(2)}) collective-permute-start(bf16[128,2048]{1,0:T(8,128)(2,1)} %param.13), channel_id=1, source_target_pairs={{0,1},{1,0},{2,3},{3,2},{4,5},{5,4},{6,7},{7,6},{8,9},{9,8},{10,11... | collective-permute-start | bytes 1572872 | tf_op jit(solution)/shard_map/ppermute | solution.py:49
  67.3 42.6 %all-to-all-start.2 = ((bf16[4,192,1024]{2,1,0:T(8,128)(2,1)}), bf16[4,192,1024]{2,1,0:T(8,128)(2,1)}, u32[]{:S(2)}, u32[]{:S(2)}) async-start(bf16[4,192,1024]{2,1,0:T(8,128)(2,1)} %pad_maximum_fusion.2), calls=%async_computation.2 | async-start | bytes 3145728 | tf_op jit(solution)/shard_map/all_to_all | solution.py:561
  171.7 104.6 %collective-permute-start.30 = (bf16[128,2048]{1,0:T(8,128)(2,1)}, bf16[128,2048]{1,0:T(8,128)(2,1)}, u32[]{:S(2)}, u32[]{:S(2)}) collective-permute-start(bf16[128,2048]{1,0:T(8,128)(2,1)} %param.24), channel_id=1, source_target_pairs={{0,1},{1,0},{2,3},{3,2},{4,5},{5,4},{6,7},{7,6},{8,9},{9,8},{10,11... | collective-permute-start | bytes 1572872 | tf_op jit(solution)/shard_map/ppermute | solution.py:49
  179.7 123.2 %all-to-all-start.5 = ((bf16[4,512,1024]{2,1,0:T(8,128)(2,1)}), bf16[4,512,1024]{2,1,0:T(8,128)(2,1)}, u32[]{:S(2)}, u32[]{:S(2)}) async-start(bf16[4,512,1024]{2,1,0:T(8,128)(2,1)} %pad_maximum_fusion.1), calls=%async_computation.5 | async-start | bytes 8388608 | tf_op jit(solution)/shard_map/all_to_all | solution.py:536
  201.4 47.9 %collective-permute-start.29 = (bf16[64,2048]{1,0:T(8,128)(2,1)S(1)}, bf16[64,2048]{1,0:T(8,128)(2,1)S(1)}, u32[]{:S(2)}, u32[]{:S(2)}) collective-permute-start(bf16[64,2048]{1,0:T(8,128)(2,1)S(1)} %slice.815), channel_id=1, source_target_pairs={{0,2},{1,3},{2,0},{3,1},{4,6},{5,7},{6,4},{7,5},{8,10},{9,11},{10,... | collective-permute-start | bytes 786440 | tf_op jit(solution)/shard_map/ppermute | solution.py:49
  204.2 46.6 %collective-permute-start.28 = (bf16[64,2048]{1,0:T(8,128)(2,1)S(1)}, bf16[64,2048]{1,0:T(8,128)(2,1)S(1)}, u32[]{:S(2)}, u32[]{:S(2)}) collective-permute-start(bf16[64,2048]{1,0:T(8,128)(2,1)S(1)} %slice.814), channel_id=1, source_target_pairs={{0,4},{1,5},{2,6},{3,7},{4,0},{5,1},{6,2},{7,3},{8,12},{9,13},{10,... | collective-permute-start | bytes 786440 | tf_op jit(solution)/shard_map/ppermute | solution.py:49
  205.7 82.4 %collective-permute-start.32 = (bf16[128,2048]{1,0:T(8,128)(2,1)}, bf16[128,2048]{1,0:T(8,128)(2,1)S(1)}, u32[]{:S(2)}, u32[]{:S(2)}) collective-permute-start(bf16[128,2048]{1,0:T(8,128)(2,1)} %collective-permute-done.27), channel_id=1, source_target_pairs={{0,1},{1,0},{2,3},{3,2},{4,5},{5,4},{6,7},{7,6},{8,9},{9,8},{10,11... | collective-permute-start | bytes 1572872 | tf_op jit(solution)/shard_map/ppermute | solution.py:49
  212.6 75.4 %collective-permute-start.31 = (bf16[128,2048]{1,0:T(8,128)(2,1)}, bf16[128,2048]{1,0:T(8,128)(2,1)S(1)}, u32[]{:S(2)}, u32[]{:S(2)}) collective-permute-start(bf16[128,2048]{1,0:T(8,128)(2,1)} %collective-permute-done.26), channel_id=1, source_target_pairs={{0,1},{1,0},{2,3},{3,2},{4,5},{5,4},{6,7},{7,6},{8,9},{9,8},{10,11... | collective-permute-start | bytes 1572872 | tf_op jit(solution)/shard_map/ppermute | solution.py:49
  302.9 53.2 %all-to-all-start.4 = ((bf16[4,512,1024]{2,1,0:T(8,128)(2,1)}), bf16[4,512,1024]{2,1,0:T(8,128)(2,1)}, u32[]{:S(2)}, u32[]{:S(2)}) async-start(bf16[4,512,1024]{2,1,0:T(8,128)(2,1)} %pad_maximum_fusion), calls=%async_computation.4 | async-start | bytes 8388608 | tf_op jit(solution)/shard_map/all_to_all | solution.py:536
  400.1 75.2 %collective-permute-start.119 = (bf16[256,2048]{1,0:T(8,128)(2,1)}, bf16[256,2048]{1,0:T(8,128)(2,1)}, u32[]{:S(2)}, u32[]{:S(2)}) collective-permute-start(bf16[256,2048]{1,0:T(8,128)(2,1)} %get-tuple-element.44), channel_id=1, source_target_pairs={{24,16},{25,17},{26,18},{27,19},{28,20},{29,21},{30,22},{31,23}} | collective-permute-start | bytes 3145736 | tf_op jit(solution)/shard_map/ppermute | solution.py:90
  421.5 55.4 %collective-permute-start.87 = (bf16[4,128,1024]{2,1,0:T(8,128)(2,1)}, bf16[4,128,1024]{2,1,0:T(8,128)(2,1)S(1)}, u32[]{:S(2)}, u32[]{:S(2)}) collective-permute-start(bf16[4,128,1024]{2,1,0:T(8,128)(2,1)} %get-tuple-element.52), channel_id=1, source_target_pairs={{24,16},{25,17},{26,18},{27,19},{28,20},{29,21},{30,22},{31,23}} | collective-permute-start | bytes 3145736 | tf_op jit(solution)/shard_map/ppermute | solution.py:90
  424.1 44.4 %collective-permute-start.100 = (bf16[4,128,1024]{2,1,0:T(8,128)(2,1)S(1)}, bf16[4,128,1024]{2,1,0:T(8,128)(2,1)S(1)}, u32[]{:S(2)}, u32[]{:S(2)}) collective-permute-start(bf16[4,128,1024]{2,1,0:T(8,128)(2,1)S(1)} %get-tuple-element.47), channel_id=1, source_target_pairs={{0,8},{1,9},{2,10},{3,11},{4,12},{5,13},{6,14},{7,15}} | collective-permute-start | bytes 3145736 | tf_op jit(solution)/shard_map/ppermute | solution.py:89
  425.4 118.9 %collective-permute-start.34 = (bf16[4,128,2048]{2,1,0:T(8,128)(2,1)}, bf16[4,128,2048]{2,1,0:T(8,128)(2,1)}, u32[]{:S(2)}, u32[]{:S(2)}) collective-permute-start(bf16[4,128,2048]{2,1,0:T(8,128)(2,1)} %bitcast.42), channel_id=1, source_target_pairs={{0,1},{1,0},{2,3},{3,2},{4,5},{5,4},{6,7},{7,6},{8,9},{9,8},{10,11... | collective-permute-start | bytes 6291464 | tf_op jit(solution)/shard_map/ppermute | solution.py:49
  446.1 44.8 %collective-permute-start.117 = (bf16[256,2048]{1,0:T(8,128)(2,1)S(1)}, bf16[256,2048]{1,0:T(8,128)(2,1)S(1)}, u32[]{:S(2)}, u32[]{:S(2)}) collective-permute-start(bf16[256,2048]{1,0:T(8,128)(2,1)S(1)} %fusion.9), channel_id=1, source_target_pairs={{0,8},{8,16},{1,9},{9,17},{2,10},{10,18},{3,11},{11,19},{4,12},{12... | collective-permute-start | bytes 3145736 | tf_op jit(solution)/shard_map/ppermute | solution.py:89
  468.5 45.0 %collective-permute-start.85 = (bf16[4,128,1024]{2,1,0:T(8,128)(2,1)}, bf16[4,128,1024]{2,1,0:T(8,128)(2,1)}, u32[]{:S(2)}, u32[]{:S(2)}) collective-permute-start(bf16[4,128,1024]{2,1,0:T(8,128)(2,1)} %fusion.19), channel_id=1, source_target_pairs={{0,8},{8,16},{1,9},{9,17},{2,10},{10,18},{3,11},{11,19},{4,12},{12... | collective-permute-start | bytes 3145736 | tf_op jit(solution)/shard_map/ppermute | solution.py:89
  475.3 46.8 %collective-permute-start.103 = (bf16[4,128,1024]{2,1,0:T(8,128)(2,1)}, bf16[4,128,1024]{2,1,0:T(8,128)(2,1)}, u32[]{:S(2)}, u32[]{:S(2)}) collective-permute-start(bf16[4,128,1024]{2,1,0:T(8,128)(2,1)} %get-tuple-element.48), channel_id=1, source_target_pairs={{24,16},{25,17},{26,18},{27,19},{28,20},{29,21},{30,22},{31,23}} | collective-permute-start | bytes 3145736 | tf_op jit(solution)/shard_map/ppermute | solution.py:90
  476.9 71.8 %collective-permute-start.21 = (bf16[4,128,2048]{2,1,0:T(8,128)(2,1)}, bf16[4,128,2048]{2,1,0:T(8,128)(2,1)}, u32[]{:S(2)}, u32[]{:S(2)}) collective-permute-start(bf16[4,128,2048]{2,1,0:T(8,128)(2,1)} %bitcast.36), channel_id=1, source_target_pairs={{0,1},{1,0},{2,3},{3,2},{4,5},{5,4},{6,7},{7,6},{8,9},{9,8},{10,11... | collective-permute-start | bytes 6291464 | tf_op jit(solution)/shard_map/ppermute | solution.py:49
  491.0 45.0 %collective-permute-start.101 = (bf16[4,128,1024]{2,1,0:T(8,128)(2,1)}, bf16[4,128,1024]{2,1,0:T(8,128)(2,1)}, u32[]{:S(2)}, u32[]{:S(2)}) collective-permute-start(bf16[4,128,1024]{2,1,0:T(8,128)(2,1)} %fusion.14), channel_id=1, source_target_pairs={{0,8},{8,16},{1,9},{9,17},{2,10},{10,18},{3,11},{11,19},{4,12},{12... | collective-permute-start | bytes 3145736 | tf_op jit(solution)/shard_map/ppermute | solution.py:89
  513.5 312.9 %collective-permute-start.118 = (bf16[256,2048]{1,0:T(8,128)(2,1)}, bf16[256,2048]{1,0:T(8,128)(2,1)}, u32[]{:S(2)}, u32[]{:S(2)}) collective-permute-start(bf16[256,2048]{1,0:T(8,128)(2,1)} %get-tuple-element.41), channel_id=1, source_target_pairs={{0,8},{8,16},{16,24},{1,9},{9,17},{17,25},{2,10},{10,18},{18,26},{... | collective-permute-start | bytes 3145736 | tf_op jit(solution)/shard_map/ppermute | solution.py:89
  522.1 78.6 %collective-permute-start.120 = (bf16[256,2048]{1,0:T(8,128)(2,1)}, bf16[256,2048]{1,0:T(8,128)(2,1)S(1)}, u32[]{:S(2)}, u32[]{:S(2)}) collective-permute-start(bf16[256,2048]{1,0:T(8,128)(2,1)} %get-tuple-element.42), channel_id=1, source_target_pairs={{24,16},{16,8},{25,17},{17,9},{26,18},{18,10},{27,19},{19,11},{28,... | collective-permute-start | bytes 3145736 | tf_op jit(solution)/shard_map/ppermute | solution.py:90
  536.0 124.5 %collective-permute-start.86 = (bf16[4,128,1024]{2,1,0:T(8,128)(2,1)}, bf16[4,128,1024]{2,1,0:T(8,128)(2,1)S(1)}, u32[]{:S(2)}, u32[]{:S(2)}) collective-permute-start(bf16[4,128,1024]{2,1,0:T(8,128)(2,1)} %get-tuple-element.49), channel_id=1, source_target_pairs={{0,8},{8,16},{16,24},{1,9},{9,17},{17,25},{2,10},{10,18},{18,26},{... | collective-permute-start | bytes 3145736 | tf_op jit(solution)/shard_map/ppermute | solution.py:89
  618.7 101.2 %collective-permute-start.102 = (bf16[4,128,1024]{2,1,0:T(8,128)(2,1)}, bf16[4,128,1024]{2,1,0:T(8,128)(2,1)}, u32[]{:S(2)}, u32[]{:S(2)}) collective-permute-start(bf16[4,128,1024]{2,1,0:T(8,128)(2,1)} %get-tuple-element.45), channel_id=1, source_target_pairs={{0,8},{8,16},{16,24},{1,9},{9,17},{17,25},{2,10},{10,18},{18,26},{... | collective-permute-start | bytes 3145736 | tf_op jit(solution)/shard_map/ppermute | solution.py:89
  656.9 63.0 %collective-permute-start.105 = (bf16[4,128,1024]{2,1,0:T(8,128)(2,1)}, bf16[4,128,1024]{2,1,0:T(8,128)(2,1)}, u32[]{:S(2)}, u32[]{:S(2)}) collective-permute-start(bf16[4,128,1024]{2,1,0:T(8,128)(2,1)} %fusion.13), channel_id=1, source_target_pairs={{24,16},{16,8},{8,0},{25,17},{17,9},{9,1},{26,18},{18,10},{10,2},{... | collective-permute-start | bytes 3145736 | tf_op jit(solution)/shard_map/ppermute | solution.py:90
  698.3 128.1 %collective-permute-start.121 = (bf16[256,2048]{1,0:T(8,128)(2,1)}, bf16[256,2048]{1,0:T(8,128)(2,1)}, u32[]{:S(2)}, u32[]{:S(2)}) collective-permute-start(bf16[256,2048]{1,0:T(8,128)(2,1)} %fusion.8), channel_id=1, source_target_pairs={{24,16},{16,8},{8,0},{25,17},{17,9},{9,1},{26,18},{18,10},{10,2},{... | collective-permute-start | bytes 3145736 | tf_op jit(solution)/shard_map/ppermute | solution.py:90
  723.4 70.9 %collective-permute-start.70 = (bf16[64,2048]{1,0:T(8,128)(2,1)S(1)}, bf16[64,2048]{1,0:T(8,128)(2,1)}, u32[]{:S(2)}, u32[]{:S(2)}) collective-permute-start(bf16[64,2048]{1,0:T(8,128)(2,1)S(1)} %get-tuple-element.67), channel_id=1, source_target_pairs={{0,8},{8,16},{16,24},{1,9},{9,17},{17,25},{2,10},{10,18},{18,26},{... | collective-permute-start | bytes 786440 | tf_op jit(solution)/shard_map/ppermute | solution.py:89
  729.4 64.9 %collective-permute-start.73 = (bf16[64,2048]{1,0:T(8,128)(2,1)}, bf16[64,2048]{1,0:T(8,128)(2,1)}, u32[]{:S(2)}, u32[]{:S(2)}) collective-permute-start(bf16[64,2048]{1,0:T(8,128)(2,1)} %fusion.53), channel_id=1, source_target_pairs={{24,16},{16,8},{8,0},{25,17},{17,9},{9,1},{26,18},{18,10},{10,2},{... | collective-permute-start | bytes 786440 | tf_op jit(solution)/shard_map/ppermute | solution.py:90
  750.8 56.9 %all-to-all-start.10 = ((bf16[4,128,1024]{2,1,0:T(8,128)(2,1)}), bf16[4,128,1024]{2,1,0:T(8,128)(2,1)S(1)}, u32[]{:S(2)}, u32[]{:S(2)}) async-start(bf16[4,128,1024]{2,1,0:T(8,128)(2,1)} %fusion.16), calls=%async_computation.10 | async-start | bytes 2097152 | tf_op jit(solution)/shard_map/all_to_all | solution.py:227
  807.8 87.4 %all-to-all-start.7 = ((bf16[4,192,1024]{2,1,0:T(8,128)(2,1)}), bf16[4,192,1024]{2,1,0:T(8,128)(2,1)}, u32[]{:S(2)}, u32[]{:S(2)}) async-start(bf16[4,192,1024]{2,1,0:T(8,128)(2,1)} %attend_backward.1), calls=%async_computation.7 | async-start | bytes 3145728 | tf_op jit(solution)/shard_map/all_to_all | solution.py:567
  837.4 60.6 %collective-permute-start.99 = (bf16[4,128,1024]{2,1,0:T(8,128)(2,1)S(1)}, bf16[4,128,1024]{2,1,0:T(8,128)(2,1)}, u32[]{:S(2)}, u32[]{:S(2)}) collective-permute-start(bf16[4,128,1024]{2,1,0:T(8,128)(2,1)S(1)} %all-to-all-done.9.refs_0_), channel_id=1, source_target_pairs={{0,4},{4,0},{1,5},{5,1},{2,6},{6,2},{3,7},{7,3},{8,12},{12,8},{9,1... | collective-permute-start | bytes 3145736 | tf_op jit(solution)/shard_map/ppermute | solution.py:208
  855.1 45.2 %collective-permute-start.93 = (bf16[4,128,1024]{2,1,0:T(8,128)(2,1)S(1)}, bf16[4,128,1024]{2,1,0:T(8,128)(2,1)}, u32[]{:S(2)}, u32[]{:S(2)}) collective-permute-start(bf16[4,128,1024]{2,1,0:T(8,128)(2,1)S(1)} %all-to-all-done.9.refs_0_), channel_id=1, source_target_pairs={{0,8},{8,16},{16,24},{1,9},{9,17},{17,25},{2,10},{10,18},{18,26},{... | collective-permute-start | bytes 3145736 | tf_op jit(solution)/shard_map/ppermute | solution.py:106
  905.5 48.0 %collective-permute-start.123 = (bf16[256,2048]{1,0:T(8,128)(2,1)S(1)}, bf16[256,2048]{1,0:T(8,128)(2,1)S(1)}, u32[]{:S(2)}, u32[]{:S(2)}) collective-permute-start(bf16[256,2048]{1,0:T(8,128)(2,1)S(1)} %copy-done.59), channel_id=1, source_target_pairs={{8,0},{16,8},{9,1},{17,9},{10,2},{18,10},{11,3},{19,11},{12,4},{20... | collective-permute-start | bytes 3145736 | tf_op jit(solution)/shard_map/ppermute | solution.py:108
  907.4 51.7 %collective-permute-start.95 = (bf16[4,128,1024]{2,1,0:T(8,128)(2,1)}, bf16[4,128,1024]{2,1,0:T(8,128)(2,1)S(1)}, u32[]{:S(2)}, u32[]{:S(2)}) collective-permute-start(bf16[4,128,1024]{2,1,0:T(8,128)(2,1)} %collective-permute-done.93), channel_id=1, source_target_pairs={{8,16},{16,24},{9,17},{17,25},{10,18},{18,26},{11,19},{19,27},{12,... | collective-permute-start | bytes 3145736 | tf_op jit(solution)/shard_map/ppermute | solution.py:106
  912.7 60.0 %collective-permute-start.91 = (bf16[4,128,1024]{2,1,0:T(8,128)(2,1)}, bf16[4,128,1024]{2,1,0:T(8,128)(2,1)S(1)}, u32[]{:S(2)}, u32[]{:S(2)}) collective-permute-start(bf16[4,128,1024]{2,1,0:T(8,128)(2,1)} %collective-permute-done.90), channel_id=1, source_target_pairs={{8,0},{16,8},{9,1},{17,9},{10,2},{18,10},{11,3},{19,11},{12,4},{20... | collective-permute-start | bytes 3145736 | tf_op jit(solution)/shard_map/ppermute | solution.py:108
  916.8 57.3 %collective-permute-start.129 = (bf16[256,2048]{1,0:T(8,128)(2,1)S(1)}, bf16[256,2048]{1,0:T(8,128)(2,1)S(1)}, u32[]{:S(2)}, u32[]{:S(2)}) collective-permute-start(bf16[256,2048]{1,0:T(8,128)(2,1)S(1)} %collective-permute-done.127), channel_id=1, source_target_pairs={{16,24},{17,25},{18,26},{19,27},{20,28},{21,29},{22,30},{23,31}} | collective-permute-start | bytes 3145736 | tf_op jit(solution)/shard_map/ppermute | solution.py:106
  972.7 43.7 %collective-permute-start.124 = (bf16[256,2048]{1,0:T(8,128)(2,1)S(1)}, bf16[256,2048]{1,0:T(8,128)(2,1)S(1)}, u32[]{:S(2)}, u32[]{:S(2)}) collective-permute-start(bf16[256,2048]{1,0:T(8,128)(2,1)S(1)} %collective-permute-done.123), channel_id=1, source_target_pairs={{8,0},{9,1},{10,2},{11,3},{12,4},{13,5},{14,6},{15,7}} | collective-permute-start | bytes 3145736 | tf_op jit(solution)/shard_map/ppermute | solution.py:108
  984.1 46.6 %collective-permute-start.128 = (bf16[256,2048]{1,0:T(8,128)(2,1)S(1)}, bf16[256,2048]{1,0:T(8,128)(2,1)S(1)}, u32[]{:S(2)}, u32[]{:S(2)}) collective-permute-start(bf16[256,2048]{1,0:T(8,128)(2,1)S(1)} %broadcast_select_fusion.1), channel_id=1, source_target_pairs={{0,4},{4,0},{1,5},{5,1},{2,6},{6,2},{3,7},{7,3},{8,12},{12,8},{9,1... | collective-permute-start | bytes 3145736 | tf_op jit(solution)/shard_map/ppermute | solution.py:208
  1023.5 45.7 %collective-permute-start.108 = (bf16[4,128,1024]{2,1,0:T(8,128)(2,1)S(1)}, bf16[4,128,1024]{2,1,0:T(8,128)(2,1)S(1)}, u32[]{:S(2)}, u32[]{:S(2)}) collective-permute-start(bf16[4,128,1024]{2,1,0:T(8,128)(2,1)S(1)} %collective-permute-done.107), channel_id=1, source_target_pairs={{8,0},{9,1},{10,2},{11,3},{12,4},{13,5},{14,6},{15,7}} | collective-permute-start | bytes 3145736 | tf_op jit(solution)/shard_map/ppermute | solution.py:108
  1032.3 47.1 %collective-permute-start.126 = (bf16[256,2048]{1,0:T(8,128)(2,1)S(1)}, bf16[256,2048]{1,0:T(8,128)(2,1)S(1)}, u32[]{:S(2)}, u32[]{:S(2)}) collective-permute-start(bf16[256,2048]{1,0:T(8,128)(2,1)S(1)} %broadcast_select_fusion.2), channel_id=1, source_target_pairs={{0,4},{4,0},{1,5},{5,1},{2,6},{6,2},{3,7},{7,3},{8,12},{12,8},{9,1... | collective-permute-start | bytes 3145736 | tf_op jit(solution)/shard_map/ppermute | solution.py:208
  1051.7 179.5 %collective-permute-start.47 = (bf16[4,128,2048]{2,1,0:T(8,128)(2,1)}, bf16[4,128,2048]{2,1,0:T(8,128)(2,1)}, u32[]{:S(2)}, u32[]{:S(2)}) collective-permute-start(bf16[4,128,2048]{2,1,0:T(8,128)(2,1)} %bitcast.53), channel_id=1, source_target_pairs={{0,1},{1,0},{2,3},{3,2},{4,5},{5,4},{6,7},{7,6},{8,9},{9,8},{10,11... | collective-permute-start | bytes 6291464 | tf_op jit(solution)/shard_map/ppermute | solution.py:49
  1070.7 53.6 %collective-permute-start.114 = (bf16[4,128,1024]{2,1,0:T(8,128)(2,1)S(1)}, bf16[4,128,1024]{2,1,0:T(8,128)(2,1)S(1)}, u32[]{:S(2)}, u32[]{:S(2)}) collective-permute-start(bf16[4,128,1024]{2,1,0:T(8,128)(2,1)S(1)} %broadcast_select_fusion.3.refs_0_), channel_id=1, source_target_pairs={{0,4},{4,0},{1,5},{5,1},{2,6},{6,2},{3,7},{7,3},{8,12},{12,8},{9,1... | collective-permute-start | bytes 3145736 | tf_op jit(solution)/shard_map/ppermute | solution.py:208
  1083.0 103.4 %collective-permute-start.96 = (bf16[4,128,1024]{2,1,0:T(8,128)(2,1)S(1)}, bf16[4,128,1024]{2,1,0:T(8,128)(2,1)}, u32[]{:S(2)}, u32[]{:S(2)}) collective-permute-start(bf16[4,128,1024]{2,1,0:T(8,128)(2,1)S(1)} %broadcast_select_fusion.6.refs_0_), channel_id=1, source_target_pairs={{0,4},{4,0},{1,5},{5,1},{2,6},{6,2},{3,7},{7,3},{8,12},{12,8},{9,1... | collective-permute-start | bytes 3145736 | tf_op jit(solution)/shard_map/ppermute | solution.py:208
  1093.8 87.8 %collective-permute-start.112 = (bf16[4,128,1024]{2,1,0:T(8,128)(2,1)}, bf16[4,128,1024]{2,1,0:T(8,128)(2,1)}, u32[]{:S(2)}, u32[]{:S(2)}) collective-permute-start(bf16[4,128,1024]{2,1,0:T(8,128)(2,1)} %broadcast_select_fusion.5.refs_0_), channel_id=1, source_target_pairs={{0,4},{4,0},{1,5},{5,1},{2,6},{6,2},{3,7},{7,3},{8,12},{12,8},{9,1... | collective-permute-start | bytes 3145736 | tf_op jit(solution)/shard_map/ppermute | solution.py:208
  1102.8 111.4 %collective-permute-start.94 = (bf16[4,128,1024]{2,1,0:T(8,128)(2,1)}, bf16[4,128,1024]{2,1,0:T(8,128)(2,1)}, u32[]{:S(2)}, u32[]{:S(2)}) collective-permute-start(bf16[4,128,1024]{2,1,0:T(8,128)(2,1)} %broadcast_select_fusion.8.refs_0_), channel_id=1, source_target_pairs={{0,4},{4,0},{1,5},{5,1},{2,6},{6,2},{3,7},{7,3},{8,12},{12,8},{9,1... | collective-permute-start | bytes 3145736 | tf_op jit(solution)/shard_map/ppermute | solution.py:208
  1125.3 84.2 %collective-permute-start.110 = (bf16[4,128,1024]{2,1,0:T(8,128)(2,1)}, bf16[4,128,1024]{2,1,0:T(8,128)(2,1)}, u32[]{:S(2)}, u32[]{:S(2)}) collective-permute-start(bf16[4,128,1024]{2,1,0:T(8,128)(2,1)} %broadcast_select_fusion.7.refs_0_), channel_id=1, source_target_pairs={{0,4},{4,0},{1,5},{5,1},{2,6},{6,2},{3,7},{7,3},{8,12},{12,8},{9,1... | collective-permute-start | bytes 3145736 | tf_op jit(solution)/shard_map/ppermute | solution.py:208
  1129.3 89.8 %all-to-all-start.8 = ((bf16[4,128,384]{2,1,0:T(8,128)(2,1)}), bf16[4,128,384]{2,1,0:T(8,128)(2,1)}, u32[]{:S(2)}, u32[]{:S(2)}) async-start(bf16[4,128,384]{2,1,0:T(8,128)(2,1)} %fusion.42), calls=%async_computation.8 | async-start | bytes 786432 | tf_op jit(solution)/shard_map/all_to_all | solution.py:227
  1257.9 51.5 %collective-permute-start.64 = (bf16[4,128,384]{2,1,0:T(8,128)(2,1)S(1)}, bf16[4,128,384]{2,1,0:T(8,128)(2,1)}, u32[]{:S(2)}, u32[]{:S(2)}) collective-permute-start(bf16[4,128,384]{2,1,0:T(8,128)(2,1)S(1)} %broadcast_select_fusion.10), channel_id=1, source_target_pairs={{0,4},{4,0},{1,5},{5,1},{2,6},{6,2},{3,7},{7,3},{8,12},{12,8},{9,1... | collective-permute-start | bytes 1179656 | tf_op jit(solution)/shard_map/ppermute | solution.py:208
  1259.5 46.3 %collective-permute-start.65 = (bf16[4,128,384]{2,1,0:T(8,128)(2,1)}, bf16[4,128,384]{2,1,0:T(8,128)(2,1)S(1)}, u32[]{:S(2)}, u32[]{:S(2)}) collective-permute-start(bf16[4,128,384]{2,1,0:T(8,128)(2,1)} %collective-permute-done.63), channel_id=1, source_target_pairs={{16,24},{17,25},{18,26},{19,27},{20,28},{21,29},{22,30},{23,31}} | collective-permute-start | bytes 1179656 | tf_op jit(solution)/shard_map/ppermute | solution.py:106
  1260.1 49.0 %collective-permute-start.60 = (bf16[4,128,384]{2,1,0:T(8,128)(2,1)}, bf16[4,128,384]{2,1,0:T(8,128)(2,1)S(1)}, u32[]{:S(2)}, u32[]{:S(2)}) collective-permute-start(bf16[4,128,384]{2,1,0:T(8,128)(2,1)} %collective-permute-done.59), channel_id=1, source_target_pairs={{8,0},{9,1},{10,2},{11,3},{12,4},{13,5},{14,6},{15,7}} | collective-permute-start | bytes 1179656 | tf_op jit(solution)/shard_map/ppermute | solution.py:108
  (191 other events, 4220.0 us)

commit v2 on v1

--- a/solution.py
+++ b/solution.py
@@ -53,63 +53,147 @@
 
 
 def slab_gather(block):
-    half = block.shape[0] // 2
-    row = swap(block, 2)
-    column = swap(block, 4)
-    far = jnp.concatenate([swap(row[:half], 4), swap(column[half:], 2)], axis=0)
-    near = [block, row, column, far]
-    return jnp.concatenate(near + [swap(v, 1) for v in near], axis=0)
+    rows = block.shape[0]
+    half = rows // 2
+    total = jnp.zeros((KVH * rows,) + block.shape[1:], block.dtype)
+
+    def put(total, pieces):
+        for index, piece in pieces:
+            total = lax.dynamic_update_slice(total, piece, (index * half,) + (0,) * (block.ndim - 1))
+        return total
+
+    total = put(total, [(0, block)])
+    row, column, other = yield [swap(block, 2), swap(block, 4), swap(block, 1)]
+    total = put(total, [(2, row), (4, column), (8, other)])
+    far_low, far_high, other_row, other_column = yield [
+        swap(row[:half], 4),
+        swap(column[half:], 2),
+        swap(row, 1),
+        swap(column, 1),
+    ]
+    total = put(total, [(6, far_low), (7, far_high), (10, other_row), (12, other_column)])
+    far_low, far_high, total = yield [swap(far_low, 1), swap(far_high, 1), total]
+    return put(total, [(14, far_low), (15, far_high)])
 
 
 def slab_reduce(partial):
     rows = partial.shape[0] // KVH
     half = partial.shape[1] // 2
     partial = partial.reshape(KVH, rows, 2 * half)
-    own = partial[:4] + swap(partial[4:].astype(bf16), 1).astype(f32)
+    (got,) = yield [swap(partial[4:].astype(bf16), 1)]
+    own = partial[:4] + got.astype(f32)
     left, right = own[..., :half], own[..., half:]
-    left = left[:2] + swap(left[2:].astype(bf16), 4).astype(f32)
-    right = right[0::2] + swap(right[1::2].astype(bf16), 2).astype(f32)
-    left = left[0] + swap(left[1].astype(bf16), 2).astype(f32)
-    right = right[0] + swap(right[1].astype(bf16), 4).astype(f32)
-    return jnp.concatenate([left, right], axis=1)
-
-
-def line_reduce(parts):
-    count = parts.shape[0]
-    place = lax.axis_index("line")
-
-    def pick(index):
-        return lax.dynamic_index_in_dim(
-            parts, jnp.clip(index, 0, count - 1), 0, keepdims=False
-        )
-
-    up = pick(place * 0 + count - 1)
-    down = pick(place * 0)
-    for step in range(1, count):
-        up_got = lax.ppermute(up, "line", [(i, i + 1) for i in range(step)])
-        down_got = lax.ppermute(
-            down, "line", [(count - 1 - i, count - 2 - i) for i in range(step)]
-        )
-        if step < count - 1:
-            up = (pick(count - 1 - step + place).astype(f32) + up_got.astype(f32)).astype(bf16)
-            down = (pick(place - (count - 1 - step)).astype(f32) + down_got.astype(f32)).astype(
-                bf16
-            )
-    return pick(place).astype(f32) + (up_got.astype(f32) + down_got.astype(f32))
-
-
-def line_gather(own):
-    count = lax.axis_size("line")
-    place = lax.axis_index("line")
-    ups, downs = [own], [own]
-    for step in range(1, count):
-        ups.append(lax.ppermute(ups[-1], "line", [(i, i + 1) for i in range(step - 1, count - 1)]))
-        downs.append(
-            lax.ppermute(downs[-1], "line", [(i + 1, i) for i in range(0, count - step)])
-        )
-    return [own] + [
-        jnp.where(place + k < count, downs[k], ups[count - k]) for k in range(1, count)
+    left_got, right_got = yield [
+        swap(left[2:].astype(bf16), 4),
+        swap(right[1::2].astype(bf16), 2),
     ]
+    left = left[:2] + left_got.astype(f32)
+    right = right[0::2] + right_got.astype(f32)
+    left_got, right_got = yield [
+        swap(left[1].astype(bf16), 2),
+        swap(right[1].astype(bf16), 4),
+    ]
+    return jnp.concatenate(
+        [left[0] + left_got.astype(f32), right[0] + right_got.astype(f32)], axis=1
+    )
+
+
+def alone(task):
+    try:
+        transfers = next(task)
+        while True:
+            transfers = task.send(transfers)
+    except StopIteration as stop:
+        return stop.value
+
+
+def after(value, *others):
+    return lax.optimization_barrier((value,) + others)[0]
+
+
+def run_tasks(tasks, box):
+    running, stage, last = {}, 0, ()
+    tasks = list(tasks)
+    while tasks or running:
+        for entry in list(tasks):
+            name, ready, make, *turn = entry
+            if ready(stage, box) and turn in ([], [stage % 2]):
+                tasks.remove(entry)
+                running[name] = (make(last), None, turn)
+        moving = {}
+        for name, (task, got, turn) in list(running.items()):
+            if turn in ([], [stage % 2]):
+                try:
+                    moving[name] = task.send(got)
+                except StopIteration as stop:
+                    del running[name]
+                    box[name] = stop.value
+        held = lax.optimization_barrier(tuple(v for values in moving.values() for v in values))
+        last = held[:1] or last
+        box["now"] = last
+        done = 0
+        for name, values in moving.items():
+            task, unused, turn = running[name]
+            running[name] = (task, held[done : done + len(values)], turn)
+            done += len(values)
+        stage += 1
+
+
+def stream(chunks, placed):
+    count, halves = lax.axis_size("line"), lax.axis_size("xpart")
+    place, side = lax.axis_index("line"), lax.axis_index("xpart")
+    sides = [lax.rem(side + halves - turn, halves) for turn in range(halves)]
+    outer = jnp.logical_or(place == 0, place == count - 1)
+    inward, outward, across = [(0, 1), (3, 2)], [(1, 0), (2, 3)], [(1, 2), (2, 1)]
+    last = len(chunks)
+    parts, sums, totals, owns = {}, {}, {}, {}
+    for stage in range(last + 3):
+        moves = {}
+        going, coming = stage, stage - 2
+        if going < last:
+            parts[going] = chunks[going][0]()
+        if count != 4:
+            if going < last:
+                moves["all"] = lax.psum(parts.pop(going), "line")
+        else:
+            if going < last and coming in totals and parts[going].shape == totals[coming].shape:
+                both = jnp.where(outer, parts[going], totals[coming])
+                moves["in"] = moves["out"] = lax.ppermute(both, "line", inward + outward)
+            else:
+                if going < last:
+                    moves["in"] = lax.ppermute(parts[going], "line", inward)
+                if coming in totals:
+                    moves["out"] = lax.ppermute(totals[coming], "line", outward)
+            if stage - 1 in sums:
+                moves["across"] = lax.ppermute(sums[stage - 1], "line", across)
+        if stage - 3 in owns:
+            for turn in range(1, halves):
+                moves[turn] = lax.ppermute(
+                    owns[stage - 3], "xpart", [(i, (i + turn) % halves) for i in range(halves)]
+                )
+        values = []
+        for value in moves.values():
+            if all(value is not other for other in values):
+                values.append(value)
+        got = yield values
+        new = {id(value): new_value for value, new_value in zip(values, got)}
+        moves = {key: new[id(value)] for key, value in moves.items()}
+        if "all" in moves:
+            totals[going] = moves["all"]
+        if "across" in moves:
+            kept = sums.pop(stage - 1)
+            totals[stage - 1] = (kept.astype(f32) + moves["across"].astype(f32)).astype(bf16)
+        if "in" in moves:
+            part = parts.pop(going)
+            sums[going] = (part.astype(f32) + moves["in"].astype(f32)).astype(bf16)
+        if "out" in moves:
+            owns[coming] = jnp.where(outer, moves["out"], totals.pop(coming))
+        elif coming in totals:
+            owns[coming] = totals.pop(coming)
+        if stage - 3 in owns:
+            pieces = [owns.pop(stage - 3)] + [moves[turn] for turn in range(1, halves)]
+            chunks[stage - 3][1](placed, pieces, sides)
+    return None
 
 
 def place_kernel(spots_ref, *refs):
@@ -152,35 +236,48 @@
     )(*operands)
 
 
-def place_rows(total, pieces, spot, sides, count):
-    rows, columns = pieces[0].shape
+def blocks_kernel(sides_ref, *refs):
+    out_ref = refs[-1]
+    for turn in range(sides_ref.shape[0]):
+
+        @pl.when(pl.program_id(0) == turn)
+        def put(turn=turn):
+            out_ref[...] = refs[turn][...].astype(f32)
+
+
+def place_blocks(total, pieces, sides, shape, block, spot):
     halves = len(pieces)
-    for piece, side in zip(pieces, sides):
-        operands = [jnp.stack([side * count + spot, side * 0]).astype(jnp.int32), piece[None]]
-        width = min(columns, 1024)
-        specs = [pl.BlockSpec((1, rows, width), lambda w, spots: (0, 0, w))]
-        aliases = {}
-        if total is not None:
-            aliases = {2: 0}
-            operands.append(total)
-            specs.append(pl.BlockSpec(memory_space=pl.ANY))
-        total = pl.pallas_call(
-            place_kernel,
-            grid_spec=pltpu.PrefetchScalarGridSpec(
-                num_scalar_prefetch=1,
-                grid=(columns // width,),
-                in_specs=specs,
-                out_specs=pl.BlockSpec((rows, width), lambda w, spots: (spots[0], w)),
-            ),
-            out_shape=jax.ShapeDtypeStruct((halves * count * rows, columns), f32),
-            input_output_aliases=aliases,
-            compiler_params=pltpu.CompilerParams(vmem_limit_bytes=32 * 1024 * 1024),
-            cost_estimate=pl.CostEstimate(
-                flops=0, transcendentals=0, bytes_accessed=6 * rows * columns
-            ),
-            name="place_rows",
-        )(*operands)
-    return total
+    steps = pieces[0].shape[0] // block[0]
+
+    def source(turn):
+        def index(t, i, sides_ref):
+            return (jnp.where(t == turn, i, jnp.where(t < turn, 0, steps - 1)), 0)
+
+        return pl.BlockSpec(block, index)
+
+    operands = [jnp.stack(sides).astype(jnp.int32)] + list(pieces)
+    specs = [source(turn) for turn in range(halves)]
+    aliases = {}
+    if total is not None:
+        aliases = {len(operands): 0}
+        operands.append(total)
+        specs.append(pl.BlockSpec(memory_space=pl.ANY))
+    return pl.pallas_call(
+        blocks_kernel,
+        grid_spec=pltpu.PrefetchScalarGridSpec(
+            num_scalar_prefetch=1,
+            grid=(halves, steps),
+            in_specs=specs,
+            out_specs=pl.BlockSpec(block, lambda t, i, sides_ref: spot(sides_ref[t], i)),
+        ),
+        out_shape=jax.ShapeDtypeStruct(shape, f32),
+        input_output_aliases=aliases,
+        compiler_params=pltpu.CompilerParams(vmem_limit_bytes=32 * 1024 * 1024),
+        cost_estimate=pl.CostEstimate(
+            flops=0, transcendentals=0, bytes_accessed=6 * halves * pieces[0].size
+        ),
+        name="place_blocks",
+    )(*operands)
 
 
 def place_narrow(total, pieces, spot, sides, count):
@@ -197,41 +294,17 @@
     return lax.dynamic_update_slice(total, block, (spot * rows, 0))
 
 
-def spread(own, places):
-    count, halves = lax.axis_size("line"), lax.axis_size("xpart")
-    place, side = lax.axis_index("line"), lax.axis_index("xpart")
-    totals = [None] * len(places)
-    sides = [lax.rem(side + halves - turn, halves) for turn in range(halves)]
-    for k, block in enumerate(line_gather(own)):
-        spot = lax.rem(place + k, count)
-        pieces = [block] + [
-            lax.ppermute(block, "xpart", [(i, (i + turn) % halves) for i in range(halves)])
-            for turn in range(1, halves)
-        ]
-        totals = [
-            put(total, [part(piece) for piece in pieces], spot, sides, count)
-            for total, (put, part) in zip(totals, places)
-        ]
-    return totals
-
-
-def whole_block(block):
-    return block
-
-
-def spread_rows(reduced):
-    return spread(reduced.astype(bf16), [(place_rows, whole_block)])[0]
-
-
-def spread_columns(reduced, places):
-    return spread(lax.all_to_all(reduced.astype(bf16), "wshard", 0, 0, tiled=True), places)
-
-
-def line_parts(partial):
+def sum_everywhere(vector):
+    for flip in (1, 2, 4):
+        (got,) = yield [swap(vector, flip)]
+        vector = vector + got
     count = lax.axis_size("line")
-    *lead, rows, columns = partial.shape
-    cut = partial.astype(bf16).reshape(*lead, count, rows // count, columns)
-    return jnp.moveaxis(cut, -3, 0)
+    flip = 1
+    while flip < count:
+        (got,) = yield [lax.ppermute(vector, "line", [(i, i ^ flip) for i in range(count)])]
+        vector = vector + got
+        flip *= 2
+    return vector
 
 
 def move_spans(load, store, order_ref, tiles, span):
@@ -514,40 +587,73 @@
     positions = (slab_spans[:, None] * span + jnp.arange(span, dtype=jnp.int32)).reshape(-1)
     cosine, sine = rotary_tables(positions, HD)
 
-    def own_columns(weight):
+    shard = lax.axis_index("wshard")
+
+    def pass_on(block, flip):
+        return lax.ppermute(block, "wshard", [(i, i ^ flip) for i in range(shards)])
+
+    def in_order(blocks):
+        first = blocks[0]
+        total = jnp.zeros((shards,) + first.shape, first.dtype)
+        for flip, block in enumerate(blocks):
+            total = lax.dynamic_update_slice(
+                total, block[None], (shard ^ flip,) + (0,) * first.ndim
+            )
+        return total
+
+    def side_columns(weight, flip):
         units = weight.shape[1] // KVH
         if units % 128 == 0 or halves == 1:
-            cuts = [
-                lax.dynamic_slice_in_dim(weight, (w * halves + side) * units, units, 1)
-                for w in range(shards)
-            ]
-        else:
-            cuts = [
-                jnp.where(
-                    side == 0,
-                    weight[:, 2 * w * units : (2 * w + 1) * units],
-                    weight[:, (2 * w + 1) * units : (2 * w + 2) * units],
-                )
-                for w in range(shards)
-            ]
-        return jnp.stack(cuts)
-
-    def gather_rows(columns):
-        return lax.all_to_all(columns, "wshard", 0, 0, tiled=True).reshape(width, -1)
-
-    gains = jnp.broadcast_to(jnp.stack([attn_gain, ffn_gain])[None], (shards, 2, rows))
-    gains = lax.all_to_all(gains, "wshard", 0, 0, tiled=True).astype(f32)
-    gain_one = gains[:, 0].reshape(width)
-    gain_two = gains[:, 1].reshape(width)
-    attn_weight = gather_rows(
-        jnp.concatenate(
-            [own_columns(query_weight), own_columns(key_weight), own_columns(value_weight)], axis=-1
-        )
-    )
+            start = ((shard ^ flip) * halves + side) * units
+            return lax.dynamic_slice_in_dim(weight, start, units, 1)
+        pair = lax.dynamic_slice_in_dim(weight, (shard ^ flip) * halves * units, halves * units, 1)
+        return jnp.where(side == 0, pair[:, :units], pair[:, units:])
+
     heads = query_weight.shape[1] // KVH
-    slab_inputs = slab_gather(inputs)
-    normed_one = (norm_parts(slab_inputs.astype(f32))[1] * gain_one).astype(bf16)
-    slab_cotangent = slab_gather(cotangent)
+    units = gate_weight.shape[1] // KVH
+
+    def side_block(weights, flip):
+        return jnp.concatenate([side_columns(weight, flip) for weight in weights], axis=1)
+
+    box = {}
+
+    def exchange(weights, flips):
+        weights = after(weights, *box["now"])
+        return [pass_on(side_block(weights, flip), flip) for flip in flips]
+
+    near, middle, far = (1,), range(2, shards // 2 + 1), range(shards // 2 + 1, shards)
+    near, middle, far = (
+        [flip for flip in flips if flip < shards] for flips in (near, middle, far)
+    )
+
+    projections = (query_weight, key_weight, value_weight)
+    ffn_weights = (gate_weight, up_weight)
+
+    def weights_task():
+        blocks = [side_block(projections, 0)]
+        blocks += yield [pass_on(side_block(projections, flip), flip) for flip in near]
+        gains = jnp.stack([attn_gain, ffn_gain])
+        gains = after(gains, *box["now"])
+        got = yield exchange(projections, middle) + [
+            pass_on(gains, flip) for flip in range(1, shards)
+        ]
+        blocks += got[: len(middle)]
+        gains = in_order([gains] + list(got[len(middle) :])).astype(f32)
+        blocks += yield exchange(projections, far)
+        attn_weight = in_order(blocks).reshape(width, -1)
+        return (gains[:, 0].reshape(width), gains[:, 1].reshape(width), attn_weight)
+
+    run_tasks(
+        [
+            ("inputs", lambda t, b: True, lambda last: slab_gather(inputs)),
+            ("weights", lambda t, b: True, lambda last: weights_task()),
+        ],
+        box,
+    )
+    gain_one, gain_two, attn_weight = box["weights"]
+    normed_one = (norm_parts(box["inputs"].astype(f32))[1] * gain_one).astype(bf16)
+
+    own_down = lax.dynamic_slice_in_dim(down_weight, side * units, units, 0)
 
     projected = contract(attn_weight, normed_one, 0, 1)
     queries = rotate(projected[:heads].reshape(GROUP, HD, tokens), cosine, sine).astype(bf16)
@@ -559,6 +665,20 @@
         axis=1,
     )
     blocks = lax.all_to_all(jnp.tile(blocks, (copies, 1, 1)), "line", 0, 0, tiled=True)
+    def ffn_pass(flips, parts, *now):
+        weights = after([ffn_weights[part] for part in parts], *now)
+        return [
+            (flip, part, pass_on(side_columns(weight, flip), flip))
+            for part, weight in zip(parts, weights)
+            for flip in flips
+        ]
+
+    def held(moves, *others):
+        values = lax.optimization_barrier(tuple(value for f, p, value in moves) + others)
+        return [(f, p, v) for (f, p, unused), v in zip(moves, values)], values[len(moves) :]
+
+    ffn_moves, (blocks,) = held(ffn_pass(near + middle, (0, 1), normed_one), blocks)
+    late_moves = ffn_pass(far, (0,), ffn_moves[-1][2])
     attended, ordered, floats, logs = attend_forward(
         blocks, sort_order, back_order, query_range, span, size
     )
@@ -570,89 +690,221 @@
     def add_copies(got):
         return got[0] if copies == 1 else jnp.sum(got.astype(f32), axis=0).astype(bf16)
 
-    attended = add_copies(from_heads(attended)).reshape(heads, tokens)
     own_output = lax.dynamic_slice_in_dim(output_weight, side * heads, heads, 0)
-    residual = inputs.astype(f32) + slab_reduce(contract(attended, own_output, 0, 0))
-
-    gate_full = gather_rows(own_columns(gate_weight))
-    up_full = gather_rows(own_columns(up_weight))
-    units = gate_full.shape[1]
-    own_down = lax.dynamic_slice_in_dim(down_weight, side * units, units, 0)
-    normed_two = slab_gather((norm_parts(residual)[1] * gain_two).astype(bf16))
-    gate_pre = contract(normed_two, gate_full, 1, 0)
-    up_pre = contract(normed_two, up_full, 1, 0)
+    late_moves, (attended,) = held(late_moves, attended)
+    last_moves = ffn_pass(far, (1,), attended)
+    late_moves, last_moves = late_moves + last_moves, len(late_moves)
+
+    def attended_task():
+        (blocks, *moves) = yield [from_heads(attended)] + [
+            v for f, p, v in late_moves[last_moves:]
+        ]
+        box["late_moves"] = late_moves[:last_moves] + [
+            (f, p, v) for (f, p, unused), v in zip(late_moves[last_moves:], moves)
+        ]
+        heads_out = add_copies(blocks).reshape(heads, tokens)
+        added = yield from slab_reduce(contract(heads_out, own_output, 0, 0))
+        return (heads_out, inputs.astype(f32) + added)
+
+    run_tasks(
+        [
+            ("attended", lambda t, b: True, lambda last: attended_task()),
+            (
+                "cotangent",
+                lambda t, b: t >= 1,
+                lambda last: slab_gather(after(cotangent, *last)),
+            ),
+        ],
+        box,
+    )
+    attended, residual = box["attended"]
+    slab_cotangent = box["cotangent"]
+
+    ffn_full = jnp.zeros((shards, rows, 2 * units), bf16)
+    moves = [(0, part, side_columns(ffn_weights[part], 0)) for part in range(2)]
+    for flip, part, block in moves + ffn_moves + box["late_moves"]:
+        ffn_full = lax.dynamic_update_slice(
+            ffn_full, block[None], (shard ^ flip, 0, part * units)
+        )
+    ffn_full = ffn_full.reshape(width, 2 * units)
+
+    normed_two = alone(
+        slab_gather((norm_parts(residual)[1] * gain_two).astype(bf16))
+    )
+    hidden_grad = contract(slab_cotangent, own_down, 1, 1)
+    normed_two, hidden_grad = lax.optimization_barrier((normed_two, hidden_grad))
+    ffn_pre = contract(normed_two, ffn_full, 1, 0)
+    gate_pre, up_pre = ffn_pre[:, :units], ffn_pre[:, units:]
     sigmoid_gate = jax.nn.sigmoid(gate_pre)
     hidden = (gate_pre * sigmoid_gate * up_pre).astype(bf16)
-    hidden_grad = contract(slab_cotangent, own_down, 1, 1)
+    down_parts = contract(hidden, slab_cotangent, 0, 0).astype(bf16)
     gate_low = (
         hidden_grad * up_pre * sigmoid_gate * (1.0 + gate_pre * (1.0 - sigmoid_gate))
     ).astype(bf16)
     up_low = (hidden_grad * gate_pre * sigmoid_gate).astype(bf16)
-    normed_two_grad = slab_reduce(
-        contract(gate_low, gate_full, 1, 1) + contract(up_low, up_full, 1, 1)
-    )
-    down_share = line_reduce(line_parts(contract(hidden, slab_cotangent, 0, 0)))
-    gate_share = line_reduce(
-        line_parts(contract(normed_two, gate_low, 0, 0).reshape(shards, rows, units))
-    )
-    up_share = line_reduce(
-        line_parts(contract(normed_two, up_low, 0, 0).reshape(shards, rows, units))
-    )
-    residual_part, ffn_gain_term = norm_back(residual, gain_two, normed_two_grad)
-    residual_grad = cotangent.astype(f32) + residual_part
-    branch_low = slab_gather(residual_grad.astype(bf16))
-
-    attended_grad = contract(own_output, branch_low, 1, 1).astype(bf16)
-    given = jnp.tile(attended_grad.reshape(GROUP, HD, tokens), (copies, 1, 1))
-    given = lax.all_to_all(given, "line", 0, 0, tiled=True)
-    raw = attend_backward(
-        ordered, floats, logs, given, sort_order, back_order, query_range, span, size
-    )
-    raw = from_heads(raw)
-    query_low = rotate(add_copies(raw[:, :, :HD]).astype(f32), cosine, -sine).astype(bf16)
-    pair_raw = jnp.sum(raw[:, :, HD:].astype(f32), axis=(0, 1))
-    key_low = rotate(pair_raw[:HD], cosine, -sine).astype(bf16)
-    value_low = pair_raw[HD:].astype(bf16)
-    low = jnp.concatenate([query_low.reshape(heads, tokens), key_low, value_low], axis=0)
-    normed_one_grad = slab_reduce(contract(low, attn_weight, 0, 1))
-    input_part, attn_gain_term = norm_back(inputs.astype(f32), gain_one, normed_one_grad)
-    input_grad = residual_grad + input_part
-
-    output_share = line_reduce(line_parts(contract(attended, branch_low, 1, 0)))
-    attn_share = line_reduce(
-        line_parts(contract(normed_one, low, 0, 1).reshape(shards, rows, heads + 2 * HD))
-    )
-
-    outputs = (residual + slab_reduce(contract(hidden, own_down, 1, 0))).astype(bf16)
-
-    down_grad = spread_rows(down_share)
-    (gate_grad,) = spread_columns(gate_share, [(place_columns, whole_block)])
-    (up_grad,) = spread_columns(up_share, [(place_columns, whole_block)])
-    output_grad = spread_rows(output_share)
-    query_grad, key_grad, value_grad = spread_columns(
-        attn_share,
+
+    def to_shards(partial):
+        return lax.all_to_all(partial, "wshard", 0, 0, tiled=True)
+
+    gate_partial = contract(normed_two, gate_low, 0, 0).astype(bf16).reshape(shards, rows, units)
+
+    def attention_back(last):
+        ffn_low = after(jnp.concatenate([gate_low, up_low], axis=1), gate_partial)
+        normed_two_grad = yield from slab_reduce(contract(ffn_low, ffn_full, 1, 1))
+        residual_part, box["ffn_gain"] = norm_back(residual, gain_two, normed_two_grad)
+        residual_grad = cotangent.astype(f32) + residual_part
+        branch_low = yield from slab_gather(residual_grad.astype(bf16))
+        attended_grad = contract(own_output, branch_low, 1, 1).astype(bf16)
+        given = jnp.tile(attended_grad.reshape(GROUP, HD, tokens), (copies, 1, 1))
+        (given,) = yield [lax.all_to_all(given, "line", 0, 0, tiled=True)]
+        box["output_parts"] = contract(attended, branch_low, 1, 0).astype(bf16)
+        raw = attend_backward(
+            ordered, floats, logs, given, sort_order, back_order, query_range, span, size
+        )
+        raw, box["output_parts"] = yield [raw, box["output_parts"]]
+        (pair_raw,) = yield [from_heads(raw[:, HD:])]
+        (query_raw,) = yield [from_heads(after(raw[:, :HD], pair_raw))]
+        query_low = rotate(add_copies(query_raw).astype(f32), cosine, -sine).astype(bf16)
+        pair_raw = jnp.sum(pair_raw.astype(f32), axis=(0, 1))
+        key_low = rotate(pair_raw[:HD], cosine, -sine).astype(bf16)
+        value_low = pair_raw[HD:].astype(bf16)
+        low = jnp.concatenate([query_low.reshape(heads, tokens), key_low, value_low], axis=0)
+        attn_partial = contract(normed_one, low, 0, 1).astype(bf16)
+        (box["attn"],) = yield [to_shards(attn_partial.reshape(shards, rows, -1))]
+        normed_one_grad = yield from slab_reduce(contract(low, attn_weight, 0, 1))
+        input_part, attn_gain_term = norm_back(inputs.astype(f32), gain_one, normed_one_grad)
+        input_grad = residual_grad + input_part
+        gain_terms = yield from sum_everywhere(jnp.stack([attn_gain_term, box["ffn_gain"]]))
+        return (input_grad, gain_terms)
+
+    half_rows = rows // 2
+
+    def feed_forward_back(last):
+        up_partial = contract(normed_two, after(up_low, gate_partial), 0, 0).astype(bf16)
+        up_partial = up_partial.reshape(shards, rows, units)
+        yield []
+        yield []
+        gate = after(gate_partial, *box["now"])
+        (box["gate0"], up_partial) = yield [to_shards(gate[:, :half_rows]), up_partial]
+        yield []
+        yield []
+        gate = after(gate_partial, *box["now"])
+        (box["gate1"],) = yield [to_shards(gate[:, half_rows:])]
+        up_now = after(up_partial, *box["now"])
+        (box["up0"],) = yield [to_shards(up_now[:, :half_rows])]
+        up_now = after(up_partial, *box["now"])
+        (box["up1"],) = yield [to_shards(up_now[:, half_rows:])]
+        return None
+
+    def feed_forward_out(last):
+        low = after(hidden, *last)
+        return (yield from slab_reduce(contract(low, own_down, 1, 0)))
+
+    half_width, half_units = width // 2, units // 2
+
+    def down_chunk(c):
+        high, right = c // 2, c % 2
+
+        def make():
+            return down_parts[
+                high * half_units : (high + 1) * half_units,
+                right * half_width : (right + 1) * half_width,
+            ]
+
+        def put(placed, pieces, sides):
+            step = half_units // 4
+            placed["down"] = place_blocks(
+                placed.get("down"),
+                pieces,
+                sides,
+                (halves * units, width),
+                (step, half_width),
+                lambda on, i: (on * 8 + high * 4 + i, right),
+            )
+
+        return (make, put)
+
+    def column_chunk(name, c, cut, entries):
+        size = rows // cut
+
+        def make():
+            if cut == 4:
+                source, start = box[name + str(c // 2)], (c % 2) * size
+            else:
+                source, start = box[name], c * size
+            return source[:, start : start + size].reshape(shards * size, -1)
+
+        def put(placed, pieces, sides):
+            pieces = [piece.reshape(shards, size, -1) for piece in pieces]
+            for key, place_part, columns in entries:
+                placed[key] = place_part(
+                    placed.get(key), [piece[..., columns] for piece in pieces], c, sides, cut
+                )
+
+        return (make, put)
+
+    def output_chunk():
+        def make():
+            partial = box["output_parts"]
+            return jnp.concatenate([partial[:, :half_width], partial[:, half_width:]], axis=0)
+
+        def put(placed, pieces, sides):
+            placed["output"] = place_blocks(
+                placed.get("output"),
+                pieces,
+                sides,
+                (halves * heads, width),
+                (heads, half_width),
+                lambda on, i: (on, i),
+            )
+
+        return (make, put)
+
+    everything = slice(None)
+    chunks = [down_chunk(c) for c in range(4)]
+    for name in ("gate", "up"):
+        chunks += [
+            column_chunk(name, c, 4, [(name, place_columns, everything)]) for c in range(4)
+        ]
+    chunks += [output_chunk()]
+    chunks += [
+        column_chunk(
+            "attn",
+            c,
+            2,
+            [
+                ("query", place_columns, slice(0, heads)),
+                ("key", place_narrow, slice(heads, heads + HD)),
+                ("value", place_narrow, slice(heads + HD, heads + 2 * HD)),
+            ],
+        )
+        for c in range(2)
+    ]
+    placed = {}
+    run_tasks(
         [
-            (place_columns, lambda block: block[..., :heads]),
-            (place_narrow, lambda block: block[..., heads : heads + HD]),
-            (place_narrow, lambda block: block[..., heads + HD :]),
+            ("attention", lambda t, b: True, attention_back),
+            ("parts", lambda t, b: True, feed_forward_back),
+            ("even", lambda t, b: True, lambda last: stream(chunks[0::2], placed), 0),
+            ("odd", lambda t, b: True, lambda last: stream(chunks[1::2], placed), 1),
+            ("out", lambda t, b: t >= 1, feed_forward_out),
         ],
-    )
-    gain_terms = lax.psum(jnp.stack([attn_gain_term, ffn_gain_term]), ("line",) + SLAB)
-    gain_terms = lax.dynamic_slice_in_dim(
-        gain_terms, lax.axis_index("wshard") * rows, rows, 1
-    )
+        box,
+    )
+    input_grad, gain_terms = box["attention"]
+    gain_terms = lax.dynamic_slice_in_dim(gain_terms, shard * rows, rows, 1)
     return (
-        outputs,
+        (residual + box["out"]).astype(bf16),
         input_grad,
         gain_terms[0],
-        query_grad,
-        key_grad,
-        value_grad,
-        output_grad,
+        placed["query"],
+        placed["key"],
+        placed["value"],
+        placed["output"],
         gain_terms[1],
-        gate_grad,
-        up_grad,
-        down_grad,
+        placed["gate"],
+        placed["up"],
+        placed["down"],
     )
 
 

time: 1350 us -> 1020 us (0.76)
  waiting for transfers between devices: 551 us -> 332 us
  starting transfers between devices: 310 us -> 212 us
  blocking collectives: 41.7 us -> 0 us
  other arithmetic: 105 us -> 137 us
  local copies, waits for them, and re-layouts: 88.1 us -> 117 us
  matrix products: 94.2 us -> 71.4 us
    ppermute x80 -> x65, waiting for transfers between devices: 322 us -> 200 us  [the longest x12 54.6 us: pass_on(): return lax.ppermute(block, 'wshard', [(i, i ^ flip) for i in range(shards)])]
    ppermute x80 -> x65, starting transfers between devices: 214 us -> 120 us  [the longest x9 39.8 us: stream(): moves['in'] = moves['out'] = lax.ppermute(both, 'line', inward + outward)]
    psum x1 -> x0, blocking collectives: 41.7 us -> none  [local(): lax.psum(jnp.stack([attn_gain_term, ffn_gain_term]), ('line',) + SLAB)]
    select_n x15 -> x29, other arithmetic: 11.5 us -> 50.9 us  [the longest x9 25.2 us: stream(): both = jnp.where(outer, parts[going], totals[coming])]
    all_to_all x1, waiting for transfers between devices: 36.5 us -> 0.01 us  [local(): lax.all_to_all(jnp.tile(blocks, (copies, 1, 1)), 'line', 0, 0, tiled=True)]
    ppermute x52 -> x59, waiting for transfers between devices: 136 us -> 99.1 us  [swap(): return lax.ppermute(value, SLAB, [(i, i ^ flip) for i in range(KVH)])]
    dynamic_update_slice x0 -> x55, local copies, waits for them, and re-layouts: none -> 34.7 us  [the longest x40 22.4 us: put(): lax.dynamic_update_slice(total, piece, (index * half,) + (0,) * (block.nd...]
    all_to_all x8 -> x6, waiting for transfers between devices: 43.5 us -> 15.8 us  [the longest x5 12.5 us: to_shards(): return lax.all_to_all(partial, 'wshard', 0, 0, tiled=True)]
  transfers between devices with their start and end apart: 143 -> 134, of which waited for: 55 -> 48; matrix products, arithmetic and copies ran while one was open for 16% -> 23% of each run, Pallas kernels for 8% -> 13%
where the time goes in v2:
time: 1020 us; the launch traced here: 1010 us
  waiting for transfers between devices  332 us (33%)
  starting transfers between devices  212 us (21%)
  other arithmetic  137 us (13%)
  Pallas kernels  133 us (13%)
  local copies, waits for them, and re-layouts  117 us (11%)
  matrix products  71.4 us (7%)
    ppermute x59, waiting for transfers between devices, swap(): return lax.ppermute(value, SLAB, [(i, i ^ flip) for i in range(KVH)])  99.1 us
    dot_general x13, matrix products, contract(): lax.dot_general(left, right, (((left_dim,), (right_dim,)), ((), ())), pre...  71.4 us
    ppermute x12, waiting for transfers between devices, pass_on(): return lax.ppermute(block, 'wshard', [(i, i ^ flip) for i in range(shards)])  54.6 us
    ppermute x6, waiting for transfers between devices, stream(): moves['in'] = lax.ppermute(parts[going], 'line', inward)  46.2 us
    ppermute x59, starting transfers between devices, swap(): return lax.ppermute(value, SLAB, [(i, i ^ flip) for i in range(KVH)])  42.6 us
    ppermute x15, waiting for transfers between devices, stream(): lax.ppermute(owns[stage - 3], 'xpart', [(i, (i + turn) % halves) for i in...  40.8 us
    pallas_call x1, Pallas kernels, attend_backward(): pl.pallas_call(functools.partial(backward_kernel, size, span), out_shape=...  39.9 us
    ppermute x9, starting transfers between devices, stream(): moves['in'] = moves['out'] = lax.ppermute(both, 'line', inward + outward)  39.8 us
  transfers between devices with their start and end apart: 134, of which 48 were waited for; matrix products, arithmetic and copies ran while one was open for 23% of the time, Pallas kernels for 13%

profile of v2, /device:TPU:0, one launch (start us, length us, event | category | flops | bytes accessed | tf_op | source)
XLA Modules:
  0.0 1006.7 jit_solution(11426807659411510966)
XLA Ops:
  37.4 8.3 collective-permute-done.5
  51.1 9.4 collective-permute-done.14
  71.8 4.9 all-to-all-start
  85.9 19.5 %collective-permute-done.18 = bf16[512,1024]{1,0:T(8,128)(2,1)} collective-permute-done((bf16[512,1024]{1,0:T(8,128)(2,1)S(1)}, bf16[512,1024]{1,0:T(8,128)(2,1)}, u32[]{:S(2)}, u32[]{:S(2)}) %collective-permute-start.18) | collective-permute-done | bytes 1048608 | tf_op jit(solution)/shard_map/ppermute | solution.py:593
  105.4 22.1 %collective-permute-done.16 = bf16[512,1024]{1,0:T(8,128)(2,1)} collective-permute-done((bf16[512,1024]{1,0:T(8,128)(2,1)}, bf16[512,1024]{1,0:T(8,128)(2,1)}, u32[]{:S(2)}, u32[]{:S(2)}) %collective-permute-start.16) | collective-permute-done | bytes 1048608 | tf_op jit(solution)/shard_map/ppermute | solution.py:593
  128.9 34.7 %attend_forward.1 = (bf16[4,64,1024]{2,1,0:T(8,128)(2,1)}, bf16[192,4096]{1,0:T(8,128)(2,1)}, f32[64,4096]{1,0:T(8,128)}, f32[1,4096]{1,0:T(1,128)}) custom-call(s32[64]{0:T(128)} %select_reduce_fusion.sort_ref, s32[64]{0:T(128)} %copy-done.90, s32[2]{0:T(128)} %get-tuple-element.422.range_ref, bf16[4,192,1024]{2,1,0:T(8,128)(2,1)} %all-to-all-done.blocks_ref), custom_call_target="tpu_custom_call" | custom-call | flops 30000001024 | bytes 8000000 | tf_op jit(solution)/shard_map/attend_forward/pallas_call | solution.py:483
  167.6 5.3 all-to-all-start.1
  172.9 14.4 %all-to-all-done.1 = bf16[4,64,1024]{2,1,0:T(8,128)(2,1)S(1)} async-done(((bf16[4,64,1024]{2,1,0:T(8,128)(2,1)}), bf16[4,64,1024]{2,1,0:T(8,128)(2,1)S(1)}, u32[]{:S(2)}, u32[]{:S(2)}) %all-to-all-start.1) | async-done | bytes 524320 | tf_op jit(solution)/shard_map/all_to_all | solution.py:687
  213.4 7.6 collective-permute-done.22
  230.2 16.3 %collective-permute-done.28 = bf16[64,2048]{1,0:T(8,128)(2,1)S(1)} collective-permute-done((bf16[64,2048]{1,0:T(8,128)(2,1)S(1)}, bf16[64,2048]{1,0:T(8,128)(2,1)S(1)}, u32[]{:S(2)}, u32[]{:S(2)}) %collective-permute-start.28) | collective-permute-done | bytes 262176 | tf_op jit(solution)/shard_map/ppermute | solution.py:49
  249.1 6.6 collective-permute-done.31
  259.1 6.5 fusion.5
  279.3 8.9 fusion.72
  288.2 5.2 multiply_convert_fusion.1
  293.3 6.2 convolution_convert_fusion.2
  302.0 11.0 %fusion.73 = f32[1024,2048]{1,0:T(8,128)S(1)} fusion(bf16[1024,2048]{1,0:T(8,128)(2,1)} %pad_maximum_fusion, bf16[2048,2048]{1,0:T(8,128)(2,1)S(1)} %bitcast.266), kind=kOutput, calls=%fused_computation.348 | convolution fusion | flops 8589934592 | bytes 20971520 | tf_op jit(solution)/shard_map/dot_general | solution.py:40
  313.6 4.7 copy-done.42
  318.3 4.9 convolution_convert_fusion.1
  330.1 22.6 %collective-permute-done.45 = bf16[512,1024]{1,0:T(8,128)(2,1)S(1)} collective-permute-done((bf16[512,1024]{1,0:T(8,128)(2,1)S(1)}, bf16[512,1024]{1,0:T(8,128)(2,1)S(1)}, u32[]{:S(2)}, u32[]{:S(2)}) %collective-permute-start.45) | collective-permute-done | bytes 1048608 | tf_op jit(solution)/shard_map/ppermute | solution.py:164
  352.8 7.5 fusion.3
  366.6 4.7 collective-permute-start.48
  379.7 14.9 %collective-permute-done.48 = bf16[512,1024]{1,0:T(8,128)(2,1)S(1)} collective-permute-done((bf16[512,1024]{1,0:T(8,128)(2,1)S(1)}, bf16[512,1024]{1,0:T(8,128)(2,1)S(1)}, u32[]{:S(2)}, u32[]{:S(2)}) %collective-permute-start.48) | collective-permute-done | bytes 1048608 | tf_op jit(solution)/shard_map/ppermute | solution.py:164
  420.0 8.3 convolution_convert_fusion
  428.3 7.2 collective-permute-start.59
  435.4 8.1 collective-permute-done.50
  461.2 7.7 collective-permute-done.61
  468.9 8.6 collective-permute-start.67
  492.9 6.2 collective-permute-done.64
  507.7 4.8 all-to-all-start.3
  520.4 5.4 collective-permute-done.71
  525.8 12.5 %all-to-all-done.3 = bf16[4,256,1024]{2,1,0:T(8,128)(2,1)} async-done(((bf16[4,256,1024]{2,1,0:T(8,128)(2,1)}), bf16[4,256,1024]{2,1,0:T(8,128)(2,1)}, u32[]{:S(2)}, u32[]{:S(2)}) %all-to-all-start.3) | async-done | bytes 2097184 | tf_op jit(solution)/shard_map/all_to_all | solution.py:747
  544.0 8.2 all-to-all-start.4
  592.0 8.5 collective-permute-done.73
  614.3 39.9 %attend_backward.1 = bf16[4,192,1024]{2,1,0:T(8,128)(2,1)} custom-call(s32[64]{0:T(128)} %select_reduce_fusion.sort_ref, s32[64]{0:T(128)} %copy-done.90, s32[2]{0:T(128)} %get-tuple-element.422.range_ref, bf16[192,4096]{1,0:T(8,128)(2,1)} %get-tuple-element.238.sorted_ref, f32[64,4096]{1,0:T(8,128)} %get-tuple-element.239.float_ref, ...), custom_call_target="tpu_custom_call" | custom-call | flops 35999997952 | bytes 8000000 | tf_op jit(solution)/shard_map/attend_backward/pallas_call | solution.py:509
  683.1 6.2 place_blocks.7.refs_2_
  699.7 8.0 collective-permute-done.79
  721.4 6.3 place_blocks.8.refs_2_
  762.0 6.2 place_blocks.9
  781.0 4.6 place_columns.12.refs_2_
  792.0 12.6 %collective-permute-start.94 = (bf16[512,1024]{1,0:T(8,128)(2,1)S(1)}, bf16[512,1024]{1,0:T(8,128)(2,1)S(1)}, u32[]{:S(2)}, u32[]{:S(2)}) collective-permute-start(bf16[512,1024]{1,0:T(8,128)(2,1)S(1)} %broadcast_select_fusion.7), channel_id=1, source_target_pairs={{0,8},{24,16},{8,0},{16,24},{1,9},{25,17},{9,1},{17,25},{2,10},{26... | collective-permute-start | bytes 3145736 | tf_op jit(solution)/shard_map/ppermute | solution.py:161
  809.9 4.6 place_columns.13.refs_2_
  862.7 14.7 %collective-permute-done.107 = bf16[512,1024]{1,0:T(8,128)(2,1)S(1)} collective-permute-done((bf16[512,1024]{1,0:T(8,128)(2,1)S(1)}, bf16[512,1024]{1,0:T(8,128)(2,1)S(1)}, u32[]{:S(2)}, u32[]{:S(2)}) %collective-permute-start.107) | collective-permute-done | bytes 1048608 | tf_op jit(solution)/shard_map/ppermute | solution.py:171
  878.7 5.1 collective-permute-done.105
  890.6 9.2 collective-permute-done.111
  899.8 7.0 collective-permute-done.109
  909.3 13.3 %collective-permute-done.112 = f32[2,2048]{1,0:T(2,128)S(1)} collective-permute-done((f32[2,2048]{1,0:T(2,128)S(1)}, f32[2,2048]{1,0:T(2,128)S(1)}, u32[]{:S(2)}, u32[]{:S(2)}) %collective-permute-start.112) | collective-permute-done | bytes 16416 | tf_op jit(solution)/shard_map/ppermute | solution.py:49
  932.0 15.0 %collective-permute-done.116 = f32[2,2048]{1,0:T(2,128)S(1)} collective-permute-done((f32[2,2048]{1,0:T(2,128)S(1)}, f32[2,2048]{1,0:T(2,128)S(1)}, u32[]{:S(2)}, u32[]{:S(2)}) %collective-permute-start.116) | collective-permute-done | bytes 16416 | tf_op jit(solution)/shard_map/ppermute | solution.py:304
  972.9 11.5 %collective-permute-done.123 = bf16[1024,384]{1,0:T(8,128)(2,1)S(1)} collective-permute-done((bf16[1024,384]{1,0:T(8,128)(2,1)S(1)}, bf16[1024,384]{1,0:T(8,128)(2,1)S(1)}, u32[]{:S(2)}, u32[]{:S(2)}) %collective-permute-start.123) | collective-permute-done | bytes 786464 | tf_op jit(solution)/shard_map/ppermute | solution.py:171
  (708 shorter events, 507.0 us)
Async XLA Ops:
  71.8 55.7 %all-to-all-start = ((bf16[4,192,1024]{2,1,0:T(8,128)(2,1)}), bf16[4,192,1024]{2,1,0:T(8,128)(2,1)}, u32[]{:S(2)}, u32[]{:S(2)}) async-start(bf16[4,192,1024]{2,1,0:T(8,128)(2,1)} %pad_maximum_fusion.1), calls=%async_computation | async-start | bytes 3145728 | tf_op jit(solution)/shard_map/all_to_all | solution.py:667
  83.1 44.4 %collective-permute-start.16 = (bf16[512,1024]{1,0:T(8,128)(2,1)}, bf16[512,1024]{1,0:T(8,128)(2,1)}, u32[]{:S(2)}, u32[]{:S(2)}) collective-permute-start(bf16[512,1024]{1,0:T(8,128)(2,1)} %get-tuple-element.336), channel_id=1, source_target_pairs={{0,2},{1,3},{2,0},{3,1},{4,6},{5,7},{6,4},{7,5},{8,10},{9,11},{10,... | collective-permute-start | bytes 3145736 | tf_op jit(solution)/shard_map/ppermute | solution.py:593
  128.8 34.8 %collective-permute-start.19 = (bf16[512,1024]{1,0:T(8,128)(2,1)S(1)}, bf16[512,1024]{1,0:T(8,128)(2,1)}, u32[]{:S(2)}, u32[]{:S(2)}) collective-permute-start(bf16[512,1024]{1,0:T(8,128)(2,1)S(1)} %constant_dynamic-slice_fusion.3), channel_id=1, source_target_pairs={{0,3},{1,2},{2,1},{3,0},{4,7},{5,6},{6,5},{7,4},{8,11},{9,10},{10,... | collective-permute-start | bytes 3145736 | tf_op jit(solution)/shard_map/ppermute | solution.py:593
  313.4 39.4 %collective-permute-start.44 = (bf16[4,128,2048]{2,1,0:T(8,128)(2,1)S(1)}, bf16[4,128,2048]{2,1,0:T(8,128)(2,1)S(1)}, u32[]{:S(2)}, u32[]{:S(2)}) collective-permute-start(bf16[4,128,2048]{2,1,0:T(8,128)(2,1)S(1)} %bitcast.284), channel_id=1, source_target_pairs={{0,1},{1,0},{2,3},{3,2},{4,5},{5,4},{6,7},{7,6},{8,9},{9,8},{10,11... | collective-permute-start | bytes 6291464 | tf_op jit(solution)/shard_map/ppermute | solution.py:49
  365.3 29.4 %collective-permute-start.49 = (bf16[4,128,2048]{2,1,0:T(8,128)(2,1)}, bf16[4,128,2048]{2,1,0:T(8,128)(2,1)}, u32[]{:S(2)}, u32[]{:S(2)}) collective-permute-start(bf16[4,128,2048]{2,1,0:T(8,128)(2,1)} %bitcast.35), channel_id=1, source_target_pairs={{0,1},{1,0},{2,3},{3,2},{4,5},{5,4},{6,7},{7,6},{8,9},{9,8},{10,11... | collective-permute-start | bytes 6291464 | tf_op jit(solution)/shard_map/ppermute | solution.py:49
  375.4 42.5 %collective-permute-start.52 = (bf16[512,1024]{1,0:T(8,128)(2,1)}, bf16[512,1024]{1,0:T(8,128)(2,1)}, u32[]{:S(2)}, u32[]{:S(2)}) collective-permute-start(bf16[512,1024]{1,0:T(8,128)(2,1)} %get-tuple-element.343), channel_id=1, source_target_pairs={{0,8},{24,16},{1,9},{25,17},{2,10},{26,18},{3,11},{27,19},{4,12},{... | collective-permute-start | bytes 3145736 | tf_op jit(solution)/shard_map/ppermute | solution.py:164
  400.2 45.0 %collective-permute-start.55 = (bf16[2,128,1024]{2,1,0:T(8,128)(2,1)}, bf16[2,128,1024]{2,1,0:T(8,128)(2,1)}, u32[]{:S(2)}, u32[]{:S(2)}) collective-permute-start(bf16[2,128,1024]{2,1,0:T(8,128)(2,1)} %slice.573), channel_id=1, source_target_pairs={{0,2},{1,3},{2,0},{3,1},{4,6},{5,7},{6,4},{7,5},{8,10},{9,11},{10,... | collective-permute-start | bytes 1572872 | tf_op jit(solution)/shard_map/ppermute | solution.py:49
  400.7 44.5 %collective-permute-start.54 = (bf16[2,128,1024]{2,1,0:T(8,128)(2,1)}, bf16[2,128,1024]{2,1,0:T(8,128)(2,1)}, u32[]{:S(2)}, u32[]{:S(2)}) collective-permute-start(bf16[2,128,1024]{2,1,0:T(8,128)(2,1)} %slice.915), channel_id=1, source_target_pairs={{0,4},{1,5},{2,6},{3,7},{4,0},{5,1},{6,2},{7,3},{8,12},{9,13},{10,... | collective-permute-start | bytes 1572872 | tf_op jit(solution)/shard_map/ppermute | solution.py:49
  404.6 40.7 %collective-permute-start.53 = (bf16[512,1024]{1,0:T(8,128)(2,1)}, bf16[512,1024]{1,0:T(8,128)(2,1)}, u32[]{:S(2)}, u32[]{:S(2)}) collective-permute-start(bf16[512,1024]{1,0:T(8,128)(2,1)} %get-tuple-element.341), channel_id=1, source_target_pairs={{8,16},{16,8},{9,17},{17,9},{10,18},{18,10},{11,19},{19,11},{12,20... | collective-permute-start | bytes 3145736 | tf_op jit(solution)/shard_map/ppermute | solution.py:168
  407.7 37.5 %all-to-all-start.2 = ((bf16[4,256,1024]{2,1,0:T(8,128)(2,1)}), bf16[4,256,1024]{2,1,0:T(8,128)(2,1)}, u32[]{:S(2)}, u32[]{:S(2)}) async-start(bf16[4,256,1024]{2,1,0:T(8,128)(2,1)} %slice.569), calls=%async_computation.2 | async-start | bytes 4194304 | tf_op jit(solution)/shard_map/all_to_all | solution.py:747
  468.9 34.7 %collective-permute-start.67 = (bf16[512,1024]{1,0:T(8,128)(2,1)S(1)}, bf16[512,1024]{1,0:T(8,128)(2,1)S(1)}, u32[]{:S(2)}, u32[]{:S(2)}) collective-permute-start(bf16[512,1024]{1,0:T(8,128)(2,1)S(1)} %bitcast_select_fusion.7), channel_id=1, source_target_pairs={{0,8},{24,16},{8,0},{16,24},{1,9},{25,17},{9,1},{17,25},{2,10},{26... | collective-permute-start | bytes 3145736 | tf_op jit(solution)/shard_map/ppermute | solution.py:161
  507.7 30.6 %all-to-all-start.3 = ((bf16[4,256,1024]{2,1,0:T(8,128)(2,1)}), bf16[4,256,1024]{2,1,0:T(8,128)(2,1)}, u32[]{:S(2)}, u32[]{:S(2)}) async-start(bf16[4,256,1024]{2,1,0:T(8,128)(2,1)} %slice.585), calls=%async_computation.3 | async-start | bytes 4194304 | tf_op jit(solution)/shard_map/all_to_all | solution.py:747
  554.9 33.6 %collective-permute-start.75 = (bf16[512,1024]{1,0:T(8,128)(2,1)S(1)}, bf16[512,1024]{1,0:T(8,128)(2,1)S(1)}, u32[]{:S(2)}, u32[]{:S(2)}) collective-permute-start(bf16[512,1024]{1,0:T(8,128)(2,1)S(1)} %broadcast_select_fusion.13.refs_0_), channel_id=1, source_target_pairs={{0,4},{4,0},{1,5},{5,1},{2,6},{6,2},{3,7},{7,3},{8,12},{12,8},{9,1... | collective-permute-start | bytes 3145736 | tf_op jit(solution)/shard_map/ppermute | solution.py:171
  558.1 33.9 %collective-permute-start.74 = (bf16[512,1024]{1,0:T(8,128)(2,1)}, bf16[512,1024]{1,0:T(8,128)(2,1)}, u32[]{:S(2)}, u32[]{:S(2)}) collective-permute-start(bf16[512,1024]{1,0:T(8,128)(2,1)} %add_convert_fusion.18), channel_id=1, source_target_pairs={{8,16},{16,8},{9,17},{17,9},{10,18},{18,10},{11,19},{19,11},{12,20... | collective-permute-start | bytes 3145736 | tf_op jit(solution)/shard_map/ppermute | solution.py:168
  567.6 32.9 %all-to-all-start.5 = ((bf16[4,256,1024]{2,1,0:T(8,128)(2,1)}), bf16[4,256,1024]{2,1,0:T(8,128)(2,1)}, u32[]{:S(2)}, u32[]{:S(2)}) async-start(bf16[4,256,1024]{2,1,0:T(8,128)(2,1)} %slice.587), calls=%async_computation.5 | async-start | bytes 4194304 | tf_op jit(solution)/shard_map/all_to_all | solution.py:747
  577.2 80.1 %collective-permute-start.78 = (bf16[512,1024]{1,0:T(8,128)(2,1)S(1)}, bf16[512,1024]{1,0:T(8,128)(2,1)}, u32[]{:S(2)}, u32[]{:S(2)}) collective-permute-start(bf16[512,1024]{1,0:T(8,128)(2,1)S(1)} %broadcast_select_fusion.12.refs_0_), channel_id=1, source_target_pairs={{0,4},{4,0},{1,5},{5,1},{2,6},{6,2},{3,7},{7,3},{8,12},{12,8},{9,1... | collective-permute-start | bytes 3145736 | tf_op jit(solution)/shard_map/ppermute | solution.py:171
  581.3 75.9 %collective-permute-start.77 = (bf16[512,1024]{1,0:T(8,128)(2,1)}, bf16[512,1024]{1,0:T(8,128)(2,1)}, u32[]{:S(2)}, u32[]{:S(2)}) collective-permute-start(bf16[512,1024]{1,0:T(8,128)(2,1)} %add_convert_fusion.16), channel_id=1, source_target_pairs={{8,16},{16,8},{9,17},{17,9},{10,18},{18,10},{11,19},{19,11},{12,20... | collective-permute-start | bytes 3145736 | tf_op jit(solution)/shard_map/ppermute | solution.py:168
  589.5 67.7 %collective-permute-start.76 = (bf16[512,1024]{1,0:T(8,128)(2,1)}, bf16[512,1024]{1,0:T(8,128)(2,1)}, u32[]{:S(2)}, u32[]{:S(2)}) collective-permute-start(bf16[512,1024]{1,0:T(8,128)(2,1)} %bitcast_select_fusion.4), channel_id=1, source_target_pairs={{0,8},{24,16},{8,0},{16,24},{1,9},{25,17},{9,1},{17,25},{2,10},{26... | collective-permute-start | bytes 3145736 | tf_op jit(solution)/shard_map/ppermute | solution.py:161
  607.6 49.7 %all-to-all-start.6 = ((bf16[4,256,1024]{2,1,0:T(8,128)(2,1)}), bf16[4,256,1024]{2,1,0:T(8,128)(2,1)}, u32[]{:S(2)}, u32[]{:S(2)}) async-start(bf16[4,256,1024]{2,1,0:T(8,128)(2,1)} %slice.589), calls=%async_computation.6 | async-start | bytes 4194304 | tf_op jit(solution)/shard_map/all_to_all | solution.py:747
  612.0 84.7 %collective-permute-start.81 = (bf16[512,1024]{1,0:T(8,128)(2,1)S(1)}, bf16[512,1024]{1,0:T(8,128)(2,1)}, u32[]{:S(2)}, u32[]{:S(2)}) collective-permute-start(bf16[512,1024]{1,0:T(8,128)(2,1)S(1)} %broadcast_select_fusion.11.refs_0_), channel_id=1, source_target_pairs={{0,4},{4,0},{1,5},{5,1},{2,6},{6,2},{3,7},{7,3},{8,12},{12,8},{9,1... | collective-permute-start | bytes 3145736 | tf_op jit(solution)/shard_map/ppermute | solution.py:171
  612.7 87.0 %collective-permute-start.80 = (bf16[512,1024]{1,0:T(8,128)(2,1)}, bf16[512,1024]{1,0:T(8,128)(2,1)}, u32[]{:S(2)}, u32[]{:S(2)}) collective-permute-start(bf16[512,1024]{1,0:T(8,128)(2,1)} %add_convert_fusion.14), channel_id=1, source_target_pairs={{8,16},{16,8},{9,17},{17,9},{10,18},{18,10},{11,19},{19,11},{12,20... | collective-permute-start | bytes 3145736 | tf_op jit(solution)/shard_map/ppermute | solution.py:168
  659.5 48.1 %all-to-all-start.7 = ((bf16[4,128,1024]{2,1,0:T(8,128)(2,1)}), bf16[4,128,1024]{2,1,0:T(8,128)(2,1)}, u32[]{:S(2)}, u32[]{:S(2)}) async-start(bf16[4,128,1024]{2,1,0:T(8,128)(2,1)} %slice.592), calls=%async_computation.7 | async-start | bytes 2097152 | tf_op jit(solution)/shard_map/all_to_all | solution.py:687
  666.6 41.1 %collective-permute-start.79 = (bf16[512,1024]{1,0:T(8,128)(2,1)S(1)}, bf16[512,1024]{1,0:T(8,128)(2,1)}, u32[]{:S(2)}, u32[]{:S(2)}) collective-permute-start(bf16[512,1024]{1,0:T(8,128)(2,1)S(1)} %bitcast_select_fusion.3), channel_id=1, source_target_pairs={{0,8},{24,16},{8,0},{16,24},{1,9},{25,17},{9,1},{17,25},{2,10},{26... | collective-permute-start | bytes 3145736 | tf_op jit(solution)/shard_map/ppermute | solution.py:161
  680.5 51.3 %collective-permute-start.84 = (bf16[512,1024]{1,0:T(8,128)(2,1)S(1)}, bf16[512,1024]{1,0:T(8,128)(2,1)}, u32[]{:S(2)}, u32[]{:S(2)}) collective-permute-start(bf16[512,1024]{1,0:T(8,128)(2,1)S(1)} %broadcast_select_fusion.10.refs_0_), channel_id=1, source_target_pairs={{0,4},{4,0},{1,5},{5,1},{2,6},{6,2},{3,7},{7,3},{8,12},{12,8},{9,1... | collective-permute-start | bytes 3145736 | tf_op jit(solution)/shard_map/ppermute | solution.py:171
  681.4 53.7 %collective-permute-start.83 = (bf16[512,1024]{1,0:T(8,128)(2,1)}, bf16[512,1024]{1,0:T(8,128)(2,1)}, u32[]{:S(2)}, u32[]{:S(2)}) collective-permute-start(bf16[512,1024]{1,0:T(8,128)(2,1)} %add_convert_fusion.12), channel_id=1, source_target_pairs={{8,16},{16,8},{9,17},{17,9},{10,18},{18,10},{11,19},{19,11},{12,20... | collective-permute-start | bytes 3145736 | tf_op jit(solution)/shard_map/ppermute | solution.py:168
  696.8 39.0 %collective-permute-start.82 = (bf16[512,1024]{1,0:T(8,128)(2,1)}, bf16[512,1024]{1,0:T(8,128)(2,1)}, u32[]{:S(2)}, u32[]{:S(2)}) collective-permute-start(bf16[512,1024]{1,0:T(8,128)(2,1)} %bitcast_select_fusion.2), channel_id=1, source_target_pairs={{0,8},{24,16},{8,0},{16,24},{1,9},{25,17},{9,1},{17,25},{2,10},{26... | collective-permute-start | bytes 3145736 | tf_op jit(solution)/shard_map/ppermute | solution.py:161
  707.6 30.9 %all-to-all-start.8 = ((bf16[4,64,1024]{2,1,0:T(8,128)(2,1)}), bf16[4,64,1024]{2,1,0:T(8,128)(2,1)}, u32[]{:S(2)}, u32[]{:S(2)}) async-start(bf16[4,64,1024]{2,1,0:T(8,128)(2,1)} %slice.591), calls=%async_computation.8 | async-start | bytes 1048576 | tf_op jit(solution)/shard_map/all_to_all | solution.py:687
  717.2 57.0 %collective-permute-start.93 = (bf16[512,1024]{1,0:T(8,128)(2,1)S(1)}, bf16[512,1024]{1,0:T(8,128)(2,1)}, u32[]{:S(2)}, u32[]{:S(2)}) collective-permute-start(bf16[512,1024]{1,0:T(8,128)(2,1)S(1)} %broadcast_select_fusion.8), channel_id=1, source_target_pairs={{0,4},{4,0},{1,5},{5,1},{2,6},{6,2},{3,7},{7,3},{8,12},{12,8},{9,1... | collective-permute-start | bytes 3145736 | tf_op jit(solution)/shard_map/ppermute | solution.py:171
  718.2 57.7 %collective-permute-start.92 = (bf16[512,1024]{1,0:T(8,128)(2,1)}, bf16[512,1024]{1,0:T(8,128)(2,1)}, u32[]{:S(2)}, u32[]{:S(2)}) collective-permute-start(bf16[512,1024]{1,0:T(8,128)(2,1)} %add_convert_fusion.9), channel_id=1, source_target_pairs={{8,16},{16,8},{9,17},{17,9},{10,18},{18,10},{11,19},{19,11},{12,20... | collective-permute-start | bytes 3145736 | tf_op jit(solution)/shard_map/ppermute | solution.py:168
  731.8 46.6 %collective-permute-start.91 = (bf16[512,1024]{1,0:T(8,128)(2,1)}, bf16[512,1024]{1,0:T(8,128)(2,1)}, u32[]{:S(2)}, u32[]{:S(2)}) collective-permute-start(bf16[512,1024]{1,0:T(8,128)(2,1)} %bitcast_select_fusion), channel_id=1, source_target_pairs={{0,8},{24,16},{8,0},{16,24},{1,9},{25,17},{9,1},{17,25},{2,10},{26... | collective-permute-start | bytes 3145736 | tf_op jit(solution)/shard_map/ppermute | solution.py:161
  745.6 32.8 %all-to-all-start.9 = ((bf16[4,512,384]{2,1,0:T(8,128)(2,1)}), bf16[4,512,384]{2,1,0:T(8,128)(2,1)}, u32[]{:S(2)}, u32[]{:S(2)}) async-start(bf16[4,512,384]{2,1,0:T(8,128)(2,1)} %bitcast.285), calls=%async_computation.9 | async-start | bytes 3145728 | tf_op jit(solution)/shard_map/all_to_all | solution.py:747
  758.0 46.7 %collective-permute-start.85 = (bf16[4,128,2048]{2,1,0:T(8,128)(2,1)}, bf16[4,128,2048]{2,1,0:T(8,128)(2,1)}, u32[]{:S(2)}, u32[]{:S(2)}) collective-permute-start(bf16[4,128,2048]{2,1,0:T(8,128)(2,1)} %bitcast.58), channel_id=1, source_target_pairs={{0,1},{1,0},{2,3},{3,2},{4,5},{5,4},{6,7},{7,6},{8,9},{9,8},{10,11... | collective-permute-start | bytes 6291464 | tf_op jit(solution)/shard_map/ppermute | solution.py:49
  761.0 30.3 %collective-permute-start.88 = (bf16[512,1024]{1,0:T(8,128)(2,1)S(1)}, bf16[512,1024]{1,0:T(8,128)(2,1)}, u32[]{:S(2)}, u32[]{:S(2)}) collective-permute-start(bf16[512,1024]{1,0:T(8,128)(2,1)S(1)} %broadcast_select_fusion.9), channel_id=1, source_target_pairs={{0,4},{4,0},{1,5},{5,1},{2,6},{6,2},{3,7},{7,3},{8,12},{12,8},{9,1... | collective-permute-start | bytes 3145736 | tf_op jit(solution)/shard_map/ppermute | solution.py:171
  775.9 28.8 %collective-permute-start.86 = (bf16[512,1024]{1,0:T(8,128)(2,1)}, bf16[512,1024]{1,0:T(8,128)(2,1)}, u32[]{:S(2)}, u32[]{:S(2)}) collective-permute-start(bf16[512,1024]{1,0:T(8,128)(2,1)} %bitcast_select_fusion.1), channel_id=1, source_target_pairs={{0,8},{24,16},{8,0},{16,24},{1,9},{25,17},{9,1},{17,25},{2,10},{26... | collective-permute-start | bytes 3145736 | tf_op jit(solution)/shard_map/ppermute | solution.py:161
  780.4 40.1 %collective-permute-start.96 = (bf16[512,1024]{1,0:T(8,128)(2,1)S(1)}, bf16[512,1024]{1,0:T(8,128)(2,1)S(1)}, u32[]{:S(2)}, u32[]{:S(2)}) collective-permute-start(bf16[512,1024]{1,0:T(8,128)(2,1)S(1)} %broadcast_select_fusion.6), channel_id=1, source_target_pairs={{0,4},{4,0},{1,5},{5,1},{2,6},{6,2},{3,7},{7,3},{8,12},{12,8},{9,1... | collective-permute-start | bytes 3145736 | tf_op jit(solution)/shard_map/ppermute | solution.py:171
  791.3 31.0 %collective-permute-start.95 = (bf16[512,1024]{1,0:T(8,128)(2,1)S(1)}, bf16[512,1024]{1,0:T(8,128)(2,1)S(1)}, u32[]{:S(2)}, u32[]{:S(2)}) collective-permute-start(bf16[512,1024]{1,0:T(8,128)(2,1)S(1)} %add_convert_fusion.6), channel_id=1, source_target_pairs={{8,16},{16,8},{9,17},{17,9},{10,18},{18,10},{11,19},{19,11},{12,20... | collective-permute-start | bytes 3145736 | tf_op jit(solution)/shard_map/ppermute | solution.py:168
  792.0 36.3 %collective-permute-start.94 = (bf16[512,1024]{1,0:T(8,128)(2,1)S(1)}, bf16[512,1024]{1,0:T(8,128)(2,1)S(1)}, u32[]{:S(2)}, u32[]{:S(2)}) collective-permute-start(bf16[512,1024]{1,0:T(8,128)(2,1)S(1)} %broadcast_select_fusion.7), channel_id=1, source_target_pairs={{0,8},{24,16},{8,0},{16,24},{1,9},{25,17},{9,1},{17,25},{2,10},{26... | collective-permute-start | bytes 3145736 | tf_op jit(solution)/shard_map/ppermute | solution.py:161
  822.2 30.5 %collective-permute-start.102 = (bf16[512,1024]{1,0:T(8,128)(2,1)S(1)}, bf16[512,1024]{1,0:T(8,128)(2,1)S(1)}, u32[]{:S(2)}, u32[]{:S(2)}) collective-permute-start(bf16[512,1024]{1,0:T(8,128)(2,1)S(1)} %broadcast_select_fusion.5), channel_id=1, source_target_pairs={{0,4},{4,0},{1,5},{5,1},{2,6},{6,2},{3,7},{7,3},{8,12},{12,8},{9,1... | collective-permute-start | bytes 3145736 | tf_op jit(solution)/shard_map/ppermute | solution.py:171
  853.5 30.2 %collective-permute-start.105 = (bf16[512,1024]{1,0:T(8,128)(2,1)S(1)}, bf16[512,1024]{1,0:T(8,128)(2,1)S(1)}, u32[]{:S(2)}, u32[]{:S(2)}) collective-permute-start(bf16[512,1024]{1,0:T(8,128)(2,1)S(1)} %add_convert_fusion.3), channel_id=1, source_target_pairs={{8,0},{16,24},{9,1},{17,25},{10,2},{18,26},{11,3},{19,27},{12,4},{... | collective-permute-start | bytes 3145736 | tf_op jit(solution)/shard_map/ppermute | solution.py:166
  860.5 39.4 %collective-permute-start.111 = (bf16[512,1024]{1,0:T(8,128)(2,1)S(1)}, bf16[512,1024]{1,0:T(8,128)(2,1)S(1)}, u32[]{:S(2)}, u32[]{:S(2)}) collective-permute-start(bf16[512,1024]{1,0:T(8,128)(2,1)S(1)} %broadcast_select_fusion.3), channel_id=1, source_target_pairs={{0,4},{4,0},{1,5},{5,1},{2,6},{6,2},{3,7},{7,3},{8,12},{12,8},{9,1... | collective-permute-start | bytes 3145736 | tf_op jit(solution)/shard_map/ppermute | solution.py:171
  877.4 29.4 %collective-permute-start.109 = (bf16[512,1024]{1,0:T(8,128)(2,1)S(1)}, bf16[512,1024]{1,0:T(8,128)(2,1)S(1)}, u32[]{:S(2)}, u32[]{:S(2)}) collective-permute-start(bf16[512,1024]{1,0:T(8,128)(2,1)S(1)} %add_convert_fusion.1), channel_id=1, source_target_pairs={{8,0},{16,24},{9,1},{17,25},{10,2},{18,26},{11,3},{19,27},{12,4},{... | collective-permute-start | bytes 3145736 | tf_op jit(solution)/shard_map/ppermute | solution.py:166
  886.3 37.7 %collective-permute-start.115 = (bf16[512,1024]{1,0:T(8,128)(2,1)S(1)}, bf16[512,1024]{1,0:T(8,128)(2,1)S(1)}, u32[]{:S(2)}, u32[]{:S(2)}) collective-permute-start(bf16[512,1024]{1,0:T(8,128)(2,1)S(1)} %broadcast_select_fusion.2), channel_id=1, source_target_pairs={{0,4},{4,0},{1,5},{5,1},{2,6},{6,2},{3,7},{7,3},{8,12},{12,8},{9,1... | collective-permute-start | bytes 3145736 | tf_op jit(solution)/shard_map/ppermute | solution.py:171
  888.6 35.3 %collective-permute-start.114 = (bf16[1024,384]{1,0:T(8,128)(2,1)S(1)}, bf16[1024,384]{1,0:T(8,128)(2,1)S(1)}, u32[]{:S(2)}, u32[]{:S(2)}) collective-permute-start(bf16[1024,384]{1,0:T(8,128)(2,1)S(1)} %add_convert_fusion.28), channel_id=1, source_target_pairs={{8,16},{16,8},{9,17},{17,9},{10,18},{18,10},{11,19},{19,11},{12,20... | collective-permute-start | bytes 2359304 | tf_op jit(solution)/shard_map/ppermute | solution.py:168
  889.3 39.1 %collective-permute-start.113 = (bf16[512,1024]{1,0:T(8,128)(2,1)S(1)}, bf16[512,1024]{1,0:T(8,128)(2,1)S(1)}, u32[]{:S(2)}, u32[]{:S(2)}) collective-permute-start(bf16[512,1024]{1,0:T(8,128)(2,1)S(1)} %add_convert_fusion), channel_id=1, source_target_pairs={{8,0},{16,24},{9,1},{17,25},{10,2},{18,26},{11,3},{19,27},{12,4},{... | collective-permute-start | bytes 3145736 | tf_op jit(solution)/shard_map/ppermute | solution.py:166
  907.9 39.1 %collective-permute-start.118 = (bf16[512,1024]{1,0:T(8,128)(2,1)S(1)}, bf16[512,1024]{1,0:T(8,128)(2,1)S(1)}, u32[]{:S(2)}, u32[]{:S(2)}) collective-permute-start(bf16[512,1024]{1,0:T(8,128)(2,1)S(1)} %broadcast_select_fusion.1), channel_id=1, source_target_pairs={{0,4},{4,0},{1,5},{5,1},{2,6},{6,2},{3,7},{7,3},{8,12},{12,8},{9,1... | collective-permute-start | bytes 3145736 | tf_op jit(solution)/shard_map/ppermute | solution.py:171
  928.6 39.0 %collective-permute-start.121 = (bf16[512,1024]{1,0:T(8,128)(2,1)S(1)}, bf16[512,1024]{1,0:T(8,128)(2,1)S(1)}, u32[]{:S(2)}, u32[]{:S(2)}) collective-permute-start(bf16[512,1024]{1,0:T(8,128)(2,1)S(1)} %broadcast_select_fusion.refs_0_), channel_id=1, source_target_pairs={{0,4},{4,0},{1,5},{5,1},{2,6},{6,2},{3,7},{7,3},{8,12},{12,8},{9,1... | collective-permute-start | bytes 3145736 | tf_op jit(solution)/shard_map/ppermute | solution.py:171
  930.7 35.9 %collective-permute-start.120 = (bf16[1024,384]{1,0:T(8,128)(2,1)S(1)}, bf16[1024,384]{1,0:T(8,128)(2,1)S(1)}, u32[]{:S(2)}, u32[]{:S(2)}) collective-permute-start(bf16[1024,384]{1,0:T(8,128)(2,1)S(1)} %add_convert_fusion.26), channel_id=1, source_target_pairs={{8,0},{16,24},{9,1},{17,25},{10,2},{18,26},{11,3},{19,27},{12,4},{... | collective-permute-start | bytes 2359304 | tf_op jit(solution)/shard_map/ppermute | solution.py:166
  949.4 35.0 %collective-permute-start.123 = (bf16[1024,384]{1,0:T(8,128)(2,1)S(1)}, bf16[1024,384]{1,0:T(8,128)(2,1)S(1)}, u32[]{:S(2)}, u32[]{:S(2)}) collective-permute-start(bf16[1024,384]{1,0:T(8,128)(2,1)S(1)} %broadcast_select_fusion.14), channel_id=1, source_target_pairs={{0,4},{4,0},{1,5},{5,1},{2,6},{6,2},{3,7},{7,3},{8,12},{12,8},{9,1... | collective-permute-start | bytes 2359304 | tf_op jit(solution)/shard_map/ppermute | solution.py:171
  (184 other events, 2574.9 us)

commit v3 on v2

--- a/solution.py
+++ b/solution.py
@@ -52,7 +52,7 @@
 FLIPS = (0, 2, 4, 6, 1, 3, 5, 7)
 
 
-def slab_gather(block):
+def slab_gather(block, turns=False):
     rows = block.shape[0]
     half = rows // 2
     total = jnp.zeros((KVH * rows,) + block.shape[1:], block.dtype)
@@ -65,6 +65,11 @@
     total = put(total, [(0, block)])
     row, column, other = yield [swap(block, 2), swap(block, 4), swap(block, 1)]
     total = put(total, [(2, row), (4, column), (8, other)])
+    if turns:
+        far, other_row, other_column = yield [swap(row, 4), swap(row, 1), swap(column, 1)]
+        total = put(total, [(6, far), (10, other_row), (12, other_column)])
+        far, total = yield [swap(far, 1), total]
+        return put(total, [(14, far)])
     far_low, far_high, other_row, other_column = yield [
         swap(row[:half], 4),
         swap(column[half:], 2),
@@ -76,12 +81,10 @@
     return put(total, [(14, far_low), (15, far_high)])
 
 
-def slab_reduce(partial):
-    rows = partial.shape[0] // KVH
-    half = partial.shape[1] // 2
-    partial = partial.reshape(KVH, rows, 2 * half)
-    (got,) = yield [swap(partial[4:].astype(bf16), 1)]
-    own = partial[:4] + got.astype(f32)
+def slab_reduce(rows_of, rows):
+    (got,) = yield [swap(rows_of(4 * rows, 8 * rows).astype(bf16), 1)]
+    own = (rows_of(0, 4 * rows) + got.astype(f32)).reshape(4, rows, -1)
+    half = own.shape[-1] // 2
     left, right = own[..., :half], own[..., half:]
     left_got, right_got = yield [
         swap(left[2:].astype(bf16), 4),
@@ -139,60 +142,151 @@
         stage += 1
 
 
-def stream(chunks, placed):
+def mix_kernel(names, block, flag_ref, *refs):
+    refs = dict(zip(names, refs))
+
+    def read(name):
+        return refs[name][...].reshape(block)
+
+    @pl.when(flag_ref[0] == 0)
+    def middle():
+        if "sum" in refs:
+            refs["sum"][...] = (read("now").astype(f32) + read("got").astype(f32)).astype(bf16)
+        if "outer" in refs and "kept" in refs:
+            refs["outer"][...] = (read("kept").astype(f32) + read("across").astype(f32)).astype(
+                bf16
+            )
+        if "own" in refs:
+            refs["own"][...] = read("before")
+
+    @pl.when(flag_ref[0] == 1)
+    def end():
+        if "outer" in refs and "next" in refs:
+            refs["outer"][...] = read("next")
+        if "own" in refs:
+            refs["own"][...] = read("got")
+
+
+def mix(outer, sources, arrays, results, steps, block):
+    at_end = {"now": 0, "next": 1, "got": None, "kept": 0, "across": 0, "before": 0}
+    names, operands, specs = [], [], []
+    for name in at_end:
+        if name in sources:
+            array, shape, index = sources[name]
+        elif name in arrays:
+            array, shape, index = arrays[name], block, lambda i: (i, 0)
+        else:
+            continue
+        if name == "got" and "sum" not in results:
+            used = 1
+        elif name == "got" and "own" not in results:
+            used = 0
+        else:
+            used = at_end[name]
+
+        def where(i, flag, index=index, used=used):
+            return index(i if used is None else jnp.where(flag[0] == used, i, 0))
+
+        names.append(name)
+        operands.append(array)
+        specs.append(pl.BlockSpec(shape, where))
+    got = pl.pallas_call(
+        functools.partial(mix_kernel, tuple(names) + tuple(results), block),
+        grid_spec=pltpu.PrefetchScalarGridSpec(
+            num_scalar_prefetch=1,
+            grid=(steps,),
+            in_specs=specs,
+            out_specs=[pl.BlockSpec(block, lambda i, flag: (i, 0)) for name in results],
+        ),
+        out_shape=[
+            jax.ShapeDtypeStruct((steps * block[0], block[1]), bf16) for name in results
+        ],
+        compiler_params=pltpu.CompilerParams(vmem_limit_bytes=32 * 1024 * 1024),
+        cost_estimate=pl.CostEstimate(
+            flops=0, transcendentals=0, bytes_accessed=10 * steps * block[0] * block[1]
+        ),
+        name="mix",
+    )(outer, *operands)
+    return dict(zip(results, got))
+
+
+def finish(task, sent):
+    try:
+        while True:
+            sent = task.send(lax.optimization_barrier(tuple(sent)))
+    except StopIteration:
+        pass
+
+
+def stream(chunks, placed, box, steps, block):
     count, halves = lax.axis_size("line"), lax.axis_size("xpart")
     place, side = lax.axis_index("line"), lax.axis_index("xpart")
     sides = [lax.rem(side + halves - turn, halves) for turn in range(halves)]
-    outer = jnp.logical_or(place == 0, place == count - 1)
+    split = count == 4
+    outer = jnp.logical_and(split, jnp.logical_or(place == 0, place == count - 1))
+    outer = outer.astype(jnp.int32).reshape(1)
     inward, outward, across = [(0, 1), (3, 2)], [(1, 0), (2, 3)], [(1, 2), (2, 1)]
     last = len(chunks)
-    parts, sums, totals, owns = {}, {}, {}, {}
+
+    def is_chunk(number):
+        return 0 <= number < last
+
+    def first(number):
+        return mix(outer * 0 + 1, {"next": chunks[number][0]()}, {}, ["outer"], steps, block)
+
+    sending = first(0)["outer"]
+    sums, owns, fresh = {}, {}, []
     for stage in range(last + 3):
         moves = {}
-        going, coming = stage, stage - 2
-        if going < last:
-            parts[going] = chunks[going][0]()
-        if count != 4:
-            if going < last:
-                moves["all"] = lax.psum(parts.pop(going), "line")
+        if not split:
+            if is_chunk(stage):
+                moves["all"] = lax.psum(first(stage)["outer"], "line")
         else:
-            if going < last and coming in totals and parts[going].shape == totals[coming].shape:
-                both = jnp.where(outer, parts[going], totals[coming])
-                moves["in"] = moves["out"] = lax.ppermute(both, "line", inward + outward)
-            else:
-                if going < last:
-                    moves["in"] = lax.ppermute(parts[going], "line", inward)
-                if coming in totals:
-                    moves["out"] = lax.ppermute(totals[coming], "line", outward)
-            if stage - 1 in sums:
+            pairs = (inward if is_chunk(stage) else []) + (outward if is_chunk(stage - 2) else [])
+            if pairs:
+                moves["got"] = lax.ppermute(sending, "line", pairs)
+            if is_chunk(stage - 1):
                 moves["across"] = lax.ppermute(sums[stage - 1], "line", across)
-        if stage - 3 in owns:
+        if is_chunk(stage - 3):
             for turn in range(1, halves):
                 moves[turn] = lax.ppermute(
                     owns[stage - 3], "xpart", [(i, (i + turn) % halves) for i in range(halves)]
                 )
-        values = []
-        for value in moves.values():
-            if all(value is not other for other in values):
-                values.append(value)
-        got = yield values
-        new = {id(value): new_value for value, new_value in zip(values, got)}
-        moves = {key: new[id(value)] for key, value in moves.items()}
-        if "all" in moves:
-            totals[going] = moves["all"]
-        if "across" in moves:
-            kept = sums.pop(stage - 1)
-            totals[stage - 1] = (kept.astype(f32) + moves["across"].astype(f32)).astype(bf16)
-        if "in" in moves:
-            part = parts.pop(going)
-            sums[going] = (part.astype(f32) + moves["in"].astype(f32)).astype(bf16)
-        if "out" in moves:
-            owns[coming] = jnp.where(outer, moves["out"], totals.pop(coming))
-        elif coming in totals:
-            owns[coming] = totals.pop(coming)
-        if stage - 3 in owns:
+        held = yield list(moves.values()) + [placed[key] for key in fresh]
+        moves = dict(zip(moves, held))
+        placed.update(zip(fresh, held[len(moves) :]))
+        if split:
+            sources, arrays, results = {}, {}, []
+            if is_chunk(stage):
+                sources["now"] = chunks[stage][0]()
+                results.append("sum")
+            if is_chunk(stage + 1):
+                sources["next"] = chunks[stage + 1][0]()
+            if is_chunk(stage - 1):
+                arrays.update(kept=sums.pop(stage - 1), across=moves["across"])
+            if is_chunk(stage + 1) or is_chunk(stage - 1):
+                results.append("outer")
+            if is_chunk(stage - 2):
+                arrays["before"] = sending
+                results.append("own")
+            if is_chunk(stage) or is_chunk(stage - 2):
+                arrays["got"] = moves["got"]
+            if results:
+                made = mix(outer, sources, arrays, results, steps, block)
+                sending = made.get("outer")
+                if is_chunk(stage):
+                    sums[stage] = made["sum"]
+                if is_chunk(stage - 2):
+                    owns[stage - 2] = made["own"]
+                box["mixed"] = (next(iter(made.values())),)
+        elif is_chunk(stage):
+            owns[stage] = moves["all"]
+        fresh = []
+        if is_chunk(stage - 3):
             pieces = [owns.pop(stage - 3)] + [moves[turn] for turn in range(1, halves)]
+            before = dict(placed)
             chunks[stage - 3][1](placed, pieces, sides)
+            fresh = [key for key in placed if placed[key] is not before.get(key)]
     return None
 
 
@@ -319,17 +413,21 @@
         store(t, jnp.where(lane < span, left, right))
         return unused
 
-    lax.fori_loop(0, tiles, step, 0)
+    lax.fori_loop(0, tiles, step, 0, unroll=min(8, tiles))
 
 
 def tile_at(index, tile):
     return pl.ds(pl.multiple_of(index * tile, tile), tile)
 
 
-def block_mask(size):
-    return lax.broadcasted_iota(jnp.int32, (size, size), 0) <= lax.broadcasted_iota(
-        jnp.int32, (size, size), 1
-    )
+def rows_at(start, amount, align):
+    return pl.ds(pl.multiple_of(start, align), amount)
+
+
+def causal(scores, offset, other):
+    key = lax.broadcasted_iota(jnp.int32, scores.shape, 0)
+    query = lax.broadcasted_iota(jnp.int32, scores.shape, 1)
+    return jnp.where(key <= query + offset, scores, other)
 
 
 def forward_kernel(
@@ -348,18 +446,16 @@
         keys_ref[tile_at(t, tile), :] = jnp.transpose(value[HD : 2 * HD, :]).astype(bf16)
 
     move_spans(load, store, sort_ref, tiles, span)
-    allowed = block_mask(size)
+    half = size // 2
 
     def query_block(i, unused):
-        here = tile_at(i, size)
-        queries = sorted_ref[0:HD, here]
-
-        def part(j, carried, masked):
+        def part(start, amount, key_start, keys, carried, offset=None):
             accum, running_max, running_sum = carried
-            there = tile_at(j, size)
+            there = rows_at(key_start, keys, size)
+            queries = sorted_ref[0:HD, rows_at(start, amount, half)]
             scores = jnp.dot(keys_ref[there, :], queries, preferred_element_type=f32)
-            if masked:
-                scores = jnp.where(allowed, scores, masked_score)
+            if offset is not None:
+                scores = causal(scores, offset, masked_score)
             new_max = jnp.maximum(running_max, jnp.max(scores, axis=0, keepdims=True))
             weights = jnp.exp(scores - new_max)
             shrink = jnp.exp(running_max - new_max)
@@ -376,10 +472,19 @@
             jnp.full((1, size), masked_score, f32),
             jnp.zeros((1, size), f32),
         )
-        carried = lax.fori_loop(0, i, functools.partial(part, masked=False), carried)
-        accum, running_max, running_sum = part(i, carried, True)
-        float_ref[:, here] = accum / running_sum
-        log_ref[:, here] = running_max + jnp.log(running_sum)
+        first = i * size
+        carried = lax.fori_loop(
+            0, i, lambda j, carried: part(first, size, j * size, size, carried), carried
+        )
+        for side in range(2):
+            start = first + side * half
+            own = tuple(c[:, side * half : (side + 1) * half] for c in carried)
+            accum, running_max, running_sum = part(
+                start, half, first, (side + 1) * half, own, side * half
+            )
+            here = rows_at(start, half, half)
+            float_ref[:, here] = accum / running_sum
+            log_ref[:, here] = running_max + jnp.log(running_sum)
         return unused
 
     float_ref[...] = jnp.zeros_like(float_ref)
@@ -425,43 +530,49 @@
         values_ref[here, :] = jnp.transpose(sorted_ref[2 * HD :, here].astype(f32)).astype(bf16)
 
     move_spans(load, store, sort_ref, tiles, span)
-    allowed = block_mask(size)
+    half = size // 2
     grads_ref[...] = jnp.zeros_like(grads_ref)
 
     def key_block(j, unused):
-        there = tile_at(j, size)
-        keys = keys_ref[there, :]
-        values = values_ref[there, :]
-        keys_across = sorted_ref[HD : 2 * HD, there]
-
-        def part(i, carried, masked):
+        first_key = j * size
+        there = rows_at(first_key, size, size)
+
+        def part(start, amount, keys, carried, offset=None):
             key_acc, value_acc = carried
-            here = tile_at(i, size)
+            here = rows_at(start, amount, half)
+            near = rows_at(first_key, keys, size)
             queries = sorted_ref[0:HD, here]
             given = given_ref[:, here]
-            scores = jnp.dot(keys, queries, preferred_element_type=f32)
+            scores = jnp.dot(keys_ref[near, :], queries, preferred_element_type=f32)
             probs = jnp.exp(scores - log_ref[:, here])
-            if masked:
-                probs = jnp.where(allowed, probs, 0.0)
-            probs_grad = jnp.dot(values, given, preferred_element_type=f32)
+            if offset is not None:
+                probs = causal(probs, offset, 0.0)
+            probs_grad = jnp.dot(values_ref[near, :], given, preferred_element_type=f32)
             score_low = (probs * (probs_grad - delta_ref[:, here])).astype(bf16)
             value_acc = value_acc + contract(given, probs.astype(bf16), 1, 1)
             key_acc = key_acc + contract(queries, score_low, 1, 1)
             grads_ref[0:HD, here] += jnp.dot(
-                keys_across, score_low, preferred_element_type=f32
+                sorted_ref[HD : 2 * HD, near], score_low, preferred_element_type=f32
             ) * (HD**-0.5)
             return (key_acc, value_acc)
+
+        def diagonal(carried):
+            near = part(first_key, half, half, tuple(c[:, :half] for c in carried), 0)
+            carried = tuple(
+                jnp.concatenate([n, c[:, half:]], axis=1) for n, c in zip(near, carried)
+            )
+            return part(first_key + half, half, size, carried, half)
 
         carried = (jnp.zeros((HD, size), f32), jnp.zeros((HD, size), f32))
         first, last = range_ref[0], range_ref[1]
         carried = lax.cond(
-            jnp.logical_and(j >= first, j < last),
-            lambda c: part(j, c, True),
-            lambda c: c,
-            carried,
+            jnp.logical_and(j >= first, j < last), diagonal, lambda c: c, carried
         )
         carried = lax.fori_loop(
-            jnp.maximum(j + 1, first), last, functools.partial(part, masked=False), carried
+            jnp.maximum(j + 1, first),
+            last,
+            lambda i, carried: part(i * size, size, size, carried),
+            carried,
         )
         grads_ref[HD : 2 * HD, there] = carried[0]
         grads_ref[2 * HD :, there] = carried[1]
@@ -579,7 +690,7 @@
         jnp.where(back_order[None, :] == numbers[:, None], numbers[None, :], 0), axis=1
     )
     total = line * tokens
-    size = min(512, total // copies)
+    size = min(1024, total // copies)
     blocks_each = total // size // copies
     first_block = (place // GROUP) * blocks_each
     query_range = jnp.stack([first_block, first_block + blocks_each]).astype(jnp.int32)
@@ -677,8 +788,12 @@
         values = lax.optimization_barrier(tuple(value for f, p, value in moves) + others)
         return [(f, p, v) for (f, p, unused), v in zip(moves, values)], values[len(moves) :]
 
-    ffn_moves, (blocks,) = held(ffn_pass(near + middle, (0, 1), normed_one), blocks)
-    late_moves = ffn_pass(far, (0,), ffn_moves[-1][2])
+    gathering = slab_gather(after(cotangent, *box["now"]), True)
+    first = next(gathering)
+    ffn_moves = ffn_pass(near + middle, (0,), first[0])
+    ffn_moves, (blocks, *first) = held(ffn_moves, blocks, *first)
+    late_moves = ffn_pass(near + middle, (1,), ffn_moves[-1][2])
+    second = gathering.send(first)
     attended, ordered, floats, logs = attend_forward(
         blocks, sort_order, back_order, query_range, span, size
     )
@@ -691,29 +806,35 @@
         return got[0] if copies == 1 else jnp.sum(got.astype(f32), axis=0).astype(bf16)
 
     own_output = lax.dynamic_slice_in_dim(output_weight, side * heads, heads, 0)
-    late_moves, (attended,) = held(late_moves, attended)
-    last_moves = ffn_pass(far, (1,), attended)
-    late_moves, last_moves = late_moves + last_moves, len(late_moves)
+    late_moves, (attended, *second) = held(late_moves, attended, *second)
+    ffn_moves += late_moves
+    third = gathering.send(second)
+    late_moves = ffn_pass(far, (0,), attended)
 
     def attended_task():
-        (blocks, *moves) = yield [from_heads(attended)] + [
-            v for f, p, v in late_moves[last_moves:]
-        ]
-        box["late_moves"] = late_moves[:last_moves] + [
-            (f, p, v) for (f, p, unused), v in zip(late_moves[last_moves:], moves)
-        ]
+        (blocks,) = yield [from_heads(attended)]
         heads_out = add_copies(blocks).reshape(heads, tokens)
-        added = yield from slab_reduce(contract(heads_out, own_output, 0, 0))
+        added = yield from slab_reduce(
+            lambda start, stop: contract(heads_out[:, start:stop], own_output, 0, 0), tok_dev
+        )
         return (heads_out, inputs.astype(f32) + added)
+
+    def rest_task():
+        got = yield [v for f, p, v in late_moves] + third
+        moves = [(f, p, v) for (f, p, unused), v in zip(late_moves, got)]
+        try:
+            gathering.send(got[len(late_moves) :])
+        except StopIteration as stop:
+            box["cotangent"] = stop.value
+        more = ffn_pass(far, (1,), *box["now"])
+        yield []
+        got = yield [v for f, p, v in more]
+        return moves + [(f, p, v) for (f, p, unused), v in zip(more, got)]
 
     run_tasks(
         [
             ("attended", lambda t, b: True, lambda last: attended_task()),
-            (
-                "cotangent",
-                lambda t, b: t >= 1,
-                lambda last: slab_gather(after(cotangent, *last)),
-            ),
+            ("moves", lambda t, b: True, lambda last: rest_task()),
         ],
         box,
     )
@@ -722,7 +843,7 @@
 
     ffn_full = jnp.zeros((shards, rows, 2 * units), bf16)
     moves = [(0, part, side_columns(ffn_weights[part], 0)) for part in range(2)]
-    for flip, part, block in moves + ffn_moves + box["late_moves"]:
+    for flip, part, block in moves + ffn_moves + box["moves"]:
         ffn_full = lax.dynamic_update_slice(
             ffn_full, block[None], (shard ^ flip, 0, part * units)
         )
@@ -749,8 +870,10 @@
     gate_partial = contract(normed_two, gate_low, 0, 0).astype(bf16).reshape(shards, rows, units)
 
     def attention_back(last):
-        ffn_low = after(jnp.concatenate([gate_low, up_low], axis=1), gate_partial)
-        normed_two_grad = yield from slab_reduce(contract(ffn_low, ffn_full, 1, 1))
+        ffn_low = after(jnp.concatenate([gate_low, up_low], axis=1), gate_partial, *box.get("mixed", ()))
+        normed_two_grad = yield from slab_reduce(
+            lambda start, stop: contract(ffn_low[start:stop], ffn_full, 1, 1), tok_dev
+        )
         residual_part, box["ffn_gain"] = norm_back(residual, gain_two, normed_two_grad)
         residual_grad = cotangent.astype(f32) + residual_part
         branch_low = yield from slab_gather(residual_grad.astype(bf16))
@@ -771,7 +894,9 @@
         low = jnp.concatenate([query_low.reshape(heads, tokens), key_low, value_low], axis=0)
         attn_partial = contract(normed_one, low, 0, 1).astype(bf16)
         (box["attn"],) = yield [to_shards(attn_partial.reshape(shards, rows, -1))]
-        normed_one_grad = yield from slab_reduce(contract(low, attn_weight, 0, 1))
+        normed_one_grad = yield from slab_reduce(
+            lambda start, stop: contract(low[:, start:stop], attn_weight, 0, 1), tok_dev
+        )
         input_part, attn_gain_term = norm_back(inputs.astype(f32), gain_one, normed_one_grad)
         input_grad = residual_grad + input_part
         gain_terms = yield from sum_everywhere(jnp.stack([attn_gain_term, box["ffn_gain"]]))
@@ -780,16 +905,14 @@
     half_rows = rows // 2
 
     def feed_forward_back(last):
-        up_partial = contract(normed_two, after(up_low, gate_partial), 0, 0).astype(bf16)
-        up_partial = up_partial.reshape(shards, rows, units)
-        yield []
-        yield []
-        gate = after(gate_partial, *box["now"])
-        (box["gate0"], up_partial) = yield [to_shards(gate[:, :half_rows]), up_partial]
+        (box["gate0"],) = yield [to_shards(gate_partial[:, :half_rows])]
+        up_partial = contract(normed_two, after(up_low, *box["now"]), 0, 0).astype(bf16)
+        (up_partial,) = yield [up_partial.reshape(shards, rows, units)]
         yield []
         yield []
         gate = after(gate_partial, *box["now"])
         (box["gate1"],) = yield [to_shards(gate[:, half_rows:])]
+        yield []
         up_now = after(up_partial, *box["now"])
         (box["up0"],) = yield [to_shards(up_now[:, :half_rows])]
         up_now = after(up_partial, *box["now"])
@@ -798,55 +921,54 @@
 
     def feed_forward_out(last):
         low = after(hidden, *last)
-        return (yield from slab_reduce(contract(low, own_down, 1, 0)))
+        return (
+            yield from slab_reduce(
+                lambda start, stop: contract(low[start:stop], own_down, 1, 0), tok_dev
+            )
+        )
 
     half_width, half_units = width // 2, units // 2
+
+    steps, block = 4, (half_units // 4, half_width)
 
     def down_chunk(c):
         high, right = c // 2, c % 2
 
-        def make():
-            return down_parts[
-                high * half_units : (high + 1) * half_units,
-                right * half_width : (right + 1) * half_width,
-            ]
+        def source():
+            return down_parts, block, lambda i: (high * steps + i, right)
 
         def put(placed, pieces, sides):
-            step = half_units // 4
             placed["down"] = place_blocks(
                 placed.get("down"),
                 pieces,
                 sides,
                 (halves * units, width),
-                (step, half_width),
-                lambda on, i: (on * 8 + high * 4 + i, right),
+                (half_units // 2, half_width),
+                lambda on, i: (on * 4 + high * 2 + i, right),
             )
 
-        return (make, put)
-
-    def column_chunk(name, c, cut, entries):
-        size = rows // cut
-
-        def make():
-            if cut == 4:
-                source, start = box[name + str(c // 2)], (c % 2) * size
-            else:
-                source, start = box[name], c * size
-            return source[:, start : start + size].reshape(shards * size, -1)
+        return (source, put)
+
+    def column_chunk(name, c):
+        size = rows // 4
+        each = shards // steps
+
+        def source():
+            return (
+                box[name + str(c // 2)],
+                (each, size, units),
+                lambda i: (i, c % 2, 0),
+            )
 
         def put(placed, pieces, sides):
-            pieces = [piece.reshape(shards, size, -1) for piece in pieces]
-            for key, place_part, columns in entries:
-                placed[key] = place_part(
-                    placed.get(key), [piece[..., columns] for piece in pieces], c, sides, cut
-                )
-
-        return (make, put)
+            pieces = [piece.reshape(shards, size, units) for piece in pieces]
+            placed[name] = place_columns(placed.get(name), pieces, c, sides, 4)
+
+        return (source, put)
 
     def output_chunk():
-        def make():
-            partial = box["output_parts"]
-            return jnp.concatenate([partial[:, :half_width], partial[:, half_width:]], axis=0)
+        def source():
+            return box["output_parts"], block, lambda i: (i % 2, i // 2)
 
         def put(placed, pieces, sides):
             placed["output"] = place_blocks(
@@ -858,39 +980,53 @@
                 lambda on, i: (on, i),
             )
 
-        return (make, put)
-
-    everything = slice(None)
+        return (source, put)
+
+    def attn_chunk(c):
+        size, columns = rows // 2, heads + 2 * HD
+        beside = 2
+        over = shards // beside
+
+        def source():
+            part = box["attn"][:, c * size : (c + 1) * size].reshape(over, beside, size, columns)
+            part = part.swapaxes(1, 2).reshape(over * size, beside * columns)
+            part = jnp.pad(part, ((0, 0), (0, half_width - beside * columns)))
+            return part, block, lambda i: (i, 0)
+
+        def put(placed, pieces, sides):
+            cut = [
+                piece[:, : beside * columns]
+                .reshape(over, size, beside, columns)
+                .swapaxes(1, 2)
+                .reshape(shards, size, columns)
+                for piece in pieces
+            ]
+            for key, place_part, start, stop in (
+                ("query", place_columns, 0, heads),
+                ("key", place_narrow, heads, heads + HD),
+                ("value", place_narrow, heads + HD, columns),
+            ):
+                placed[key] = place_part(
+                    placed.get(key), [piece[..., start:stop] for piece in cut], c, sides, 2
+                )
+
+        return (source, put)
+
     chunks = [down_chunk(c) for c in range(4)]
-    for name in ("gate", "up"):
-        chunks += [
-            column_chunk(name, c, 4, [(name, place_columns, everything)]) for c in range(4)
-        ]
-    chunks += [output_chunk()]
-    chunks += [
-        column_chunk(
-            "attn",
-            c,
-            2,
-            [
-                ("query", place_columns, slice(0, heads)),
-                ("key", place_narrow, slice(heads, heads + HD)),
-                ("value", place_narrow, slice(heads + HD, heads + 2 * HD)),
-            ],
-        )
-        for c in range(2)
-    ]
+    chunks += [column_chunk(name, c) for name in ("gate", "up") for c in range(4)]
+    chunks += [output_chunk()] + [attn_chunk(c) for c in range(2)]
     placed = {}
+    gradients = stream(chunks, placed, box, steps, block)
+    sent = gradients.send(lax.optimization_barrier(tuple(next(gradients))))
     run_tasks(
         [
             ("attention", lambda t, b: True, attention_back),
             ("parts", lambda t, b: True, feed_forward_back),
-            ("even", lambda t, b: True, lambda last: stream(chunks[0::2], placed), 0),
-            ("odd", lambda t, b: True, lambda last: stream(chunks[1::2], placed), 1),
             ("out", lambda t, b: t >= 1, feed_forward_out),
         ],
         box,
     )
+    finish(gradients, sent)
     input_grad, gain_terms = box["attention"]
     gain_terms = lax.dynamic_slice_in_dim(gain_terms, shard * rows, rows, 1)
     return (

time: 1020 us -> 928 us (0.910)
  other arithmetic: 137 us -> 44.7 us
  waiting for transfers between devices: 332 us -> 289 us
  Pallas kernels: 133 us -> 167 us
  starting transfers between devices: 212 us -> 191 us
  local copies, waits for them, and re-layouts: 117 us -> 136 us
  matrix products: 71.4 us -> 84.5 us
    pallas_call x0 -> x18, Pallas kernels: none -> 49.3 us  [mix(): pl.pallas_call(functools.partial(mix_kernel, tuple(names) + tuple(results...]
    select_n x24 -> x0, other arithmetic: 47.9 us -> none  [the longest x9 25.2 us: stream(): both = jnp.where(outer, parts[going], totals[coming])]
    convert_element_type x20 -> x0, other arithmetic: 31.1 us -> none  [the longest x13 26.5 us: stream(): sums[going] = (part.astype(f32) + moves['in'].astype(f32)).astype(bf16)]
    dynamic_update_slice x40 -> x38, local copies, waits for them, and re-layouts: 22.4 us -> 40.8 us  [put(): lax.dynamic_update_slice(total, piece, (index * half,) + (0,) * (block.nd...]
    ppermute x21 -> x17, waiting for transfers between devices: 89.7 us -> 72.7 us  [stream(): moves['got'] = lax.ppermute(sending, 'line', pairs)]
    ppermute x21 -> x17, starting transfers between devices: 72.5 us -> 56.1 us  [stream(): moves['got'] = lax.ppermute(sending, 'line', pairs)]
    ppermute x15, waiting for transfers between devices: 40.8 us -> 56 us  [stream(): lax.ppermute(owns[stage - 3], 'xpart', [(i, (i + turn) % halves) for i in...]
    slice x24 -> x10, local copies, waits for them, and re-layouts: 24.1 us -> 9.49 us  [the longest x4 5.38 us: put(): piece[:, :beside * columns].reshape(over, size, beside, columns)]
  transfers between devices with their start and end apart: 134 -> 128, of which waited for: 48 -> 46; matrix products, arithmetic and copies ran while one was open for 23% -> 21% of each run, Pallas kernels for 13% -> 18%
where the time goes in v3:
time: 928 us; the launch traced here: 914 us
  waiting for transfers between devices  289 us (31%)
  starting transfers between devices  191 us (21%)
  Pallas kernels  167 us (18%)
  local copies, waits for them, and re-layouts  136 us (15%)
  matrix products  84.5 us (9%)
  other arithmetic  44.7 us (5%)
    ppermute x57, waiting for transfers between devices, swap(): return lax.ppermute(value, SLAB, [(i, i ^ flip) for i in range(KVH)])  91.9 us
    dot_general x17, matrix products, contract(): lax.dot_general(left, right, (((left_dim,), (right_dim,)), ((), ())), pre...  84.5 us
    ppermute x17, waiting for transfers between devices, stream(): moves['got'] = lax.ppermute(sending, 'line', pairs)  72.7 us
    ppermute x17, starting transfers between devices, stream(): moves['got'] = lax.ppermute(sending, 'line', pairs)  56.1 us
    ppermute x15, waiting for transfers between devices, stream(): lax.ppermute(owns[stage - 3], 'xpart', [(i, (i + turn) % halves) for i in...  56 us
    ppermute x12, waiting for transfers between devices, pass_on(): return lax.ppermute(block, 'wshard', [(i, i ^ flip) for i in range(shards)])  50.4 us
    pallas_call x18, Pallas kernels, mix(): pl.pallas_call(functools.partial(mix_kernel, tuple(names) + tuple(results...  49.3 us
    ppermute x57, starting transfers between devices, swap(): return lax.ppermute(value, SLAB, [(i, i ^ flip) for i in range(KVH)])  42.7 us
  transfers between devices with their start and end apart: 128, of which 46 were waited for; matrix products, arithmetic and copies ran while one was open for 21% of the time, Pallas kernels for 18%

profile of v3, /device:TPU:0, one launch (start us, length us, event | category | flops | bytes accessed | tf_op | source)
XLA Modules:
  0.0 914.3 jit_solution(14374796731352592747)
XLA Ops:
  42.0 7.1 collective-permute-done.8
  54.4 9.3 %collective-permute-done.14 = bf16[512,384]{1,0:T(8,128)(2,1)S(1)} collective-permute-done((bf16[512,384]{1,0:T(8,128)(2,1)S(1)}, bf16[512,384]{1,0:T(8,128)(2,1)S(1)}, u32[]{:S(2)}, u32[]{:S(2)}) %collective-permute-start.14) | collective-permute-done | bytes 393248 | tf_op jit(solution)/shard_map/ppermute | solution.py:704
  74.0 5.0 all-to-all-start
  79.5 13.2 %collective-permute-done.15 = bf16[128,2048]{1,0:T(8,128)(2,1)S(1)} collective-permute-done((bf16[128,2048]{1,0:T(8,128)(2,1)S(1)}, bf16[128,2048]{1,0:T(8,128)(2,1)S(1)}, u32[]{:S(2)}, u32[]{:S(2)}) %collective-permute-start.15) | collective-permute-done | bytes 524320 | tf_op jit(solution)/shard_map/ppermute | solution.py:49
  101.6 8.9 collective-permute-done.18
  110.4 11.2 %collective-permute-done.17 = bf16[512,1024]{1,0:T(8,128)(2,1)} collective-permute-done((bf16[512,1024]{1,0:T(8,128)(2,1)}, bf16[512,1024]{1,0:T(8,128)(2,1)}, u32[]{:S(2)}, u32[]{:S(2)}) %collective-permute-start.17) | collective-permute-done | bytes 1048608 | tf_op jit(solution)/shard_map/ppermute | solution.py:704
  125.9 22.3 %attend_forward.1 = (bf16[4,64,1024]{2,1,0:T(8,128)(2,1)}, bf16[192,4096]{1,0:T(8,128)(2,1)}, f32[64,4096]{1,0:T(8,128)}, f32[1,4096]{1,0:T(1,128)}) custom-call(s32[64]{0:T(128)} %select_reduce_fusion.sort_ref, s32[64]{0:T(128)} %copy-done.103, s32[2]{0:T(128)} %pad_add_fusion.range_ref, bf16[4,192,1024]{2,1,0:T(8,128)(2,1)} %all-to-all-done.blocks_ref), custom_call_target="tpu_custom_call" | custom-call | flops 30000001024 | bytes 8000000 | tf_op jit(solution)/shard_map/attend_forward/pallas_call | solution.py:594
  156.9 4.8 all-to-all-start.1
  169.2 7.1 all-to-all-done.1
  196.0 18.4 %collective-permute-done.30 = bf16[512,1024]{1,0:T(8,128)(2,1)S(1)} collective-permute-done((bf16[512,1024]{1,0:T(8,128)(2,1)S(1)}, bf16[512,1024]{1,0:T(8,128)(2,1)S(1)}, u32[]{:S(2)}, u32[]{:S(2)}) %collective-permute-start.30) | collective-permute-done | bytes 1048608 | tf_op jit(solution)/shard_map/ppermute | solution.py:704
  214.4 11.7 %collective-permute-done.29 = bf16[2,128,1024]{2,1,0:T(8,128)(2,1)S(1)} collective-permute-done((bf16[2,128,1024]{2,1,0:T(8,128)(2,1)S(1)}, bf16[2,128,1024]{2,1,0:T(8,128)(2,1)S(1)}, u32[]{:S(2)}, u32[]{:S(2)}) %collective-permute-start.29) | collective-permute-done | bytes 524320 | tf_op jit(solution)/shard_map/ppermute | solution.py:49
  228.2 7.0 fusion.7
  241.9 8.6 collective-permute-done.33
  260.1 8.8 fusion.89
  272.9 8.1 convolution_convert_fusion.1.refs_0_.refs_1_
  287.6 6.2 convolution_convert_fusion.2
  293.8 14.0 %collective-permute-done.42.refs_2_ = bf16[512,1024]{1,0:T(8,128)(2,1)S(1)} collective-permute-done((bf16[512,1024]{1,0:T(8,128)(2,1)S(1)}, bf16[512,1024]{1,0:T(8,128)(2,1)S(1)}, u32[]{:S(2)}, u32[]{:S(2)}) %collective-permute-start.42) | collective-permute-done | bytes 1048608 | tf_op jit(solution)/shard_map/ppermute | solution.py:247
  310.7 5.8 convolution_convert_fusion.5
  327.6 22.5 %collective-permute-done.72.refs_2_ = bf16[512,1024]{1,0:T(8,128)(2,1)S(1)} collective-permute-done((bf16[512,1024]{1,0:T(8,128)(2,1)}, bf16[512,1024]{1,0:T(8,128)(2,1)S(1)}, u32[]{:S(2)}, u32[]{:S(2)}) %collective-permute-start.72) | collective-permute-done | bytes 1048608 | tf_op jit(solution)/shard_map/ppermute | solution.py:247
  360.7 5.0 fusion.9
  365.8 8.7 convert_add_fusion.2
  377.1 6.6 convolution_convert_fusion
  401.6 10.0 %collective-permute-done.48 = bf16[128,1024]{1,0:T(8,128)(2,1)S(1)} collective-permute-done((bf16[128,1024]{1,0:T(8,128)(2,1)S(1)}, bf16[128,1024]{1,0:T(8,128)(2,1)S(1)}, u32[]{:S(2)}, u32[]{:S(2)}) %collective-permute-start.48) | collective-permute-done | bytes 262176 | tf_op jit(solution)/shard_map/ppermute | solution.py:49
  417.3 5.4 collective-permute-done.76.refs_2_
  423.9 13.8 %collective-permute-done.78.refs_1_ = bf16[512,1024]{1,0:T(8,128)(2,1)S(1)} collective-permute-done((bf16[512,1024]{1,0:T(8,128)(2,1)S(1)}, bf16[512,1024]{1,0:T(8,128)(2,1)S(1)}, u32[]{:S(2)}, u32[]{:S(2)}) %collective-permute-start.78) | collective-permute-done | bytes 1048608 | tf_op jit(solution)/shard_map/ppermute | solution.py:252
  444.5 7.6 collective-permute-done.55
  467.5 9.2 %collective-permute-done.81.refs_1_ = bf16[512,1024]{1,0:T(8,128)(2,1)} collective-permute-done((bf16[512,1024]{1,0:T(8,128)(2,1)S(1)}, bf16[512,1024]{1,0:T(8,128)(2,1)}, u32[]{:S(2)}, u32[]{:S(2)}) %collective-permute-start.81) | collective-permute-done | bytes 1048608 | tf_op jit(solution)/shard_map/ppermute | solution.py:252
  514.8 4.9 place_blocks.6.refs_2_
  526.0 8.1 collective-permute-start.85
  541.9 5.1 place_blocks.7.refs_2_
  546.9 6.7 collective-permute-done.85.refs_2_
  566.6 4.9 place_blocks.8
  592.5 33.0 %attend_backward.1 = bf16[4,192,1024]{2,1,0:T(8,128)(2,1)} custom-call(s32[64]{0:T(128)} %select_reduce_fusion.sort_ref, s32[64]{0:T(128)} %copy-done.103, s32[2]{0:T(128)} %pad_add_fusion.range_ref, bf16[192,4096]{1,0:T(8,128)(2,1)} %get-tuple-element.278.sorted_ref, f32[64,4096]{1,0:T(8,128)} %get-tuple-element.279.float_ref, ...), custom_call_target="tpu_custom_call" | custom-call | flops 35999997952 | bytes 8000000 | tf_op jit(solution)/shard_map/attend_backward/pallas_call | solution.py:620
  632.0 4.8 place_columns.10.refs_2_
  647.4 9.4 %all-to-all-done.7 = bf16[4,128,1024]{2,1,0:T(8,128)(2,1)} async-done(((bf16[4,128,1024]{2,1,0:T(8,128)(2,1)}), bf16[4,128,1024]{2,1,0:T(8,128)(2,1)}, u32[]{:S(2)}, u32[]{:S(2)}) %all-to-all-start.7) | async-done | bytes 1048608 | tf_op jit(solution)/shard_map/all_to_all | solution.py:802
  661.4 4.8 place_columns.11.refs_2_
  666.3 8.2 collective-permute-done.94.refs_2_
  678.5 11.4 %collective-permute-start.97 = (bf16[512,1024]{1,0:T(8,128)(2,1)}, bf16[512,1024]{1,0:T(8,128)(2,1)}, u32[]{:S(2)}, u32[]{:S(2)}) collective-permute-start(bf16[512,1024]{1,0:T(8,128)(2,1)} %get-tuple-element.359.refs_5_), channel_id=1, source_target_pairs={{0,8},{24,16},{8,0},{16,24},{1,9},{25,17},{9,1},{17,25},{2,10},{26... | collective-permute-start | bytes 3145736 | tf_op jit(solution)/shard_map/ppermute | solution.py:247
  699.2 4.8 place_columns.12.refs_2_
  704.0 7.9 collective-permute-done.97.refs_2_
  722.0 5.0 place_columns.13
  760.6 4.8 place_columns.14.refs_2_
  769.2 8.6 collective-permute-done.105
  798.9 4.6 place_columns.15.refs_2_
  803.6 5.2 collective-permute-done.108
  817.8 4.6 place_columns.16.refs_2_
  828.1 7.4 collective-permute-done.111
  840.8 16.0 %collective-permute-done.69 = f32[2,2048]{1,0:T(2,128)S(1)} collective-permute-done((f32[2,2048]{1,0:T(2,128)S(1)}, f32[2,2048]{1,0:T(2,128)S(1)}, u32[]{:S(2)}, u32[]{:S(2)}) %collective-permute-start.69) | collective-permute-done | bytes 16416 | tf_op jit(solution)/shard_map/ppermute | solution.py:49
  (700 shorter events, 474.3 us)
Async XLA Ops:
  20.4 28.7 %collective-permute-start.6 = (bf16[128,2048]{1,0:T(8,128)(2,1)}, bf16[128,2048]{1,0:T(8,128)(2,1)S(1)}, u32[]{:S(2)}, u32[]{:S(2)}) collective-permute-start(bf16[128,2048]{1,0:T(8,128)(2,1)} %collective-permute-done), channel_id=1, source_target_pairs={{0,1},{1,0},{2,3},{3,2},{4,5},{5,4},{6,7},{7,6},{8,9},{9,8},{10,11... | collective-permute-start | bytes 1572872 | tf_op jit(solution)/shard_map/ppermute | solution.py:49
  22.4 26.7 %collective-permute-start.7 = (bf16[128,2048]{1,0:T(8,128)(2,1)}, bf16[128,2048]{1,0:T(8,128)(2,1)S(1)}, u32[]{:S(2)}, u32[]{:S(2)}) collective-permute-start(bf16[128,2048]{1,0:T(8,128)(2,1)} %collective-permute-done.1), channel_id=1, source_target_pairs={{0,1},{1,0},{2,3},{3,2},{4,5},{5,4},{6,7},{7,6},{8,9},{9,8},{10,11... | collective-permute-start | bytes 1572872 | tf_op jit(solution)/shard_map/ppermute | solution.py:49
  74.0 47.6 %all-to-all-start = ((bf16[4,192,1024]{2,1,0:T(8,128)(2,1)}), bf16[4,192,1024]{2,1,0:T(8,128)(2,1)}, u32[]{:S(2)}, u32[]{:S(2)}) async-start(bf16[4,192,1024]{2,1,0:T(8,128)(2,1)} %pad_maximum_fusion.1), calls=%async_computation | async-start | bytes 3145728 | tf_op jit(solution)/shard_map/all_to_all | solution.py:778
  95.7 25.9 %collective-permute-start.17 = (bf16[512,1024]{1,0:T(8,128)(2,1)}, bf16[512,1024]{1,0:T(8,128)(2,1)}, u32[]{:S(2)}, u32[]{:S(2)}) collective-permute-start(bf16[512,1024]{1,0:T(8,128)(2,1)} %get-tuple-element.426), channel_id=1, source_target_pairs={{0,2},{1,3},{2,0},{3,1},{4,6},{5,7},{6,4},{7,5},{8,10},{9,11},{10,... | collective-permute-start | bytes 3145736 | tf_op jit(solution)/shard_map/ppermute | solution.py:704
  121.6 27.4 %collective-permute-start.22 = (bf16[128,2048]{1,0:T(8,128)(2,1)S(1)}, bf16[128,2048]{1,0:T(8,128)(2,1)S(1)}, u32[]{:S(2)}, u32[]{:S(2)}) collective-permute-start(bf16[128,2048]{1,0:T(8,128)(2,1)S(1)} %collective-permute-done.15), channel_id=1, source_target_pairs={{0,4},{1,5},{2,6},{3,7},{4,0},{5,1},{6,2},{7,3},{8,12},{9,13},{10,... | collective-permute-start | bytes 1572872 | tf_op jit(solution)/shard_map/ppermute | solution.py:49
  123.1 26.0 %collective-permute-start.23 = (bf16[128,2048]{1,0:T(8,128)(2,1)S(1)}, bf16[128,2048]{1,0:T(8,128)(2,1)S(1)}, u32[]{:S(2)}, u32[]{:S(2)}) collective-permute-start(bf16[128,2048]{1,0:T(8,128)(2,1)S(1)} %collective-permute-done.15), channel_id=1, source_target_pairs={{0,1},{1,0},{2,3},{3,2},{4,5},{5,4},{6,7},{7,6},{8,9},{9,8},{10,11... | collective-permute-start | bytes 1572872 | tf_op jit(solution)/shard_map/ppermute | solution.py:49
  124.8 24.3 %collective-permute-start.20 = (bf16[512,1024]{1,0:T(8,128)(2,1)S(1)}, bf16[512,1024]{1,0:T(8,128)(2,1)S(1)}, u32[]{:S(2)}, u32[]{:S(2)}) collective-permute-start(bf16[512,1024]{1,0:T(8,128)(2,1)S(1)} %get-tuple-element.425), channel_id=1, source_target_pairs={{0,1},{1,0},{2,3},{3,2},{4,5},{5,4},{6,7},{7,6},{8,9},{9,8},{10,11... | collective-permute-start | bytes 3145736 | tf_op jit(solution)/shard_map/ppermute | solution.py:704
  125.4 25.1 %collective-permute-start.21 = (bf16[512,1024]{1,0:T(8,128)(2,1)S(1)}, bf16[512,1024]{1,0:T(8,128)(2,1)S(1)}, u32[]{:S(2)}, u32[]{:S(2)}) collective-permute-start(bf16[512,1024]{1,0:T(8,128)(2,1)S(1)} %get-tuple-element.424), channel_id=1, source_target_pairs={{0,2},{1,3},{2,0},{3,1},{4,6},{5,7},{6,4},{7,5},{8,10},{9,11},{10,... | collective-permute-start | bytes 3145736 | tf_op jit(solution)/shard_map/ppermute | solution.py:704
  153.8 25.5 %collective-permute-start.25 = (bf16[512,1024]{1,0:T(8,128)(2,1)}, bf16[512,1024]{1,0:T(8,128)(2,1)}, u32[]{:S(2)}, u32[]{:S(2)}) collective-permute-start(bf16[512,1024]{1,0:T(8,128)(2,1)} %constant_dynamic-slice_fusion.3), channel_id=1, source_target_pairs={{0,3},{1,2},{2,1},{3,0},{4,7},{5,6},{6,5},{7,4},{8,11},{9,10},{10,... | collective-permute-start | bytes 3145736 | tf_op jit(solution)/shard_map/ppermute | solution.py:704
  189.3 25.1 %collective-permute-start.30 = (bf16[512,1024]{1,0:T(8,128)(2,1)S(1)}, bf16[512,1024]{1,0:T(8,128)(2,1)S(1)}, u32[]{:S(2)}, u32[]{:S(2)}) collective-permute-start(bf16[512,1024]{1,0:T(8,128)(2,1)S(1)} %constant_dynamic-slice_fusion.2), channel_id=1, source_target_pairs={{0,3},{1,2},{2,1},{3,0},{4,7},{5,6},{6,5},{7,4},{8,11},{9,10},{10,... | collective-permute-start | bytes 3145736 | tf_op jit(solution)/shard_map/ppermute | solution.py:704
  193.2 32.8 %collective-permute-start.29 = (bf16[2,128,1024]{2,1,0:T(8,128)(2,1)S(1)}, bf16[2,128,1024]{2,1,0:T(8,128)(2,1)S(1)}, u32[]{:S(2)}, u32[]{:S(2)}) collective-permute-start(bf16[2,128,1024]{2,1,0:T(8,128)(2,1)S(1)} %slice.485), channel_id=1, source_target_pairs={{0,2},{1,3},{2,0},{3,1},{4,6},{5,7},{6,4},{7,5},{8,10},{9,11},{10,... | collective-permute-start | bytes 1572872 | tf_op jit(solution)/shard_map/ppermute | solution.py:49
  281.4 26.4 %collective-permute-start.42 = (bf16[512,1024]{1,0:T(8,128)(2,1)S(1)}, bf16[512,1024]{1,0:T(8,128)(2,1)S(1)}, u32[]{:S(2)}, u32[]{:S(2)}) collective-permute-start(bf16[512,1024]{1,0:T(8,128)(2,1)S(1)} %mix.18), channel_id=1, source_target_pairs={{0,8},{24,16},{1,9},{25,17},{2,10},{26,18},{3,11},{27,19},{4,12},{... | collective-permute-start | bytes 3145736 | tf_op jit(solution)/shard_map/ppermute | solution.py:247
  316.5 44.2 %collective-permute-start.43 = (bf16[512,2048]{1,0:T(8,128)(2,1)}, bf16[512,2048]{1,0:T(8,128)(2,1)}, u32[]{:S(2)}, u32[]{:S(2)}) collective-permute-start(bf16[512,2048]{1,0:T(8,128)(2,1)} %convolution_convert_fusion.5), channel_id=1, source_target_pairs={{0,1},{1,0},{2,3},{3,2},{4,5},{5,4},{6,7},{7,6},{8,9},{9,8},{10,11... | collective-permute-start | bytes 6291464 | tf_op jit(solution)/shard_map/ppermute | solution.py:49
  318.0 42.7 %all-to-all-start.2 = ((bf16[4,256,1024]{2,1,0:T(8,128)(2,1)}), bf16[4,256,1024]{2,1,0:T(8,128)(2,1)}, u32[]{:S(2)}, u32[]{:S(2)}) async-start(bf16[4,256,1024]{2,1,0:T(8,128)(2,1)} %slice.615), calls=%async_computation.2 | async-start | bytes 4194304 | tf_op jit(solution)/shard_map/all_to_all | solution.py:868
  322.5 27.6 %collective-permute-start.72 = (bf16[512,1024]{1,0:T(8,128)(2,1)}, bf16[512,1024]{1,0:T(8,128)(2,1)S(1)}, u32[]{:S(2)}, u32[]{:S(2)}) collective-permute-start(bf16[512,1024]{1,0:T(8,128)(2,1)} %copy-done.21), channel_id=1, source_target_pairs={{0,8},{24,16},{1,9},{25,17},{2,10},{26,18},{3,11},{27,19},{4,12},{... | collective-permute-start | bytes 3145736 | tf_op jit(solution)/shard_map/ppermute | solution.py:247
  355.2 39.9 %collective-permute-start.74 = (bf16[512,1024]{1,0:T(8,128)(2,1)}, bf16[512,1024]{1,0:T(8,128)(2,1)}, u32[]{:S(2)}, u32[]{:S(2)}) collective-permute-start(bf16[512,1024]{1,0:T(8,128)(2,1)} %get-tuple-element.310.refs_5_), channel_id=1, source_target_pairs={{0,8},{24,16},{8,0},{16,24},{1,9},{25,17},{9,1},{17,25},{2,10},{26... | collective-permute-start | bytes 3145736 | tf_op jit(solution)/shard_map/ppermute | solution.py:247
  359.0 36.8 %collective-permute-start.75 = (bf16[512,1024]{1,0:T(8,128)(2,1)S(1)}, bf16[512,1024]{1,0:T(8,128)(2,1)}, u32[]{:S(2)}, u32[]{:S(2)}) collective-permute-start(bf16[512,1024]{1,0:T(8,128)(2,1)S(1)} %get-tuple-element.311.refs_3_), channel_id=1, source_target_pairs={{8,16},{16,8},{9,17},{17,9},{10,18},{18,10},{11,19},{19,11},{12,20... | collective-permute-start | bytes 3145736 | tf_op jit(solution)/shard_map/ppermute | solution.py:249
  398.3 24.4 %collective-permute-start.76 = (bf16[512,1024]{1,0:T(8,128)(2,1)S(1)}, bf16[512,1024]{1,0:T(8,128)(2,1)S(1)}, u32[]{:S(2)}, u32[]{:S(2)}) collective-permute-start(bf16[512,1024]{1,0:T(8,128)(2,1)S(1)} %get-tuple-element.314.refs_5_), channel_id=1, source_target_pairs={{0,8},{24,16},{8,0},{16,24},{1,9},{25,17},{9,1},{17,25},{2,10},{26... | collective-permute-start | bytes 3145736 | tf_op jit(solution)/shard_map/ppermute | solution.py:247
  411.5 26.1 %collective-permute-start.78 = (bf16[512,1024]{1,0:T(8,128)(2,1)S(1)}, bf16[512,1024]{1,0:T(8,128)(2,1)S(1)}, u32[]{:S(2)}, u32[]{:S(2)}) collective-permute-start(bf16[512,1024]{1,0:T(8,128)(2,1)S(1)} %get-tuple-element.316.refs_0_), channel_id=1, source_target_pairs={{0,4},{4,0},{1,5},{5,1},{2,6},{6,2},{3,7},{7,3},{8,12},{12,8},{9,1... | collective-permute-start | bytes 3145736 | tf_op jit(solution)/shard_map/ppermute | solution.py:252
  414.9 38.8 %collective-permute-start.51 = (bf16[128,2048]{1,0:T(8,128)(2,1)S(1)}, bf16[128,2048]{1,0:T(8,128)(2,1)S(1)}, u32[]{:S(2)}, u32[]{:S(2)}) collective-permute-start(bf16[128,2048]{1,0:T(8,128)(2,1)S(1)} %get-tuple-element.417), channel_id=1, source_target_pairs={{0,2},{1,3},{2,0},{3,1},{4,6},{5,7},{6,4},{7,5},{8,10},{9,11},{10,... | collective-permute-start | bytes 1572872 | tf_op jit(solution)/shard_map/ppermute | solution.py:49
  416.2 38.0 %collective-permute-start.52 = (bf16[128,2048]{1,0:T(8,128)(2,1)S(1)}, bf16[128,2048]{1,0:T(8,128)(2,1)S(1)}, u32[]{:S(2)}, u32[]{:S(2)}) collective-permute-start(bf16[128,2048]{1,0:T(8,128)(2,1)S(1)} %get-tuple-element.417), channel_id=1, source_target_pairs={{0,4},{1,5},{2,6},{3,7},{4,0},{5,1},{6,2},{7,3},{8,12},{9,13},{10,... | collective-permute-start | bytes 1572872 | tf_op jit(solution)/shard_map/ppermute | solution.py:49
  422.7 31.6 %collective-permute-start.53 = (bf16[128,2048]{1,0:T(8,128)(2,1)S(1)}, bf16[128,2048]{1,0:T(8,128)(2,1)S(1)}, u32[]{:S(2)}, u32[]{:S(2)}) collective-permute-start(bf16[128,2048]{1,0:T(8,128)(2,1)S(1)} %get-tuple-element.417), channel_id=1, source_target_pairs={{0,1},{1,0},{2,3},{3,2},{4,5},{5,4},{6,7},{7,6},{8,9},{9,8},{10,11... | collective-permute-start | bytes 1572872 | tf_op jit(solution)/shard_map/ppermute | solution.py:49
  457.4 41.2 %all-to-all-start.3 = ((bf16[4,256,1024]{2,1,0:T(8,128)(2,1)}), bf16[4,256,1024]{2,1,0:T(8,128)(2,1)}, u32[]{:S(2)}, u32[]{:S(2)}) async-start(bf16[4,256,1024]{2,1,0:T(8,128)(2,1)} %slice.521), calls=%async_computation.3 | async-start | bytes 4194304 | tf_op jit(solution)/shard_map/all_to_all | solution.py:868
  481.0 38.7 %collective-permute-start.82 = (bf16[512,1024]{1,0:T(8,128)(2,1)}, bf16[512,1024]{1,0:T(8,128)(2,1)}, u32[]{:S(2)}, u32[]{:S(2)}) collective-permute-start(bf16[512,1024]{1,0:T(8,128)(2,1)} %get-tuple-element.325.refs_5_), channel_id=1, source_target_pairs={{0,8},{24,16},{8,0},{16,24},{1,9},{25,17},{9,1},{17,25},{2,10},{26... | collective-permute-start | bytes 3145736 | tf_op jit(solution)/shard_map/ppermute | solution.py:247
  495.5 24.2 %collective-permute-start.83 = (bf16[512,1024]{1,0:T(8,128)(2,1)}, bf16[512,1024]{1,0:T(8,128)(2,1)}, u32[]{:S(2)}, u32[]{:S(2)}) collective-permute-start(bf16[512,1024]{1,0:T(8,128)(2,1)} %get-tuple-element.326.refs_3_), channel_id=1, source_target_pairs={{8,16},{16,8},{9,17},{17,9},{10,18},{18,10},{11,19},{19,11},{12,20... | collective-permute-start | bytes 3145736 | tf_op jit(solution)/shard_map/ppermute | solution.py:249
  497.1 24.7 %collective-permute-start.84 = (bf16[512,1024]{1,0:T(8,128)(2,1)}, bf16[512,1024]{1,0:T(8,128)(2,1)}, u32[]{:S(2)}, u32[]{:S(2)}) collective-permute-start(bf16[512,1024]{1,0:T(8,128)(2,1)} %get-tuple-element.327.refs_0_), channel_id=1, source_target_pairs={{0,4},{4,0},{1,5},{5,1},{2,6},{6,2},{3,7},{7,3},{8,12},{12,8},{9,1... | collective-permute-start | bytes 3145736 | tf_op jit(solution)/shard_map/ppermute | solution.py:252
  511.0 26.2 %all-to-all-start.4 = ((bf16[4,64,1024]{2,1,0:T(8,128)(2,1)}), bf16[4,64,1024]{2,1,0:T(8,128)(2,1)S(1)}, u32[]{:S(2)}, u32[]{:S(2)}) async-start(bf16[4,64,1024]{2,1,0:T(8,128)(2,1)} %bitcast.284), calls=%async_computation.4 | async-start | bytes 1048576 | tf_op jit(solution)/shard_map/all_to_all | solution.py:882
  526.0 27.7 %collective-permute-start.85 = (bf16[512,1024]{1,0:T(8,128)(2,1)}, bf16[512,1024]{1,0:T(8,128)(2,1)}, u32[]{:S(2)}, u32[]{:S(2)}) collective-permute-start(bf16[512,1024]{1,0:T(8,128)(2,1)} %get-tuple-element.332.refs_5_), channel_id=1, source_target_pairs={{0,8},{24,16},{8,0},{16,24},{1,9},{25,17},{9,1},{17,25},{2,10},{26... | collective-permute-start | bytes 3145736 | tf_op jit(solution)/shard_map/ppermute | solution.py:247
  538.0 33.5 %all-to-all-start.5 = ((bf16[4,256,1024]{2,1,0:T(8,128)(2,1)}), bf16[4,256,1024]{2,1,0:T(8,128)(2,1)S(1)}, u32[]{:S(2)}, u32[]{:S(2)}) async-start(bf16[4,256,1024]{2,1,0:T(8,128)(2,1)} %slice.522), calls=%async_computation.5 | async-start | bytes 4194304 | tf_op jit(solution)/shard_map/all_to_all | solution.py:868
  575.3 50.1 %all-to-all-start.6 = ((bf16[4,256,1024]{2,1,0:T(8,128)(2,1)}), bf16[4,256,1024]{2,1,0:T(8,128)(2,1)S(1)}, u32[]{:S(2)}, u32[]{:S(2)}) async-start(bf16[4,256,1024]{2,1,0:T(8,128)(2,1)} %slice.523), calls=%async_computation.6 | async-start | bytes 4194304 | tf_op jit(solution)/shard_map/all_to_all | solution.py:868
  586.7 50.2 %collective-permute-start.91 = (bf16[512,1024]{1,0:T(8,128)(2,1)}, bf16[512,1024]{1,0:T(8,128)(2,1)}, u32[]{:S(2)}, u32[]{:S(2)}) collective-permute-start(bf16[512,1024]{1,0:T(8,128)(2,1)} %get-tuple-element.346.refs_5_), channel_id=1, source_target_pairs={{0,8},{24,16},{8,0},{16,24},{1,9},{25,17},{9,1},{17,25},{2,10},{26... | collective-permute-start | bytes 3145736 | tf_op jit(solution)/shard_map/ppermute | solution.py:247
  589.3 47.6 %collective-permute-start.92 = (bf16[512,1024]{1,0:T(8,128)(2,1)}, bf16[512,1024]{1,0:T(8,128)(2,1)}, u32[]{:S(2)}, u32[]{:S(2)}) collective-permute-start(bf16[512,1024]{1,0:T(8,128)(2,1)} %get-tuple-element.347.refs_3_), channel_id=1, source_target_pairs={{8,16},{16,8},{9,17},{17,9},{10,18},{18,10},{11,19},{19,11},{12,20... | collective-permute-start | bytes 3145736 | tf_op jit(solution)/shard_map/ppermute | solution.py:249
  591.0 45.9 %collective-permute-start.93 = (bf16[512,1024]{1,0:T(8,128)(2,1)}, bf16[512,1024]{1,0:T(8,128)(2,1)}, u32[]{:S(2)}, u32[]{:S(2)}) collective-permute-start(bf16[512,1024]{1,0:T(8,128)(2,1)} %get-tuple-element.348), channel_id=1, source_target_pairs={{0,4},{4,0},{1,5},{5,1},{2,6},{6,2},{3,7},{7,3},{8,12},{12,8},{9,1... | collective-permute-start | bytes 3145736 | tf_op jit(solution)/shard_map/ppermute | solution.py:252
  627.7 29.1 %all-to-all-start.7 = ((bf16[4,128,1024]{2,1,0:T(8,128)(2,1)}), bf16[4,128,1024]{2,1,0:T(8,128)(2,1)}, u32[]{:S(2)}, u32[]{:S(2)}) async-start(bf16[4,128,1024]{2,1,0:T(8,128)(2,1)} %slice.525), calls=%async_computation.7 | async-start | bytes 2097152 | tf_op jit(solution)/shard_map/all_to_all | solution.py:802
  640.9 33.6 %collective-permute-start.94 = (bf16[512,1024]{1,0:T(8,128)(2,1)}, bf16[512,1024]{1,0:T(8,128)(2,1)}, u32[]{:S(2)}, u32[]{:S(2)}) collective-permute-start(bf16[512,1024]{1,0:T(8,128)(2,1)} %get-tuple-element.352.refs_5_), channel_id=1, source_target_pairs={{0,8},{24,16},{8,0},{16,24},{1,9},{25,17},{9,1},{17,25},{2,10},{26... | collective-permute-start | bytes 3145736 | tf_op jit(solution)/shard_map/ppermute | solution.py:247
  643.4 31.1 %collective-permute-start.95 = (bf16[512,1024]{1,0:T(8,128)(2,1)}, bf16[512,1024]{1,0:T(8,128)(2,1)}, u32[]{:S(2)}, u32[]{:S(2)}) collective-permute-start(bf16[512,1024]{1,0:T(8,128)(2,1)} %get-tuple-element.353.refs_3_), channel_id=1, source_target_pairs={{8,16},{16,8},{9,17},{17,9},{10,18},{18,10},{11,19},{19,11},{12,20... | collective-permute-start | bytes 3145736 | tf_op jit(solution)/shard_map/ppermute | solution.py:249
  645.0 29.5 %collective-permute-start.96 = (bf16[512,1024]{1,0:T(8,128)(2,1)}, bf16[512,1024]{1,0:T(8,128)(2,1)}, u32[]{:S(2)}, u32[]{:S(2)}) collective-permute-start(bf16[512,1024]{1,0:T(8,128)(2,1)} %get-tuple-element.354), channel_id=1, source_target_pairs={{0,4},{4,0},{1,5},{5,1},{2,6},{6,2},{3,7},{7,3},{8,12},{12,8},{9,1... | collective-permute-start | bytes 3145736 | tf_op jit(solution)/shard_map/ppermute | solution.py:252
  656.8 38.0 %all-to-all-start.8 = ((bf16[4,64,1024]{2,1,0:T(8,128)(2,1)}), bf16[4,64,1024]{2,1,0:T(8,128)(2,1)}, u32[]{:S(2)}, u32[]{:S(2)}) async-start(bf16[4,64,1024]{2,1,0:T(8,128)(2,1)} %slice.524), calls=%async_computation.8 | async-start | bytes 1048576 | tf_op jit(solution)/shard_map/all_to_all | solution.py:802
  678.5 33.4 %collective-permute-start.97 = (bf16[512,1024]{1,0:T(8,128)(2,1)}, bf16[512,1024]{1,0:T(8,128)(2,1)}, u32[]{:S(2)}, u32[]{:S(2)}) collective-permute-start(bf16[512,1024]{1,0:T(8,128)(2,1)} %get-tuple-element.359.refs_5_), channel_id=1, source_target_pairs={{0,8},{24,16},{8,0},{16,24},{1,9},{25,17},{9,1},{17,25},{2,10},{26... | collective-permute-start | bytes 3145736 | tf_op jit(solution)/shard_map/ppermute | solution.py:247
  699.1 52.6 %collective-permute-start.62 = (bf16[512,2048]{1,0:T(8,128)(2,1)}, bf16[512,2048]{1,0:T(8,128)(2,1)}, u32[]{:S(2)}, u32[]{:S(2)}) collective-permute-start(bf16[512,2048]{1,0:T(8,128)(2,1)} %convolution_convert_fusion.4), channel_id=1, source_target_pairs={{0,1},{1,0},{2,3},{3,2},{4,5},{5,4},{6,7},{7,6},{8,9},{9,8},{10,11... | collective-permute-start | bytes 6291464 | tf_op jit(solution)/shard_map/ppermute | solution.py:49
  731.2 34.2 %all-to-all-start.9 = ((bf16[4,512,384]{2,1,0:T(8,128)(2,1)}), bf16[4,512,384]{2,1,0:T(8,128)(2,1)}, u32[]{:S(2)}, u32[]{:S(2)}) async-start(bf16[4,512,384]{2,1,0:T(8,128)(2,1)} %bitcast.283), calls=%async_computation.9 | async-start | bytes 3145728 | tf_op jit(solution)/shard_map/all_to_all | solution.py:868
  751.4 26.3 %collective-permute-start.105 = (bf16[512,1024]{1,0:T(8,128)(2,1)}, bf16[512,1024]{1,0:T(8,128)(2,1)S(1)}, u32[]{:S(2)}, u32[]{:S(2)}) collective-permute-start(bf16[512,1024]{1,0:T(8,128)(2,1)} %get-tuple-element.375), channel_id=1, source_target_pairs={{0,4},{4,0},{1,5},{5,1},{2,6},{6,2},{3,7},{7,3},{8,12},{12,8},{9,1... | collective-permute-start | bytes 3145736 | tf_op jit(solution)/shard_map/ppermute | solution.py:252
  756.3 31.1 %collective-permute-start.63 = (bf16[2,128,1024]{2,1,0:T(8,128)(2,1)}, bf16[2,128,1024]{2,1,0:T(8,128)(2,1)}, u32[]{:S(2)}, u32[]{:S(2)}) collective-permute-start(bf16[2,128,1024]{2,1,0:T(8,128)(2,1)} %slice.848), channel_id=1, source_target_pairs={{0,4},{1,5},{2,6},{3,7},{4,0},{5,1},{6,2},{7,3},{8,12},{9,13},{10,... | collective-permute-start | bytes 1572872 | tf_op jit(solution)/shard_map/ppermute | solution.py:49
  759.0 28.5 %collective-permute-start.64 = (bf16[2,128,1024]{2,1,0:T(8,128)(2,1)}, bf16[2,128,1024]{2,1,0:T(8,128)(2,1)}, u32[]{:S(2)}, u32[]{:S(2)}) collective-permute-start(bf16[2,128,1024]{2,1,0:T(8,128)(2,1)} %slice.536), channel_id=1, source_target_pairs={{0,2},{1,3},{2,0},{3,1},{4,6},{5,7},{6,4},{7,5},{8,10},{9,11},{10,... | collective-permute-start | bytes 1572872 | tf_op jit(solution)/shard_map/ppermute | solution.py:49
  790.4 25.7 %collective-permute-start.65 = (bf16[128,1024]{1,0:T(8,128)(2,1)}, bf16[128,1024]{1,0:T(8,128)(2,1)S(1)}, u32[]{:S(2)}, u32[]{:S(2)}) collective-permute-start(bf16[128,1024]{1,0:T(8,128)(2,1)} %fusion.54), channel_id=1, source_target_pairs={{0,2},{1,3},{2,0},{3,1},{4,6},{5,7},{6,4},{7,5},{8,10},{9,11},{10,... | collective-permute-start | bytes 786440 | tf_op jit(solution)/shard_map/ppermute | solution.py:49
  835.6 27.7 %collective-permute-start.112 = (bf16[512,1024]{1,0:T(8,128)(2,1)S(1)}, bf16[512,1024]{1,0:T(8,128)(2,1)S(1)}, u32[]{:S(2)}, u32[]{:S(2)}) collective-permute-start(bf16[512,1024]{1,0:T(8,128)(2,1)S(1)} %get-tuple-element.393.refs_3_), channel_id=1, source_target_pairs={{8,0},{16,24},{9,1},{17,25},{10,2},{18,26},{11,3},{19,27},{12,4},{... | collective-permute-start | bytes 3145736 | tf_op jit(solution)/shard_map/ppermute | solution.py:247
  836.9 26.4 %collective-permute-start.113 = (bf16[512,1024]{1,0:T(8,128)(2,1)S(1)}, bf16[512,1024]{1,0:T(8,128)(2,1)S(1)}, u32[]{:S(2)}, u32[]{:S(2)}) collective-permute-start(bf16[512,1024]{1,0:T(8,128)(2,1)S(1)} %get-tuple-element.394.refs_1_), channel_id=1, source_target_pairs={{8,16},{16,8},{9,17},{17,9},{10,18},{18,10},{11,19},{19,11},{12,20... | collective-permute-start | bytes 3145736 | tf_op jit(solution)/shard_map/ppermute | solution.py:249
  837.6 25.7 %collective-permute-start.114 = (bf16[512,1024]{1,0:T(8,128)(2,1)S(1)}, bf16[512,1024]{1,0:T(8,128)(2,1)S(1)}, u32[]{:S(2)}, u32[]{:S(2)}) collective-permute-start(bf16[512,1024]{1,0:T(8,128)(2,1)S(1)} %get-tuple-element.395.refs_0_), channel_id=1, source_target_pairs={{0,4},{4,0},{1,5},{5,1},{2,6},{6,2},{3,7},{7,3},{8,12},{12,8},{9,1... | collective-permute-start | bytes 3145736 | tf_op jit(solution)/shard_map/ppermute | solution.py:252
  (187 other events, 2495.1 us)

commit v4 on v3

--- a/solution.py
+++ b/solution.py
@@ -134,6 +134,7 @@
         held = lax.optimization_barrier(tuple(v for values in moving.values() for v in values))
         last = held[:1] or last
         box["now"] = last
+        box["stage", stage] = last
         done = 0
         for name, values in moving.items():
             task, unused, turn = running[name]
@@ -167,14 +168,15 @@
             refs["own"][...] = read("got")
 
 
-def mix(outer, sources, arrays, results, steps, block):
+def mix(outer, sources, arrays, results, block):
     at_end = {"now": 0, "next": 1, "got": None, "kept": 0, "across": 0, "before": 0}
     names, operands, specs = [], [], []
     for name in at_end:
         if name in sources:
-            array, shape, index = sources[name]
+            array, shape, index, blocks = sources[name]
         elif name in arrays:
-            array, shape, index = arrays[name], block, lambda i: (i, 0)
+            array, blocks = arrays[name]
+            shape, index = block, lambda i: (i, 0)
         else:
             continue
         if name == "got" and "sum" not in results:
@@ -184,7 +186,8 @@
         else:
             used = at_end[name]
 
-        def where(i, flag, index=index, used=used):
+        def where(i, flag, index=index, used=used, blocks=blocks):
+            i = jnp.minimum(i, blocks - 1)
             return index(i if used is None else jnp.where(flag[0] == used, i, 0))
 
         names.append(name)
@@ -194,31 +197,46 @@
         functools.partial(mix_kernel, tuple(names) + tuple(results), block),
         grid_spec=pltpu.PrefetchScalarGridSpec(
             num_scalar_prefetch=1,
-            grid=(steps,),
+            grid=(max(results.values()),),
             in_specs=specs,
-            out_specs=[pl.BlockSpec(block, lambda i, flag: (i, 0)) for name in results],
+            out_specs=[
+                pl.BlockSpec(block, lambda i, flag, blocks=blocks: (jnp.minimum(i, blocks - 1), 0))
+                for blocks in results.values()
+            ],
         ),
         out_shape=[
-            jax.ShapeDtypeStruct((steps * block[0], block[1]), bf16) for name in results
+            jax.ShapeDtypeStruct((blocks * block[0], block[1]), bf16)
+            for blocks in results.values()
         ],
         compiler_params=pltpu.CompilerParams(vmem_limit_bytes=32 * 1024 * 1024),
         cost_estimate=pl.CostEstimate(
-            flops=0, transcendentals=0, bytes_accessed=10 * steps * block[0] * block[1]
+            flops=0,
+            transcendentals=0,
+            bytes_accessed=10 * max(results.values()) * block[0] * block[1],
         ),
         name="mix",
     )(outer, *operands)
     return dict(zip(results, got))
 
 
-def finish(task, sent):
-    try:
-        while True:
-            sent = task.send(lax.optimization_barrier(tuple(sent)))
-    except StopIteration:
-        pass
-
-
-def stream(chunks, placed, box, steps, block):
+def finish(tasks):
+    results, running = [None] * len(tasks), dict(enumerate(tasks))
+    while running:
+        held = lax.optimization_barrier(
+            tuple(value for task, sent in running.values() for value in sent)
+        )
+        done = 0
+        for number, (task, sent) in list(running.items()):
+            try:
+                running[number] = (task, task.send(held[done : done + len(sent)]))
+            except StopIteration as stop:
+                del running[number]
+                results[number] = stop.value
+            done += len(sent)
+    return results
+
+
+def stream(chunks, placed, box, block):
     count, halves = lax.axis_size("line"), lax.axis_size("xpart")
     place, side = lax.axis_index("line"), lax.axis_index("xpart")
     sides = [lax.rem(side + halves - turn, halves) for turn in range(halves)]
@@ -227,14 +245,20 @@
     outer = outer.astype(jnp.int32).reshape(1)
     inward, outward, across = [(0, 1), (3, 2)], [(1, 0), (2, 3)], [(1, 2), (2, 1)]
     last = len(chunks)
+    sizes = [blocks for source, put, blocks in chunks]
 
     def is_chunk(number):
         return 0 <= number < last
 
+    def chunk(number):
+        return chunks[number][0]() + (sizes[number],)
+
     def first(number):
-        return mix(outer * 0 + 1, {"next": chunks[number][0]()}, {}, ["outer"], steps, block)
-
-    sending = first(0)["outer"]
+        return mix(
+            outer * 0 + 1, {"next": chunk(number)}, {}, {"outer": sizes[number]}, block
+        )
+
+    sending, width = first(0)["outer"], sizes[0]
     sums, owns, fresh = {}, {}, []
     for stage in range(last + 3):
         moves = {}
@@ -256,24 +280,25 @@
         moves = dict(zip(moves, held))
         placed.update(zip(fresh, held[len(moves) :]))
         if split:
-            sources, arrays, results = {}, {}, []
+            sources, arrays, results = {}, {}, {}
             if is_chunk(stage):
-                sources["now"] = chunks[stage][0]()
-                results.append("sum")
+                sources["now"] = chunk(stage)
+                results["sum"] = sizes[stage]
             if is_chunk(stage + 1):
-                sources["next"] = chunks[stage + 1][0]()
+                sources["next"] = chunk(stage + 1)
             if is_chunk(stage - 1):
-                arrays.update(kept=sums.pop(stage - 1), across=moves["across"])
+                arrays["kept"] = (sums.pop(stage - 1), sizes[stage - 1])
+                arrays["across"] = (moves["across"], sizes[stage - 1])
             if is_chunk(stage + 1) or is_chunk(stage - 1):
-                results.append("outer")
+                results["outer"] = max(sizes[n] for n in (stage - 1, stage + 1) if is_chunk(n))
             if is_chunk(stage - 2):
-                arrays["before"] = sending
-                results.append("own")
+                arrays["before"] = (sending, sizes[stage - 2])
+                results["own"] = sizes[stage - 2]
             if is_chunk(stage) or is_chunk(stage - 2):
-                arrays["got"] = moves["got"]
+                arrays["got"] = (moves["got"], width)
             if results:
-                made = mix(outer, sources, arrays, results, steps, block)
-                sending = made.get("outer")
+                made = mix(outer, sources, arrays, results, block)
+                sending, width = made.get("outer"), results.get("outer")
                 if is_chunk(stage):
                     sums[stage] = made["sum"]
                 if is_chunk(stage - 2):
@@ -374,31 +399,85 @@
     )(*operands)
 
 
-def place_narrow(total, pieces, spot, sides, count):
-    shards, rows, columns = pieces[0].shape
+def attn_kernel(deep, heads, sides_ref, *refs):
+    *others, query_ref, key_ref, value_ref = refs
+    halves = sides_ref.shape[0]
+    pieces = others[:halves]
+    across = pieces[0].shape[1] // 128
+    kinds = heads // 128
+    count = query_ref.shape[1] // heads
+    first = lax.broadcasted_iota(jnp.int32, (1, 128), 1) < HD
+
+    def square(order, number, kind, high):
+        spot = ((number // halves) * (kinds + 1) + kind) * deep + high
+        down, right = spot // across * 128, spot % across * 128
+        piece = pieces[order[number % halves]]
+        return piece[down : down + 128, right : right + 128].astype(f32)
+
+    for turn in range(halves):
+
+        @pl.when(sides_ref[0] == turn)
+        def put(turn=turn):
+            order = [(side + turn) % halves for side in range(halves)]
+            for high in range(deep):
+                rows = slice(high * 128, (high + 1) * 128)
+                for number in range(count):
+                    for kind in range(kinds):
+                        left = number * heads + kind * 128
+                        query_ref[rows, left : left + 128] = square(order, number, kind, high)
+                for pair in range(count // 2):
+                    even = square(order, 2 * pair, kinds, high)
+                    odd = square(order, 2 * pair + 1, kinds, high)
+                    here = slice(pair * 128, (pair + 1) * 128)
+                    key_ref[rows, here] = jnp.where(first, even, pltpu.roll(odd, HD, 1))
+                    value_ref[rows, here] = jnp.where(first, pltpu.roll(even, HD, 1), odd)
+
+
+def place_attn(totals, pieces, spot, sides, size, heads, shards, count):
     halves = len(pieces)
-    ordered = [pieces[0]]
-    if halves == 2:
-        ordered = [jnp.where(sides[0] == t, pieces[0], pieces[1]) for t in range(2)]
-    block = jnp.concatenate(
-        [ordered[t][w] for w in range(shards) for t in range(halves)], axis=1
-    ).astype(f32)
-    if total is None:
-        total = jnp.zeros((count * rows, block.shape[1]), f32)
-    return lax.dynamic_update_slice(total, block, (spot * rows, 0))
-
-
-def sum_everywhere(vector):
-    for flip in (1, 2, 4):
-        (got,) = yield [swap(vector, flip)]
-        vector = vector + got
+    columns = [shards * halves * width for width in (heads, HD, HD)]
+    operands = [jnp.stack(sides).astype(jnp.int32)] + list(pieces)
+    specs = [pl.BlockSpec(memory_space=pltpu.VMEM)] * halves
+    aliases = {}
+    if totals is not None:
+        aliases = {len(operands) + i: i for i in range(3)}
+        operands += totals
+        specs += [pl.BlockSpec(memory_space=pl.ANY)] * 3
+
+    def kernel(sides_ref, *refs):
+        attn_kernel(size // 128, heads, sides_ref, *refs[:halves], *refs[-3:])
+
+    return pl.pallas_call(
+        kernel,
+        grid_spec=pltpu.PrefetchScalarGridSpec(
+            num_scalar_prefetch=1,
+            grid=(1,),
+            in_specs=specs,
+            out_specs=[
+                pl.BlockSpec((size, width), lambda i, sides_ref: (spot, 0)) for width in columns
+            ],
+        ),
+        out_shape=[jax.ShapeDtypeStruct((count * size, width), f32) for width in columns],
+        input_output_aliases=aliases,
+        compiler_params=pltpu.CompilerParams(vmem_limit_bytes=32 * 1024 * 1024),
+        cost_estimate=pl.CostEstimate(
+            flops=0, transcendentals=0, bytes_accessed=6 * size * sum(columns)
+        ),
+        name="place_attn",
+    )(*operands)
+
+
+def sum_everywhere(vector, stages):
+    for unused in range(stages):
+        yield []
+    got = yield [swap(vector, flip) for flip in range(1, KVH)]
+    vector = sum(got, vector)
     count = lax.axis_size("line")
-    flip = 1
-    while flip < count:
-        (got,) = yield [lax.ppermute(vector, "line", [(i, i ^ flip) for i in range(count)])]
-        vector = vector + got
-        flip *= 2
-    return vector
+    got = yield [
+        lax.ppermute(vector, "line", [(i, (i + turn) % count) for i in range(count)])
+        for turn in range(1, count)
+    ]
+    return sum(got, vector)
 
 
 def move_spans(load, store, order_ref, tiles, span):
@@ -899,20 +978,20 @@
         )
         input_part, attn_gain_term = norm_back(inputs.astype(f32), gain_one, normed_one_grad)
         input_grad = residual_grad + input_part
-        gain_terms = yield from sum_everywhere(jnp.stack([attn_gain_term, box["ffn_gain"]]))
-        return (input_grad, gain_terms)
+        return (input_grad, jnp.stack([attn_gain_term, box["ffn_gain"]]))
 
     half_rows = rows // 2
 
     def feed_forward_back(last):
-        (box["gate0"],) = yield [to_shards(gate_partial[:, :half_rows])]
+        gate0 = to_shards(gate_partial[:, :half_rows])
+        yield []
         up_partial = contract(normed_two, after(up_low, *box["now"]), 0, 0).astype(bf16)
         (up_partial,) = yield [up_partial.reshape(shards, rows, units)]
+        box["gate0"], gate_now = yield [gate0, gate_partial]
+        gate1 = to_shards(gate_now[:, half_rows:])
         yield []
         yield []
-        gate = after(gate_partial, *box["now"])
-        (box["gate1"],) = yield [to_shards(gate[:, half_rows:])]
-        yield []
+        (box["gate1"],) = yield [gate1]
         up_now = after(up_partial, *box["now"])
         (box["up0"],) = yield [to_shards(up_now[:, :half_rows])]
         up_now = after(up_partial, *box["now"])
@@ -920,7 +999,7 @@
         return None
 
     def feed_forward_out(last):
-        low = after(hidden, *last)
+        low = after(hidden, *box["stage", 1])
         return (
             yield from slab_reduce(
                 lambda start, stop: contract(low[start:stop], own_down, 1, 0), tok_dev
@@ -947,7 +1026,7 @@
                 lambda on, i: (on * 4 + high * 2 + i, right),
             )
 
-        return (source, put)
+        return (source, put, steps)
 
     def column_chunk(name, c):
         size = rows // 4
@@ -964,7 +1043,7 @@
             pieces = [piece.reshape(shards, size, units) for piece in pieces]
             placed[name] = place_columns(placed.get(name), pieces, c, sides, 4)
 
-        return (source, put)
+        return (source, put, steps)
 
     def output_chunk():
         def source():
@@ -980,54 +1059,52 @@
                 lambda on, i: (on, i),
             )
 
-        return (source, put)
+        return (source, put, steps)
 
     def attn_chunk(c):
         size, columns = rows // 2, heads + 2 * HD
-        beside = 2
-        over = shards // beside
+        deep, wide, across = size // 128, columns // 128, half_width // 128
+        blocks = shards * deep * wide // across
 
         def source():
-            part = box["attn"][:, c * size : (c + 1) * size].reshape(over, beside, size, columns)
-            part = part.swapaxes(1, 2).reshape(over * size, beside * columns)
-            part = jnp.pad(part, ((0, 0), (0, half_width - beside * columns)))
-            return part, block, lambda i: (i, 0)
+            part = box["attn"][:, c * size : (c + 1) * size]
+            squares = [
+                part[w, h * 128 : (h + 1) * 128, b * 128 : (b + 1) * 128]
+                for w in range(shards)
+                for b in range(wide)
+                for h in range(deep)
+            ]
+            lines = [
+                jnp.concatenate(squares[g * across : (g + 1) * across], axis=1)
+                for g in range(blocks)
+            ]
+            return jnp.concatenate(lines, axis=0), block, lambda i: (i, 0)
 
         def put(placed, pieces, sides):
-            cut = [
-                piece[:, : beside * columns]
-                .reshape(over, size, beside, columns)
-                .swapaxes(1, 2)
-                .reshape(shards, size, columns)
-                for piece in pieces
-            ]
-            for key, place_part, start, stop in (
-                ("query", place_columns, 0, heads),
-                ("key", place_narrow, heads, heads + HD),
-                ("value", place_narrow, heads + HD, columns),
-            ):
-                placed[key] = place_part(
-                    placed.get(key), [piece[..., start:stop] for piece in cut], c, sides, 2
-                )
-
-        return (source, put)
+            names = ("query", "key", "value")
+            totals = [placed[name] for name in names] if "query" in placed else None
+            totals = place_attn(totals, pieces, c, sides, size, heads, shards, 2)
+            placed.update(zip(names, totals))
+
+        return (source, put, blocks)
 
     chunks = [down_chunk(c) for c in range(4)]
     chunks += [column_chunk(name, c) for name in ("gate", "up") for c in range(4)]
     chunks += [output_chunk()] + [attn_chunk(c) for c in range(2)]
     placed = {}
-    gradients = stream(chunks, placed, box, steps, block)
+    gradients = stream(chunks, placed, box, block)
     sent = gradients.send(lax.optimization_barrier(tuple(next(gradients))))
     run_tasks(
         [
             ("attention", lambda t, b: True, attention_back),
             ("parts", lambda t, b: True, feed_forward_back),
-            ("out", lambda t, b: t >= 1, feed_forward_out),
         ],
         box,
     )
-    finish(gradients, sent)
+    run_tasks([("out", lambda t, b: True, feed_forward_out)], box)
     input_grad, gain_terms = box["attention"]
+    gain_sums = sum_everywhere(gain_terms, len(chunks) - 1)
+    gain_terms = finish([(gradients, sent), (gain_sums, next(gain_sums))])[1]
     gain_terms = lax.dynamic_slice_in_dim(gain_terms, shard * rows, rows, 1)
     return (
         (residual + box["out"]).astype(bf16),

time: 928 us -> 923 us (level)
  waiting for transfers between devices: 289 us -> 315 us
  local copies, waits for them, and re-layouts: 136 us -> 116 us
    ppermute x17, waiting for transfers between devices: 72.7 us -> 98.5 us  [stream(): moves['got'] = lax.ppermute(sending, 'line', pairs)]
    ppermute x15, waiting for transfers between devices: 56 us -> 34 us  [stream(): lax.ppermute(owns[stage - 3], 'xpart', [(i, (i + turn) % halves) for i in...]
    ppermute x57 -> x61, waiting for transfers between devices: 91.9 us -> 108 us  [swap(): return lax.ppermute(value, SLAB, [(i, i ^ flip) for i in range(KVH)])]
    reshape x8 -> x0, local copies, waits for them, and re-layouts: 10.7 us -> none  [put(): cut = [piece[:, :beside * columns].reshape(over, size, beside, columns).s...]
    pallas_call x10 -> x8, Pallas kernels: 41.4 us -> 33.1 us  [place_columns(): pl.pallas_call(place_kernel, grid_spec=pltpu.PrefetchScalarGridSpec(num_s...]
    unnamed x216 -> x183, local copies, waits for them, and re-layouts: 27 us -> 22.4 us
    ppermute x57 -> x61, starting transfers between devices: 42.7 us -> 44.6 us  [swap(): return lax.ppermute(value, SLAB, [(i, i ^ flip) for i in range(KVH)])]
  transfers between devices with their start and end apart: 128 -> 133, of which waited for: 46 -> 48; matrix products, arithmetic and copies ran while one was open for 21% -> 20% of each run, Pallas kernels for 18% -> 17%
where the time goes in v4:
time: 923 us; the launch traced here: 910 us
  waiting for transfers between devices  315 us (34%)
  starting transfers between devices  190 us (21%)
  Pallas kernels  162 us (18%)
  local copies, waits for them, and re-layouts  116 us (13%)
  matrix products  79.9 us (9%)
  other arithmetic  42.8 us (5%)
    ppermute x61, waiting for transfers between devices, swap(): return lax.ppermute(value, SLAB, [(i, i ^ flip) for i in range(KVH)])  108 us
    ppermute x17, waiting for transfers between devices, stream(): moves['got'] = lax.ppermute(sending, 'line', pairs)  98.5 us
    dot_general x17, matrix products, contract(): lax.dot_general(left, right, (((left_dim,), (right_dim,)), ((), ())), pre...  79.9 us
    ppermute x17, starting transfers between devices, stream(): moves['got'] = lax.ppermute(sending, 'line', pairs)  51.6 us
    ppermute x12, waiting for transfers between devices, pass_on(): return lax.ppermute(block, 'wshard', [(i, i ^ flip) for i in range(shards)])  50.5 us
    dynamic_update_slice x38, local copies, waits for them, and re-layouts, put(): lax.dynamic_update_slice(total, piece, (index * half,) + (0,) * (block.nd...  44.7 us
    ppermute x61, starting transfers between devices, swap(): return lax.ppermute(value, SLAB, [(i, i ^ flip) for i in range(KVH)])  44.6 us
    pallas_call x18, Pallas kernels, mix(): pl.pallas_call(functools.partial(mix_kernel, tuple(names) + tuple(results...  44 us
  transfers between devices with their start and end apart: 133, of which 48 were waited for; matrix products, arithmetic and copies ran while one was open for 20% of the time, Pallas kernels for 17%

profile of v4, /device:TPU:0, one launch (start us, length us, event | category | flops | bytes accessed | tf_op | source)
XLA Modules:
  0.0 909.8 jit_solution(13376411984866287430)
XLA Ops:
  42.0 7.1 collective-permute-done.8
  54.4 9.3 %collective-permute-done.14 = bf16[512,384]{1,0:T(8,128)(2,1)S(1)} collective-permute-done((bf16[512,384]{1,0:T(8,128)(2,1)S(1)}, bf16[512,384]{1,0:T(8,128)(2,1)S(1)}, u32[]{:S(2)}, u32[]{:S(2)}) %collective-permute-start.14) | collective-permute-done | bytes 393248 | tf_op jit(solution)/shard_map/ppermute | solution.py:783
  74.0 5.0 all-to-all-start
  79.5 13.2 %collective-permute-done.15 = bf16[128,2048]{1,0:T(8,128)(2,1)S(1)} collective-permute-done((bf16[128,2048]{1,0:T(8,128)(2,1)S(1)}, bf16[128,2048]{1,0:T(8,128)(2,1)S(1)}, u32[]{:S(2)}, u32[]{:S(2)}) %collective-permute-start.15) | collective-permute-done | bytes 524320 | tf_op jit(solution)/shard_map/ppermute | solution.py:49
  101.5 8.9 collective-permute-done.18
  110.4 11.2 %collective-permute-done.17 = bf16[512,1024]{1,0:T(8,128)(2,1)} collective-permute-done((bf16[512,1024]{1,0:T(8,128)(2,1)}, bf16[512,1024]{1,0:T(8,128)(2,1)}, u32[]{:S(2)}, u32[]{:S(2)}) %collective-permute-start.17) | collective-permute-done | bytes 1048608 | tf_op jit(solution)/shard_map/ppermute | solution.py:783
  125.9 22.3 %attend_forward.1 = (bf16[4,64,1024]{2,1,0:T(8,128)(2,1)}, bf16[192,4096]{1,0:T(8,128)(2,1)}, f32[64,4096]{1,0:T(8,128)}, f32[1,4096]{1,0:T(1,128)}) custom-call(s32[64]{0:T(128)} %select_reduce_fusion.sort_ref, s32[64]{0:T(128)} %copy-done.82, s32[2]{0:T(128)} %pad_add_fusion.range_ref, bf16[4,192,1024]{2,1,0:T(8,128)(2,1)} %all-to-all-done.blocks_ref), custom_call_target="tpu_custom_call" | custom-call | flops 30000001024 | bytes 8000000 | tf_op jit(solution)/shard_map/attend_forward/pallas_call | solution.py:673
  156.9 4.8 all-to-all-start.1
  169.2 7.1 all-to-all-done.1
  195.9 18.4 %collective-permute-done.30 = bf16[512,1024]{1,0:T(8,128)(2,1)S(1)} collective-permute-done((bf16[512,1024]{1,0:T(8,128)(2,1)S(1)}, bf16[512,1024]{1,0:T(8,128)(2,1)S(1)}, u32[]{:S(2)}, u32[]{:S(2)}) %collective-permute-start.30) | collective-permute-done | bytes 1048608 | tf_op jit(solution)/shard_map/ppermute | solution.py:783
  214.3 11.7 %collective-permute-done.29 = bf16[2,128,1024]{2,1,0:T(8,128)(2,1)S(1)} collective-permute-done((bf16[2,128,1024]{2,1,0:T(8,128)(2,1)S(1)}, bf16[2,128,1024]{2,1,0:T(8,128)(2,1)S(1)}, u32[]{:S(2)}, u32[]{:S(2)}) %collective-permute-start.29) | collective-permute-done | bytes 524320 | tf_op jit(solution)/shard_map/ppermute | solution.py:49
  228.2 7.0 fusion.7
  242.0 8.6 collective-permute-done.33
  260.2 8.8 fusion.89
  273.0 7.4 convolution_convert_fusion.1.refs_0_.refs_1_
  286.9 6.2 convolution_convert_fusion.2
  293.1 14.0 %collective-permute-done.42.refs_2_ = bf16[512,1024]{1,0:T(8,128)(2,1)S(1)} collective-permute-done((bf16[512,1024]{1,0:T(8,128)(2,1)S(1)}, bf16[512,1024]{1,0:T(8,128)(2,1)S(1)}, u32[]{:S(2)}, u32[]{:S(2)}) %collective-permute-start.42) | collective-permute-done | bytes 1048608 | tf_op jit(solution)/shard_map/ppermute | solution.py:271
  309.7 5.7 convolution_convert_fusion.5
  317.1 7.3 collective-permute-start.67
  324.4 6.1 convert_add_fusion.2
  334.2 6.2 convolution_convert_fusion
  375.5 8.7 collective-permute-done.69.refs_2_
  404.9 8.5 collective-permute-done.71.refs_2_
  413.3 4.9 collective-permute-done.73.refs_1_
  430.4 13.2 %collective-permute-done.74.refs_2_ = bf16[512,1024]{1,0:T(8,128)(2,1)S(1)} collective-permute-done((bf16[512,1024]{1,0:T(8,128)(2,1)S(1)}, bf16[512,1024]{1,0:T(8,128)(2,1)S(1)}, u32[]{:S(2)}, u32[]{:S(2)}) %collective-permute-start.74) | collective-permute-done | bytes 1048608 | tf_op jit(solution)/shard_map/ppermute | solution.py:271
  452.2 5.1 place_blocks.5.refs_2_
  500.6 4.9 place_blocks.6.refs_2_
  523.6 5.1 place_blocks.7.refs_2_
  528.7 9.8 %collective-permute-done.80.refs_2_ = bf16[512,1024]{1,0:T(8,128)(2,1)} collective-permute-done((bf16[512,1024]{1,0:T(8,128)(2,1)}, bf16[512,1024]{1,0:T(8,128)(2,1)}, u32[]{:S(2)}, u32[]{:S(2)}) %collective-permute-start.80) | collective-permute-done | bytes 1048608 | tf_op jit(solution)/shard_map/ppermute | solution.py:271
  553.1 4.9 place_blocks.8
  580.7 33.0 %attend_backward.1 = bf16[4,192,1024]{2,1,0:T(8,128)(2,1)} custom-call(s32[64]{0:T(128)} %select_reduce_fusion.sort_ref, s32[64]{0:T(128)} %copy-done.82, s32[2]{0:T(128)} %pad_add_fusion.range_ref, bf16[192,4096]{1,0:T(8,128)(2,1)} %get-tuple-element.290.sorted_ref, f32[64,4096]{1,0:T(8,128)} %get-tuple-element.291.float_ref, ...), custom_call_target="tpu_custom_call" | custom-call | flops 35999997952 | bytes 8000000 | tf_op jit(solution)/shard_map/attend_backward/pallas_call | solution.py:699
  620.2 4.8 place_columns.8.refs_2_
  636.9 7.7 all-to-all-done.7
  648.8 4.8 place_columns.9.refs_2_
  653.7 7.3 collective-permute-done.89.refs_2_
  665.0 12.8 %collective-permute-start.92 = (bf16[512,1024]{1,0:T(8,128)(2,1)}, bf16[512,1024]{1,0:T(8,128)(2,1)}, u32[]{:S(2)}, u32[]{:S(2)}) collective-permute-start(bf16[512,1024]{1,0:T(8,128)(2,1)} %get-tuple-element.371.refs_5_), channel_id=1, source_target_pairs={{0,8},{24,16},{8,0},{16,24},{1,9},{25,17},{9,1},{17,25},{2,10},{26... | collective-permute-start | bytes 3145736 | tf_op jit(solution)/shard_map/ppermute | solution.py:271
  695.6 4.8 place_columns.10.refs_2_
  706.3 4.9 place_columns.11
  717.3 11.4 %collective-permute-done.95.refs_2_ = bf16[512,1024]{1,0:T(8,128)(2,1)S(1)} collective-permute-done((bf16[512,1024]{1,0:T(8,128)(2,1)S(1)}, bf16[512,1024]{1,0:T(8,128)(2,1)S(1)}, u32[]{:S(2)}, u32[]{:S(2)}) %collective-permute-start.95) | collective-permute-done | bytes 1048608 | tf_op jit(solution)/shard_map/ppermute | solution.py:271
  747.8 10.6 %collective-permute-done.98.refs_2_ = bf16[512,1024]{1,0:T(8,128)(2,1)S(1)} collective-permute-done((bf16[512,1024]{1,0:T(8,128)(2,1)}, bf16[512,1024]{1,0:T(8,128)(2,1)S(1)}, u32[]{:S(2)}, u32[]{:S(2)}) %collective-permute-start.98) | collective-permute-done | bytes 1048608 | tf_op jit(solution)/shard_map/ppermute | solution.py:271
  774.5 4.6 place_columns.13.refs_2_
  779.3 23.1 %collective-permute-done.63 = bf16[2,128,1024]{2,1,0:T(8,128)(2,1)S(1)} collective-permute-done((bf16[2,128,1024]{2,1,0:T(8,128)(2,1)S(1)}, bf16[2,128,1024]{2,1,0:T(8,128)(2,1)S(1)}, u32[]{:S(2)}, u32[]{:S(2)}) %collective-permute-start.63) | collective-permute-done | bytes 524320 | tf_op jit(solution)/shard_map/ppermute | solution.py:49
  812.8 12.9 %collective-permute-done.104.refs_1_ = bf16[512,1024]{1,0:T(8,128)(2,1)S(1)} collective-permute-done((bf16[512,1024]{1,0:T(8,128)(2,1)S(1)}, bf16[512,1024]{1,0:T(8,128)(2,1)S(1)}, u32[]{:S(2)}, u32[]{:S(2)}) %collective-permute-start.104) | collective-permute-done | bytes 1048608 | tf_op jit(solution)/shard_map/ppermute | solution.py:271
  825.7 5.8 collective-permute-done.106
  832.0 5.1 collective-permute-done.66
  844.5 11.5 %collective-permute-done.113 = f32[2,2048]{1,0:T(2,128)S(1)} collective-permute-done((f32[2,2048]{1,0:T(2,128)S(1)}, f32[2,2048]{1,0:T(2,128)S(1)}, u32[]{:S(2)}, u32[]{:S(2)}) %collective-permute-start.113) | collective-permute-done | bytes 16416 | tf_op jit(solution)/shard_map/ppermute | solution.py:49
  875.0 10.0 %collective-permute-done.121 = f32[2,2048]{1,0:T(2,128)S(1)} collective-permute-done((f32[2,2048]{1,0:T(2,128)S(1)}, f32[2,2048]{1,0:T(2,128)S(1)}, u32[]{:S(2)}, u32[]{:S(2)}) %collective-permute-start.121) | collective-permute-done | bytes 16416 | tf_op jit(solution)/shard_map/ppermute | solution.py:477
  894.3 12.5 %collective-permute-done.122.refs_1_ = bf16[384,1024]{1,0:T(8,128)(2,1)S(1)} collective-permute-done((bf16[384,1024]{1,0:T(8,128)(2,1)S(1)}, bf16[384,1024]{1,0:T(8,128)(2,1)S(1)}, u32[]{:S(2)}, u32[]{:S(2)}) %collective-permute-start.122) | collective-permute-done | bytes 786464 | tf_op jit(solution)/shard_map/ppermute | solution.py:276
  (638 shorter events, 457.8 us)
Async XLA Ops:
  20.4 28.7 %collective-permute-start.6 = (bf16[128,2048]{1,0:T(8,128)(2,1)}, bf16[128,2048]{1,0:T(8,128)(2,1)S(1)}, u32[]{:S(2)}, u32[]{:S(2)}) collective-permute-start(bf16[128,2048]{1,0:T(8,128)(2,1)} %collective-permute-done), channel_id=1, source_target_pairs={{0,1},{1,0},{2,3},{3,2},{4,5},{5,4},{6,7},{7,6},{8,9},{9,8},{10,11... | collective-permute-start | bytes 1572872 | tf_op jit(solution)/shard_map/ppermute | solution.py:49
  22.4 26.7 %collective-permute-start.7 = (bf16[128,2048]{1,0:T(8,128)(2,1)}, bf16[128,2048]{1,0:T(8,128)(2,1)S(1)}, u32[]{:S(2)}, u32[]{:S(2)}) collective-permute-start(bf16[128,2048]{1,0:T(8,128)(2,1)} %collective-permute-done.1), channel_id=1, source_target_pairs={{0,1},{1,0},{2,3},{3,2},{4,5},{5,4},{6,7},{7,6},{8,9},{9,8},{10,11... | collective-permute-start | bytes 1572872 | tf_op jit(solution)/shard_map/ppermute | solution.py:49
  74.0 47.6 %all-to-all-start = ((bf16[4,192,1024]{2,1,0:T(8,128)(2,1)}), bf16[4,192,1024]{2,1,0:T(8,128)(2,1)}, u32[]{:S(2)}, u32[]{:S(2)}) async-start(bf16[4,192,1024]{2,1,0:T(8,128)(2,1)} %pad_maximum_fusion.1), calls=%async_computation | async-start | bytes 3145728 | tf_op jit(solution)/shard_map/all_to_all | solution.py:857
  95.7 25.9 %collective-permute-start.17 = (bf16[512,1024]{1,0:T(8,128)(2,1)}, bf16[512,1024]{1,0:T(8,128)(2,1)}, u32[]{:S(2)}, u32[]{:S(2)}) collective-permute-start(bf16[512,1024]{1,0:T(8,128)(2,1)} %get-tuple-element.454), channel_id=1, source_target_pairs={{0,2},{1,3},{2,0},{3,1},{4,6},{5,7},{6,4},{7,5},{8,10},{9,11},{10,... | collective-permute-start | bytes 3145736 | tf_op jit(solution)/shard_map/ppermute | solution.py:783
  121.6 27.4 %collective-permute-start.22 = (bf16[128,2048]{1,0:T(8,128)(2,1)S(1)}, bf16[128,2048]{1,0:T(8,128)(2,1)S(1)}, u32[]{:S(2)}, u32[]{:S(2)}) collective-permute-start(bf16[128,2048]{1,0:T(8,128)(2,1)S(1)} %collective-permute-done.15), channel_id=1, source_target_pairs={{0,4},{1,5},{2,6},{3,7},{4,0},{5,1},{6,2},{7,3},{8,12},{9,13},{10,... | collective-permute-start | bytes 1572872 | tf_op jit(solution)/shard_map/ppermute | solution.py:49
  123.1 25.9 %collective-permute-start.23 = (bf16[128,2048]{1,0:T(8,128)(2,1)S(1)}, bf16[128,2048]{1,0:T(8,128)(2,1)S(1)}, u32[]{:S(2)}, u32[]{:S(2)}) collective-permute-start(bf16[128,2048]{1,0:T(8,128)(2,1)S(1)} %collective-permute-done.15), channel_id=1, source_target_pairs={{0,1},{1,0},{2,3},{3,2},{4,5},{5,4},{6,7},{7,6},{8,9},{9,8},{10,11... | collective-permute-start | bytes 1572872 | tf_op jit(solution)/shard_map/ppermute | solution.py:49
  153.8 25.5 %collective-permute-start.25 = (bf16[512,1024]{1,0:T(8,128)(2,1)}, bf16[512,1024]{1,0:T(8,128)(2,1)}, u32[]{:S(2)}, u32[]{:S(2)}) collective-permute-start(bf16[512,1024]{1,0:T(8,128)(2,1)} %constant_dynamic-slice_fusion.5), channel_id=1, source_target_pairs={{0,3},{1,2},{2,1},{3,0},{4,7},{5,6},{6,5},{7,4},{8,11},{9,10},{10,... | collective-permute-start | bytes 3145736 | tf_op jit(solution)/shard_map/ppermute | solution.py:783
  193.3 32.8 %collective-permute-start.29 = (bf16[2,128,1024]{2,1,0:T(8,128)(2,1)S(1)}, bf16[2,128,1024]{2,1,0:T(8,128)(2,1)S(1)}, u32[]{:S(2)}, u32[]{:S(2)}) collective-permute-start(bf16[2,128,1024]{2,1,0:T(8,128)(2,1)S(1)} %slice.577), channel_id=1, source_target_pairs={{0,2},{1,3},{2,0},{3,1},{4,6},{5,7},{6,4},{7,5},{8,10},{9,11},{10,... | collective-permute-start | bytes 1572872 | tf_op jit(solution)/shard_map/ppermute | solution.py:49
  280.7 26.4 %collective-permute-start.42 = (bf16[512,1024]{1,0:T(8,128)(2,1)S(1)}, bf16[512,1024]{1,0:T(8,128)(2,1)S(1)}, u32[]{:S(2)}, u32[]{:S(2)}) collective-permute-start(bf16[512,1024]{1,0:T(8,128)(2,1)S(1)} %mix.18), channel_id=1, source_target_pairs={{0,8},{24,16},{1,9},{25,17},{2,10},{26,18},{3,11},{27,19},{4,12},{... | collective-permute-start | bytes 3145736 | tf_op jit(solution)/shard_map/ppermute | solution.py:271
  315.4 39.4 %collective-permute-start.68 = (bf16[512,1024]{1,0:T(8,128)(2,1)S(1)}, bf16[512,1024]{1,0:T(8,128)(2,1)}, u32[]{:S(2)}, u32[]{:S(2)}) collective-permute-start(bf16[512,1024]{1,0:T(8,128)(2,1)S(1)} %get-tuple-element.278.refs_3_), channel_id=1, source_target_pairs={{8,16},{16,8},{9,17},{17,9},{10,18},{18,10},{11,19},{19,11},{12,20... | collective-permute-start | bytes 3145736 | tf_op jit(solution)/shard_map/ppermute | solution.py:273
  317.1 37.8 %collective-permute-start.67 = (bf16[512,1024]{1,0:T(8,128)(2,1)}, bf16[512,1024]{1,0:T(8,128)(2,1)}, u32[]{:S(2)}, u32[]{:S(2)}) collective-permute-start(bf16[512,1024]{1,0:T(8,128)(2,1)} %get-tuple-element.319), channel_id=1, source_target_pairs={{0,8},{24,16},{1,9},{25,17},{2,10},{26,18},{3,11},{27,19},{4,12},{... | collective-permute-start | bytes 3145736 | tf_op jit(solution)/shard_map/ppermute | solution.py:271
  350.3 42.9 %all-to-all-start.2 = ((bf16[4,256,1024]{2,1,0:T(8,128)(2,1)}), bf16[4,256,1024]{2,1,0:T(8,128)(2,1)}, u32[]{:S(2)}, u32[]{:S(2)}) async-start(bf16[4,256,1024]{2,1,0:T(8,128)(2,1)} %slice.718), calls=%async_computation.2 | async-start | bytes 4194304 | tf_op jit(solution)/shard_map/all_to_all | solution.py:947
  358.6 25.6 %collective-permute-start.69 = (bf16[512,1024]{1,0:T(8,128)(2,1)S(1)}, bf16[512,1024]{1,0:T(8,128)(2,1)S(1)}, u32[]{:S(2)}, u32[]{:S(2)}) collective-permute-start(bf16[512,1024]{1,0:T(8,128)(2,1)S(1)} %get-tuple-element.322.refs_5_), channel_id=1, source_target_pairs={{0,8},{24,16},{8,0},{16,24},{1,9},{25,17},{9,1},{17,25},{2,10},{26... | collective-permute-start | bytes 3145736 | tf_op jit(solution)/shard_map/ppermute | solution.py:271
  358.8 27.1 %collective-permute-start.70 = (bf16[512,1024]{1,0:T(8,128)(2,1)S(1)}, bf16[512,1024]{1,0:T(8,128)(2,1)S(1)}, u32[]{:S(2)}, u32[]{:S(2)}) collective-permute-start(bf16[512,1024]{1,0:T(8,128)(2,1)S(1)} %get-tuple-element.323.refs_3_), channel_id=1, source_target_pairs={{8,16},{16,8},{9,17},{17,9},{10,18},{18,10},{11,19},{19,11},{12,20... | collective-permute-start | bytes 3145736 | tf_op jit(solution)/shard_map/ppermute | solution.py:273
  361.3 28.8 %collective-permute-start.51 = (bf16[128,1024]{1,0:T(8,128)(2,1)S(1)}, bf16[128,1024]{1,0:T(8,128)(2,1)S(1)}, u32[]{:S(2)}, u32[]{:S(2)}) collective-permute-start(bf16[128,1024]{1,0:T(8,128)(2,1)S(1)} %fusion.52), channel_id=1, source_target_pairs={{0,2},{1,3},{2,0},{3,1},{4,6},{5,7},{6,4},{7,5},{8,10},{9,11},{10,... | collective-permute-start | bytes 786440 | tf_op jit(solution)/shard_map/ppermute | solution.py:49
  364.4 27.4 %collective-permute-start.52 = (bf16[128,1024]{1,0:T(8,128)(2,1)S(1)}, bf16[128,1024]{1,0:T(8,128)(2,1)}, u32[]{:S(2)}, u32[]{:S(2)}) collective-permute-start(bf16[128,1024]{1,0:T(8,128)(2,1)S(1)} %fusion.53), channel_id=1, source_target_pairs={{0,4},{1,5},{2,6},{3,7},{4,0},{5,1},{6,2},{7,3},{8,12},{9,13},{10,... | collective-permute-start | bytes 786440 | tf_op jit(solution)/shard_map/ppermute | solution.py:49
  391.8 26.4 %collective-permute-start.73 = (bf16[512,1024]{1,0:T(8,128)(2,1)}, bf16[512,1024]{1,0:T(8,128)(2,1)}, u32[]{:S(2)}, u32[]{:S(2)}) collective-permute-start(bf16[512,1024]{1,0:T(8,128)(2,1)} %get-tuple-element.328.refs_0_), channel_id=1, source_target_pairs={{0,4},{4,0},{1,5},{5,1},{2,6},{6,2},{3,7},{7,3},{8,12},{12,8},{9,1... | collective-permute-start | bytes 3145736 | tf_op jit(solution)/shard_map/ppermute | solution.py:276
  400.1 26.1 %collective-permute-start.49 = (bf16[128,1024]{1,0:T(8,128)(2,1)S(1)}, bf16[128,1024]{1,0:T(8,128)(2,1)S(1)}, u32[]{:S(2)}, u32[]{:S(2)}) collective-permute-start(bf16[128,1024]{1,0:T(8,128)(2,1)S(1)} %fusion.50), channel_id=1, source_target_pairs={{0,2},{1,3},{2,0},{3,1},{4,6},{5,7},{6,4},{7,5},{8,10},{9,11},{10,... | collective-permute-start | bytes 786440 | tf_op jit(solution)/shard_map/ppermute | solution.py:49
  423.3 34.0 %collective-permute-start.75 = (bf16[512,1024]{1,0:T(8,128)(2,1)}, bf16[512,1024]{1,0:T(8,128)(2,1)}, u32[]{:S(2)}, u32[]{:S(2)}) collective-permute-start(bf16[512,1024]{1,0:T(8,128)(2,1)} %get-tuple-element.332.refs_3_), channel_id=1, source_target_pairs={{8,16},{16,8},{9,17},{17,9},{10,18},{18,10},{11,19},{19,11},{12,20... | collective-permute-start | bytes 3145736 | tf_op jit(solution)/shard_map/ppermute | solution.py:273
  424.9 32.4 %collective-permute-start.76 = (bf16[512,1024]{1,0:T(8,128)(2,1)S(1)}, bf16[512,1024]{1,0:T(8,128)(2,1)}, u32[]{:S(2)}, u32[]{:S(2)}) collective-permute-start(bf16[512,1024]{1,0:T(8,128)(2,1)S(1)} %get-tuple-element.333.refs_0_), channel_id=1, source_target_pairs={{0,4},{4,0},{1,5},{5,1},{2,6},{6,2},{3,7},{7,3},{8,12},{12,8},{9,1... | collective-permute-start | bytes 3145736 | tf_op jit(solution)/shard_map/ppermute | solution.py:276
  428.1 38.4 %collective-permute-start.53 = (bf16[128,2048]{1,0:T(8,128)(2,1)}, bf16[128,2048]{1,0:T(8,128)(2,1)}, u32[]{:S(2)}, u32[]{:S(2)}) collective-permute-start(bf16[128,2048]{1,0:T(8,128)(2,1)} %get-tuple-element.445), channel_id=1, source_target_pairs={{0,2},{1,3},{2,0},{3,1},{4,6},{5,7},{6,4},{7,5},{8,10},{9,11},{10,... | collective-permute-start | bytes 1572872 | tf_op jit(solution)/shard_map/ppermute | solution.py:49
  429.7 36.8 %collective-permute-start.54 = (bf16[128,2048]{1,0:T(8,128)(2,1)}, bf16[128,2048]{1,0:T(8,128)(2,1)}, u32[]{:S(2)}, u32[]{:S(2)}) collective-permute-start(bf16[128,2048]{1,0:T(8,128)(2,1)} %get-tuple-element.445), channel_id=1, source_target_pairs={{0,4},{1,5},{2,6},{3,7},{4,0},{5,1},{6,2},{7,3},{8,12},{9,13},{10,... | collective-permute-start | bytes 1572872 | tf_op jit(solution)/shard_map/ppermute | solution.py:49
  447.7 41.8 %all-to-all-start.3 = ((bf16[4,256,1024]{2,1,0:T(8,128)(2,1)}), bf16[4,256,1024]{2,1,0:T(8,128)(2,1)}, u32[]{:S(2)}, u32[]{:S(2)}) async-start(bf16[4,256,1024]{2,1,0:T(8,128)(2,1)} %slice.613), calls=%async_computation.3 | async-start | bytes 4194304 | tf_op jit(solution)/shard_map/all_to_all | solution.py:947
  461.3 44.2 %collective-permute-start.77 = (bf16[512,1024]{1,0:T(8,128)(2,1)}, bf16[512,1024]{1,0:T(8,128)(2,1)}, u32[]{:S(2)}, u32[]{:S(2)}) collective-permute-start(bf16[512,1024]{1,0:T(8,128)(2,1)} %get-tuple-element.337.refs_5_), channel_id=1, source_target_pairs={{0,8},{24,16},{8,0},{16,24},{1,9},{25,17},{9,1},{17,25},{2,10},{26... | collective-permute-start | bytes 3145736 | tf_op jit(solution)/shard_map/ppermute | solution.py:271
  478.2 27.4 %collective-permute-start.78 = (bf16[512,1024]{1,0:T(8,128)(2,1)}, bf16[512,1024]{1,0:T(8,128)(2,1)}, u32[]{:S(2)}, u32[]{:S(2)}) collective-permute-start(bf16[512,1024]{1,0:T(8,128)(2,1)} %get-tuple-element.338.refs_3_), channel_id=1, source_target_pairs={{8,16},{16,8},{9,17},{17,9},{10,18},{18,10},{11,19},{19,11},{12,20... | collective-permute-start | bytes 3145736 | tf_op jit(solution)/shard_map/ppermute | solution.py:273
  512.6 25.8 %collective-permute-start.80 = (bf16[512,1024]{1,0:T(8,128)(2,1)}, bf16[512,1024]{1,0:T(8,128)(2,1)}, u32[]{:S(2)}, u32[]{:S(2)}) collective-permute-start(bf16[512,1024]{1,0:T(8,128)(2,1)} %get-tuple-element.344.refs_5_), channel_id=1, source_target_pairs={{0,8},{24,16},{8,0},{16,24},{1,9},{25,17},{9,1},{17,25},{2,10},{26... | collective-permute-start | bytes 3145736 | tf_op jit(solution)/shard_map/ppermute | solution.py:271
  519.8 38.3 %all-to-all-start.5 = ((bf16[4,256,1024]{2,1,0:T(8,128)(2,1)}), bf16[4,256,1024]{2,1,0:T(8,128)(2,1)S(1)}, u32[]{:S(2)}, u32[]{:S(2)}) async-start(bf16[4,256,1024]{2,1,0:T(8,128)(2,1)} %slice.614), calls=%async_computation.5 | async-start | bytes 4194304 | tf_op jit(solution)/shard_map/all_to_all | solution.py:947
  561.9 51.7 %all-to-all-start.6 = ((bf16[4,256,1024]{2,1,0:T(8,128)(2,1)}), bf16[4,256,1024]{2,1,0:T(8,128)(2,1)S(1)}, u32[]{:S(2)}, u32[]{:S(2)}) async-start(bf16[4,256,1024]{2,1,0:T(8,128)(2,1)} %slice.615), calls=%async_computation.6 | async-start | bytes 4194304 | tf_op jit(solution)/shard_map/all_to_all | solution.py:947
  575.5 49.5 %collective-permute-start.86 = (bf16[512,1024]{1,0:T(8,128)(2,1)}, bf16[512,1024]{1,0:T(8,128)(2,1)}, u32[]{:S(2)}, u32[]{:S(2)}) collective-permute-start(bf16[512,1024]{1,0:T(8,128)(2,1)} %get-tuple-element.358.refs_5_), channel_id=1, source_target_pairs={{0,8},{24,16},{8,0},{16,24},{1,9},{25,17},{9,1},{17,25},{2,10},{26... | collective-permute-start | bytes 3145736 | tf_op jit(solution)/shard_map/ppermute | solution.py:271
  578.8 46.3 %collective-permute-start.87 = (bf16[512,1024]{1,0:T(8,128)(2,1)}, bf16[512,1024]{1,0:T(8,128)(2,1)}, u32[]{:S(2)}, u32[]{:S(2)}) collective-permute-start(bf16[512,1024]{1,0:T(8,128)(2,1)} %get-tuple-element.359.refs_3_), channel_id=1, source_target_pairs={{8,16},{16,8},{9,17},{17,9},{10,18},{18,10},{11,19},{19,11},{12,20... | collective-permute-start | bytes 3145736 | tf_op jit(solution)/shard_map/ppermute | solution.py:273
  580.4 44.7 %collective-permute-start.88 = (bf16[512,1024]{1,0:T(8,128)(2,1)}, bf16[512,1024]{1,0:T(8,128)(2,1)}, u32[]{:S(2)}, u32[]{:S(2)}) collective-permute-start(bf16[512,1024]{1,0:T(8,128)(2,1)} %get-tuple-element.360), channel_id=1, source_target_pairs={{0,4},{4,0},{1,5},{5,1},{2,6},{6,2},{3,7},{7,3},{8,12},{12,8},{9,1... | collective-permute-start | bytes 3145736 | tf_op jit(solution)/shard_map/ppermute | solution.py:276
  615.9 28.7 %all-to-all-start.7 = ((bf16[4,128,1024]{2,1,0:T(8,128)(2,1)}), bf16[4,128,1024]{2,1,0:T(8,128)(2,1)}, u32[]{:S(2)}, u32[]{:S(2)}) async-start(bf16[4,128,1024]{2,1,0:T(8,128)(2,1)} %slice.617), calls=%async_computation.7 | async-start | bytes 2097152 | tf_op jit(solution)/shard_map/all_to_all | solution.py:881
  629.1 31.9 %collective-permute-start.89 = (bf16[512,1024]{1,0:T(8,128)(2,1)}, bf16[512,1024]{1,0:T(8,128)(2,1)}, u32[]{:S(2)}, u32[]{:S(2)}) collective-permute-start(bf16[512,1024]{1,0:T(8,128)(2,1)} %get-tuple-element.364.refs_5_), channel_id=1, source_target_pairs={{0,8},{24,16},{8,0},{16,24},{1,9},{25,17},{9,1},{17,25},{2,10},{26... | collective-permute-start | bytes 3145736 | tf_op jit(solution)/shard_map/ppermute | solution.py:271
  631.6 29.4 %collective-permute-start.90 = (bf16[512,1024]{1,0:T(8,128)(2,1)}, bf16[512,1024]{1,0:T(8,128)(2,1)}, u32[]{:S(2)}, u32[]{:S(2)}) collective-permute-start(bf16[512,1024]{1,0:T(8,128)(2,1)} %get-tuple-element.365.refs_3_), channel_id=1, source_target_pairs={{8,16},{16,8},{9,17},{17,9},{10,18},{18,10},{11,19},{19,11},{12,20... | collective-permute-start | bytes 3145736 | tf_op jit(solution)/shard_map/ppermute | solution.py:273
  633.3 27.7 %collective-permute-start.91 = (bf16[512,1024]{1,0:T(8,128)(2,1)}, bf16[512,1024]{1,0:T(8,128)(2,1)}, u32[]{:S(2)}, u32[]{:S(2)}) collective-permute-start(bf16[512,1024]{1,0:T(8,128)(2,1)} %get-tuple-element.366), channel_id=1, source_target_pairs={{0,4},{4,0},{1,5},{5,1},{2,6},{6,2},{3,7},{7,3},{8,12},{12,8},{9,1... | collective-permute-start | bytes 3145736 | tf_op jit(solution)/shard_map/ppermute | solution.py:276
  644.6 40.2 %all-to-all-start.8 = ((bf16[4,64,1024]{2,1,0:T(8,128)(2,1)}), bf16[4,64,1024]{2,1,0:T(8,128)(2,1)}, u32[]{:S(2)}, u32[]{:S(2)}) async-start(bf16[4,64,1024]{2,1,0:T(8,128)(2,1)} %slice.616), calls=%async_computation.8 | async-start | bytes 1048576 | tf_op jit(solution)/shard_map/all_to_all | solution.py:881
  665.0 35.4 %collective-permute-start.92 = (bf16[512,1024]{1,0:T(8,128)(2,1)}, bf16[512,1024]{1,0:T(8,128)(2,1)}, u32[]{:S(2)}, u32[]{:S(2)}) collective-permute-start(bf16[512,1024]{1,0:T(8,128)(2,1)} %get-tuple-element.371.refs_5_), channel_id=1, source_target_pairs={{0,8},{24,16},{8,0},{16,24},{1,9},{25,17},{9,1},{17,25},{2,10},{26... | collective-permute-start | bytes 3145736 | tf_op jit(solution)/shard_map/ppermute | solution.py:271
  691.2 49.3 %all-to-all-start.9 = ((bf16[4,512,384]{2,1,0:T(8,128)(2,1)}), bf16[4,512,384]{2,1,0:T(8,128)(2,1)}, u32[]{:S(2)}, u32[]{:S(2)}) async-start(bf16[4,512,384]{2,1,0:T(8,128)(2,1)} %bitcast.376), calls=%async_computation.9 | async-start | bytes 3145728 | tf_op jit(solution)/shard_map/all_to_all | solution.py:947
  702.8 25.8 %collective-permute-start.95 = (bf16[512,1024]{1,0:T(8,128)(2,1)S(1)}, bf16[512,1024]{1,0:T(8,128)(2,1)S(1)}, u32[]{:S(2)}, u32[]{:S(2)}) collective-permute-start(bf16[512,1024]{1,0:T(8,128)(2,1)S(1)} %get-tuple-element.378.refs_5_), channel_id=1, source_target_pairs={{0,8},{24,16},{8,0},{16,24},{1,9},{25,17},{9,1},{17,25},{2,10},{26... | collective-permute-start | bytes 3145736 | tf_op jit(solution)/shard_map/ppermute | solution.py:271
  714.0 54.5 %collective-permute-start.62 = (bf16[512,2048]{1,0:T(8,128)(2,1)}, bf16[512,2048]{1,0:T(8,128)(2,1)}, u32[]{:S(2)}, u32[]{:S(2)}) collective-permute-start(bf16[512,2048]{1,0:T(8,128)(2,1)} %convolution_convert_fusion.4), channel_id=1, source_target_pairs={{0,1},{1,0},{2,3},{3,2},{4,5},{5,4},{6,7},{7,6},{8,9},{9,8},{10,11... | collective-permute-start | bytes 6291464 | tf_op jit(solution)/shard_map/ppermute | solution.py:49
  764.4 38.1 %collective-permute-start.101 = (bf16[512,1024]{1,0:T(8,128)(2,1)S(1)}, bf16[512,1024]{1,0:T(8,128)(2,1)S(1)}, u32[]{:S(2)}, u32[]{:S(2)}) collective-permute-start(bf16[512,1024]{1,0:T(8,128)(2,1)S(1)} %get-tuple-element.391.refs_5_), channel_id=1, source_target_pairs={{0,8},{24,16},{8,0},{16,24},{1,9},{25,17},{9,1},{17,25},{2,10},{26... | collective-permute-start | bytes 3145736 | tf_op jit(solution)/shard_map/ppermute | solution.py:271
  767.4 35.1 %collective-permute-start.102 = (bf16[512,1024]{1,0:T(8,128)(2,1)S(1)}, bf16[512,1024]{1,0:T(8,128)(2,1)S(1)}, u32[]{:S(2)}, u32[]{:S(2)}) collective-permute-start(bf16[512,1024]{1,0:T(8,128)(2,1)S(1)} %get-tuple-element.392.refs_3_), channel_id=1, source_target_pairs={{8,16},{16,8},{9,17},{17,9},{10,18},{18,10},{11,19},{19,11},{12,20... | collective-permute-start | bytes 3145736 | tf_op jit(solution)/shard_map/ppermute | solution.py:273
  768.1 34.4 %collective-permute-start.103 = (bf16[512,1024]{1,0:T(8,128)(2,1)S(1)}, bf16[512,1024]{1,0:T(8,128)(2,1)S(1)}, u32[]{:S(2)}, u32[]{:S(2)}) collective-permute-start(bf16[512,1024]{1,0:T(8,128)(2,1)S(1)} %get-tuple-element.393), channel_id=1, source_target_pairs={{0,4},{4,0},{1,5},{5,1},{2,6},{6,2},{3,7},{7,3},{8,12},{12,8},{9,1... | collective-permute-start | bytes 3145736 | tf_op jit(solution)/shard_map/ppermute | solution.py:276
  771.2 31.3 %collective-permute-start.63 = (bf16[2,128,1024]{2,1,0:T(8,128)(2,1)S(1)}, bf16[2,128,1024]{2,1,0:T(8,128)(2,1)S(1)}, u32[]{:S(2)}, u32[]{:S(2)}) collective-permute-start(bf16[2,128,1024]{2,1,0:T(8,128)(2,1)S(1)} %slice.1035), channel_id=1, source_target_pairs={{0,4},{1,5},{2,6},{3,7},{4,0},{5,1},{6,2},{7,3},{8,12},{9,13},{10,... | collective-permute-start | bytes 1572872 | tf_op jit(solution)/shard_map/ppermute | solution.py:49
  773.0 29.4 %collective-permute-start.64 = (bf16[2,128,1024]{2,1,0:T(8,128)(2,1)S(1)}, bf16[2,128,1024]{2,1,0:T(8,128)(2,1)S(1)}, u32[]{:S(2)}, u32[]{:S(2)}) collective-permute-start(bf16[2,128,1024]{2,1,0:T(8,128)(2,1)S(1)} %slice.628), channel_id=1, source_target_pairs={{0,2},{1,3},{2,0},{3,1},{4,6},{5,7},{6,4},{7,5},{8,10},{9,11},{10,... | collective-permute-start | bytes 1572872 | tf_op jit(solution)/shard_map/ppermute | solution.py:49
  805.4 26.1 %collective-permute-start.106 = (bf16[512,1024]{1,0:T(8,128)(2,1)S(1)}, bf16[512,1024]{1,0:T(8,128)(2,1)S(1)}, u32[]{:S(2)}, u32[]{:S(2)}) collective-permute-start(bf16[512,1024]{1,0:T(8,128)(2,1)S(1)} %get-tuple-element.400), channel_id=1, source_target_pairs={{0,4},{4,0},{1,5},{5,1},{2,6},{6,2},{3,7},{7,3},{8,12},{12,8},{9,1... | collective-permute-start | bytes 3145736 | tf_op jit(solution)/shard_map/ppermute | solution.py:276
  808.0 29.1 %collective-permute-start.66 = (bf16[128,1024]{1,0:T(8,128)(2,1)S(1)}, bf16[128,1024]{1,0:T(8,128)(2,1)S(1)}, u32[]{:S(2)}, u32[]{:S(2)}) collective-permute-start(bf16[128,1024]{1,0:T(8,128)(2,1)S(1)} %fusion.55), channel_id=1, source_target_pairs={{0,4},{1,5},{2,6},{3,7},{4,0},{5,1},{6,2},{7,3},{8,12},{9,13},{10,... | collective-permute-start | bytes 786440 | tf_op jit(solution)/shard_map/ppermute | solution.py:49
  831.6 29.0 %collective-permute-start.109 = (bf16[512,1024]{1,0:T(8,128)(2,1)S(1)}, bf16[512,1024]{1,0:T(8,128)(2,1)S(1)}, u32[]{:S(2)}, u32[]{:S(2)}) collective-permute-start(bf16[512,1024]{1,0:T(8,128)(2,1)S(1)} %get-tuple-element.407.refs_0_), channel_id=1, source_target_pairs={{0,4},{4,0},{1,5},{5,1},{2,6},{6,2},{3,7},{7,3},{8,12},{12,8},{9,1... | collective-permute-start | bytes 3145736 | tf_op jit(solution)/shard_map/ppermute | solution.py:276
  (173 other events, 2497.0 us)

commit v5 on v4

--- a/solution.py
+++ b/solution.py
@@ -990,8 +990,8 @@
         box["gate0"], gate_now = yield [gate0, gate_partial]
         gate1 = to_shards(gate_now[:, half_rows:])
         yield []
+        (box["gate1"],) = yield [gate1]
         yield []
-        (box["gate1"],) = yield [gate1]
         up_now = after(up_partial, *box["now"])
         (box["up0"],) = yield [to_shards(up_now[:, :half_rows])]
         up_now = after(up_partial, *box["now"])

time: 923 us -> 915 us (level)
  waiting for transfers between devices: 315 us -> 301 us
    ppermute x17, waiting for transfers between devices: 98.5 us -> 81.2 us  [stream(): moves['got'] = lax.ppermute(sending, 'line', pairs)]
where the time goes in v5:
time: 915 us; the launch traced here: 902 us
  waiting for transfers between devices  301 us (33%)
  starting transfers between devices  197 us (22%)
  Pallas kernels  162 us (18%)
  local copies, waits for them, and re-layouts  117 us (13%)
  matrix products  79.9 us (9%)
  other arithmetic  42.6 us (5%)
    ppermute x61, waiting for transfers between devices, swap(): return lax.ppermute(value, SLAB, [(i, i ^ flip) for i in range(KVH)])  106 us
    ppermute x17, waiting for transfers between devices, stream(): moves['got'] = lax.ppermute(sending, 'line', pairs)  81.2 us
    dot_general x17, matrix products, contract(): lax.dot_general(left, right, (((left_dim,), (right_dim,)), ((), ())), pre...  79.9 us
    ppermute x17, starting transfers between devices, stream(): moves['got'] = lax.ppermute(sending, 'line', pairs)  59 us
    ppermute x12, waiting for transfers between devices, pass_on(): return lax.ppermute(block, 'wshard', [(i, i ^ flip) for i in range(shards)])  50.5 us
    dynamic_update_slice x38, local copies, waits for them, and re-layouts, put(): lax.dynamic_update_slice(total, piece, (index * half,) + (0,) * (block.nd...  44.9 us
    pallas_call x18, Pallas kernels, mix(): pl.pallas_call(functools.partial(mix_kernel, tuple(names) + tuple(results...  43.9 us
    ppermute x61, starting transfers between devices, swap(): return lax.ppermute(value, SLAB, [(i, i ^ flip) for i in range(KVH)])  40 us
  transfers between devices with their start and end apart: 133, of which 48 were waited for; matrix products, arithmetic and copies ran while one was open for 20% of the time, Pallas kernels for 17%

profile of v5, /device:TPU:0, one launch (start us, length us, event | category | flops | bytes accessed | tf_op | source)
XLA Modules:
  0.0 901.6 jit_solution(3261337660071198013)
XLA Ops:
  42.0 7.1 collective-permute-done.8
  54.4 9.3 %collective-permute-done.14 = bf16[512,384]{1,0:T(8,128)(2,1)S(1)} collective-permute-done((bf16[512,384]{1,0:T(8,128)(2,1)S(1)}, bf16[512,384]{1,0:T(8,128)(2,1)S(1)}, u32[]{:S(2)}, u32[]{:S(2)}) %collective-permute-start.14) | collective-permute-done | bytes 393248 | tf_op jit(solution)/shard_map/ppermute | solution.py:783
  74.0 5.0 all-to-all-start
  79.5 13.2 %collective-permute-done.15 = bf16[128,2048]{1,0:T(8,128)(2,1)S(1)} collective-permute-done((bf16[128,2048]{1,0:T(8,128)(2,1)S(1)}, bf16[128,2048]{1,0:T(8,128)(2,1)S(1)}, u32[]{:S(2)}, u32[]{:S(2)}) %collective-permute-start.15) | collective-permute-done | bytes 524320 | tf_op jit(solution)/shard_map/ppermute | solution.py:49
  101.5 8.9 collective-permute-done.18
  110.4 11.2 %collective-permute-done.17 = bf16[512,1024]{1,0:T(8,128)(2,1)} collective-permute-done((bf16[512,1024]{1,0:T(8,128)(2,1)}, bf16[512,1024]{1,0:T(8,128)(2,1)}, u32[]{:S(2)}, u32[]{:S(2)}) %collective-permute-start.17) | collective-permute-done | bytes 1048608 | tf_op jit(solution)/shard_map/ppermute | solution.py:783
  125.9 22.3 %attend_forward.1 = (bf16[4,64,1024]{2,1,0:T(8,128)(2,1)}, bf16[192,4096]{1,0:T(8,128)(2,1)}, f32[64,4096]{1,0:T(8,128)}, f32[1,4096]{1,0:T(1,128)}) custom-call(s32[64]{0:T(128)} %select_reduce_fusion.sort_ref, s32[64]{0:T(128)} %copy-done.82, s32[2]{0:T(128)} %pad_add_fusion.range_ref, bf16[4,192,1024]{2,1,0:T(8,128)(2,1)} %all-to-all-done.blocks_ref), custom_call_target="tpu_custom_call" | custom-call | flops 30000001024 | bytes 8000000 | tf_op jit(solution)/shard_map/attend_forward/pallas_call | solution.py:673
  156.9 4.8 all-to-all-start.1
  169.2 7.1 all-to-all-done.1
  195.9 18.4 %collective-permute-done.30 = bf16[512,1024]{1,0:T(8,128)(2,1)S(1)} collective-permute-done((bf16[512,1024]{1,0:T(8,128)(2,1)S(1)}, bf16[512,1024]{1,0:T(8,128)(2,1)S(1)}, u32[]{:S(2)}, u32[]{:S(2)}) %collective-permute-start.30) | collective-permute-done | bytes 1048608 | tf_op jit(solution)/shard_map/ppermute | solution.py:783
  214.3 11.7 %collective-permute-done.29 = bf16[2,128,1024]{2,1,0:T(8,128)(2,1)S(1)} collective-permute-done((bf16[2,128,1024]{2,1,0:T(8,128)(2,1)S(1)}, bf16[2,128,1024]{2,1,0:T(8,128)(2,1)S(1)}, u32[]{:S(2)}, u32[]{:S(2)}) %collective-permute-start.29) | collective-permute-done | bytes 524320 | tf_op jit(solution)/shard_map/ppermute | solution.py:49
  228.2 7.0 fusion.7
  241.9 8.6 collective-permute-done.33
  260.1 8.8 fusion.89
  273.0 7.4 convolution_convert_fusion.1.refs_0_.refs_1_
  286.8 6.2 convolution_convert_fusion.2
  293.0 14.0 %collective-permute-done.42.refs_2_ = bf16[512,1024]{1,0:T(8,128)(2,1)S(1)} collective-permute-done((bf16[512,1024]{1,0:T(8,128)(2,1)S(1)}, bf16[512,1024]{1,0:T(8,128)(2,1)S(1)}, u32[]{:S(2)}, u32[]{:S(2)}) %collective-permute-start.42) | collective-permute-done | bytes 1048608 | tf_op jit(solution)/shard_map/ppermute | solution.py:271
  309.6 5.7 convolution_convert_fusion.5
  317.0 7.3 collective-permute-start.67
  324.3 6.1 convert_add_fusion.2
  334.1 6.2 convolution_convert_fusion
  375.6 8.6 collective-permute-done.69.refs_2_
  413.2 5.0 collective-permute-done.73.refs_1_
  426.3 5.8 collective-permute-done.49
  434.9 8.5 collective-permute-done.74.refs_2_
  444.5 5.1 place_blocks.5.refs_2_
  490.7 4.9 place_blocks.6.refs_2_
  502.7 7.9 collective-permute-start.80
  519.2 5.1 place_blocks.7.refs_2_
  524.3 6.7 collective-permute-done.80.refs_2_
  535.8 5.0 collective-permute-start.83
  546.8 4.9 place_blocks.8
  573.2 33.0 %attend_backward.1 = bf16[4,192,1024]{2,1,0:T(8,128)(2,1)} custom-call(s32[64]{0:T(128)} %select_reduce_fusion.sort_ref, s32[64]{0:T(128)} %copy-done.82, s32[2]{0:T(128)} %pad_add_fusion.range_ref, bf16[192,4096]{1,0:T(8,128)(2,1)} %get-tuple-element.290.sorted_ref, f32[64,4096]{1,0:T(8,128)} %get-tuple-element.291.float_ref, ...), custom_call_target="tpu_custom_call" | custom-call | flops 35999997952 | bytes 8000000 | tf_op jit(solution)/shard_map/attend_backward/pallas_call | solution.py:699
  612.8 4.8 place_columns.8.refs_2_
  629.3 7.9 all-to-all-done.7
  641.4 4.8 place_columns.9.refs_2_
  646.3 8.0 collective-permute-done.89.refs_2_
  658.3 12.1 %collective-permute-start.92 = (bf16[512,1024]{1,0:T(8,128)(2,1)}, bf16[512,1024]{1,0:T(8,128)(2,1)}, u32[]{:S(2)}, u32[]{:S(2)}) collective-permute-start(bf16[512,1024]{1,0:T(8,128)(2,1)} %get-tuple-element.371.refs_5_), channel_id=1, source_target_pairs={{0,8},{24,16},{8,0},{16,24},{1,9},{25,17},{9,1},{17,25},{2,10},{26... | collective-permute-start | bytes 3145736 | tf_op jit(solution)/shard_map/ppermute | solution.py:271
  688.1 4.8 place_columns.10.refs_2_
  699.3 4.9 place_columns.11
  710.3 10.7 %collective-permute-done.95.refs_2_ = bf16[512,1024]{1,0:T(8,128)(2,1)S(1)} collective-permute-done((bf16[512,1024]{1,0:T(8,128)(2,1)S(1)}, bf16[512,1024]{1,0:T(8,128)(2,1)S(1)}, u32[]{:S(2)}, u32[]{:S(2)}) %collective-permute-start.95) | collective-permute-done | bytes 1048608 | tf_op jit(solution)/shard_map/ppermute | solution.py:271
  740.8 8.7 collective-permute-done.98.refs_2_
  770.2 22.9 %collective-permute-done.63 = bf16[2,128,1024]{2,1,0:T(8,128)(2,1)S(1)} collective-permute-done((bf16[2,128,1024]{2,1,0:T(8,128)(2,1)S(1)}, bf16[2,128,1024]{2,1,0:T(8,128)(2,1)S(1)}, u32[]{:S(2)}, u32[]{:S(2)}) %collective-permute-start.63) | collective-permute-done | bytes 524320 | tf_op jit(solution)/shard_map/ppermute | solution.py:49
  803.2 13.3 %collective-permute-done.104.refs_1_ = bf16[512,1024]{1,0:T(8,128)(2,1)S(1)} collective-permute-done((bf16[512,1024]{1,0:T(8,128)(2,1)S(1)}, bf16[512,1024]{1,0:T(8,128)(2,1)S(1)}, u32[]{:S(2)}, u32[]{:S(2)}) %collective-permute-start.104) | collective-permute-done | bytes 1048608 | tf_op jit(solution)/shard_map/ppermute | solution.py:271
  816.4 7.0 collective-permute-done.106
  837.9 9.8 %collective-permute-done.113 = f32[2,2048]{1,0:T(2,128)S(1)} collective-permute-done((f32[2,2048]{1,0:T(2,128)S(1)}, f32[2,2048]{1,0:T(2,128)S(1)}, u32[]{:S(2)}, u32[]{:S(2)}) %collective-permute-start.113) | collective-permute-done | bytes 16416 | tf_op jit(solution)/shard_map/ppermute | solution.py:49
  866.6 10.1 %collective-permute-done.121 = f32[2,2048]{1,0:T(2,128)S(1)} collective-permute-done((f32[2,2048]{1,0:T(2,128)S(1)}, f32[2,2048]{1,0:T(2,128)S(1)}, u32[]{:S(2)}, u32[]{:S(2)}) %collective-permute-start.121) | collective-permute-done | bytes 16416 | tf_op jit(solution)/shard_map/ppermute | solution.py:477
  886.6 11.9 %collective-permute-done.122.refs_1_ = bf16[384,1024]{1,0:T(8,128)(2,1)S(1)} collective-permute-done((bf16[384,1024]{1,0:T(8,128)(2,1)S(1)}, bf16[384,1024]{1,0:T(8,128)(2,1)S(1)}, u32[]{:S(2)}, u32[]{:S(2)}) %collective-permute-start.122) | collective-permute-done | bytes 786464 | tf_op jit(solution)/shard_map/ppermute | solution.py:276
  (638 shorter events, 459.9 us)
Async XLA Ops:
  20.4 28.7 %collective-permute-start.6 = (bf16[128,2048]{1,0:T(8,128)(2,1)}, bf16[128,2048]{1,0:T(8,128)(2,1)S(1)}, u32[]{:S(2)}, u32[]{:S(2)}) collective-permute-start(bf16[128,2048]{1,0:T(8,128)(2,1)} %collective-permute-done), channel_id=1, source_target_pairs={{0,1},{1,0},{2,3},{3,2},{4,5},{5,4},{6,7},{7,6},{8,9},{9,8},{10,11... | collective-permute-start | bytes 1572872 | tf_op jit(solution)/shard_map/ppermute | solution.py:49
  22.4 26.7 %collective-permute-start.7 = (bf16[128,2048]{1,0:T(8,128)(2,1)}, bf16[128,2048]{1,0:T(8,128)(2,1)S(1)}, u32[]{:S(2)}, u32[]{:S(2)}) collective-permute-start(bf16[128,2048]{1,0:T(8,128)(2,1)} %collective-permute-done.1), channel_id=1, source_target_pairs={{0,1},{1,0},{2,3},{3,2},{4,5},{5,4},{6,7},{7,6},{8,9},{9,8},{10,11... | collective-permute-start | bytes 1572872 | tf_op jit(solution)/shard_map/ppermute | solution.py:49
  74.0 47.6 %all-to-all-start = ((bf16[4,192,1024]{2,1,0:T(8,128)(2,1)}), bf16[4,192,1024]{2,1,0:T(8,128)(2,1)}, u32[]{:S(2)}, u32[]{:S(2)}) async-start(bf16[4,192,1024]{2,1,0:T(8,128)(2,1)} %pad_maximum_fusion.1), calls=%async_computation | async-start | bytes 3145728 | tf_op jit(solution)/shard_map/all_to_all | solution.py:857
  95.7 25.9 %collective-permute-start.17 = (bf16[512,1024]{1,0:T(8,128)(2,1)}, bf16[512,1024]{1,0:T(8,128)(2,1)}, u32[]{:S(2)}, u32[]{:S(2)}) collective-permute-start(bf16[512,1024]{1,0:T(8,128)(2,1)} %get-tuple-element.454), channel_id=1, source_target_pairs={{0,2},{1,3},{2,0},{3,1},{4,6},{5,7},{6,4},{7,5},{8,10},{9,11},{10,... | collective-permute-start | bytes 3145736 | tf_op jit(solution)/shard_map/ppermute | solution.py:783
  121.6 27.4 %collective-permute-start.22 = (bf16[128,2048]{1,0:T(8,128)(2,1)S(1)}, bf16[128,2048]{1,0:T(8,128)(2,1)S(1)}, u32[]{:S(2)}, u32[]{:S(2)}) collective-permute-start(bf16[128,2048]{1,0:T(8,128)(2,1)S(1)} %collective-permute-done.15), channel_id=1, source_target_pairs={{0,4},{1,5},{2,6},{3,7},{4,0},{5,1},{6,2},{7,3},{8,12},{9,13},{10,... | collective-permute-start | bytes 1572872 | tf_op jit(solution)/shard_map/ppermute | solution.py:49
  123.1 25.9 %collective-permute-start.23 = (bf16[128,2048]{1,0:T(8,128)(2,1)S(1)}, bf16[128,2048]{1,0:T(8,128)(2,1)S(1)}, u32[]{:S(2)}, u32[]{:S(2)}) collective-permute-start(bf16[128,2048]{1,0:T(8,128)(2,1)S(1)} %collective-permute-done.15), channel_id=1, source_target_pairs={{0,1},{1,0},{2,3},{3,2},{4,5},{5,4},{6,7},{7,6},{8,9},{9,8},{10,11... | collective-permute-start | bytes 1572872 | tf_op jit(solution)/shard_map/ppermute | solution.py:49
  153.8 25.5 %collective-permute-start.25 = (bf16[512,1024]{1,0:T(8,128)(2,1)}, bf16[512,1024]{1,0:T(8,128)(2,1)}, u32[]{:S(2)}, u32[]{:S(2)}) collective-permute-start(bf16[512,1024]{1,0:T(8,128)(2,1)} %constant_dynamic-slice_fusion.5), channel_id=1, source_target_pairs={{0,3},{1,2},{2,1},{3,0},{4,7},{5,6},{6,5},{7,4},{8,11},{9,10},{10,... | collective-permute-start | bytes 3145736 | tf_op jit(solution)/shard_map/ppermute | solution.py:783
  193.2 32.8 %collective-permute-start.29 = (bf16[2,128,1024]{2,1,0:T(8,128)(2,1)S(1)}, bf16[2,128,1024]{2,1,0:T(8,128)(2,1)S(1)}, u32[]{:S(2)}, u32[]{:S(2)}) collective-permute-start(bf16[2,128,1024]{2,1,0:T(8,128)(2,1)S(1)} %slice.577), channel_id=1, source_target_pairs={{0,2},{1,3},{2,0},{3,1},{4,6},{5,7},{6,4},{7,5},{8,10},{9,11},{10,... | collective-permute-start | bytes 1572872 | tf_op jit(solution)/shard_map/ppermute | solution.py:49
  280.7 26.4 %collective-permute-start.42 = (bf16[512,1024]{1,0:T(8,128)(2,1)S(1)}, bf16[512,1024]{1,0:T(8,128)(2,1)S(1)}, u32[]{:S(2)}, u32[]{:S(2)}) collective-permute-start(bf16[512,1024]{1,0:T(8,128)(2,1)S(1)} %mix.18), channel_id=1, source_target_pairs={{0,8},{24,16},{1,9},{25,17},{2,10},{26,18},{3,11},{27,19},{4,12},{... | collective-permute-start | bytes 3145736 | tf_op jit(solution)/shard_map/ppermute | solution.py:271
  315.3 39.5 %collective-permute-start.68 = (bf16[512,1024]{1,0:T(8,128)(2,1)S(1)}, bf16[512,1024]{1,0:T(8,128)(2,1)}, u32[]{:S(2)}, u32[]{:S(2)}) collective-permute-start(bf16[512,1024]{1,0:T(8,128)(2,1)S(1)} %get-tuple-element.278.refs_3_), channel_id=1, source_target_pairs={{8,16},{16,8},{9,17},{17,9},{10,18},{18,10},{11,19},{19,11},{12,20... | collective-permute-start | bytes 3145736 | tf_op jit(solution)/shard_map/ppermute | solution.py:273
  317.0 37.8 %collective-permute-start.67 = (bf16[512,1024]{1,0:T(8,128)(2,1)}, bf16[512,1024]{1,0:T(8,128)(2,1)}, u32[]{:S(2)}, u32[]{:S(2)}) collective-permute-start(bf16[512,1024]{1,0:T(8,128)(2,1)} %get-tuple-element.319), channel_id=1, source_target_pairs={{0,8},{24,16},{1,9},{25,17},{2,10},{26,18},{3,11},{27,19},{4,12},{... | collective-permute-start | bytes 3145736 | tf_op jit(solution)/shard_map/ppermute | solution.py:271
  350.3 42.9 %all-to-all-start.2 = ((bf16[4,256,1024]{2,1,0:T(8,128)(2,1)}), bf16[4,256,1024]{2,1,0:T(8,128)(2,1)}, u32[]{:S(2)}, u32[]{:S(2)}) async-start(bf16[4,256,1024]{2,1,0:T(8,128)(2,1)} %slice.718), calls=%async_computation.2 | async-start | bytes 4194304 | tf_op jit(solution)/shard_map/all_to_all | solution.py:947
  358.6 25.6 %collective-permute-start.69 = (bf16[512,1024]{1,0:T(8,128)(2,1)S(1)}, bf16[512,1024]{1,0:T(8,128)(2,1)S(1)}, u32[]{:S(2)}, u32[]{:S(2)}) collective-permute-start(bf16[512,1024]{1,0:T(8,128)(2,1)S(1)} %get-tuple-element.322.refs_5_), channel_id=1, source_target_pairs={{0,8},{24,16},{8,0},{16,24},{1,9},{25,17},{9,1},{17,25},{2,10},{26... | collective-permute-start | bytes 3145736 | tf_op jit(solution)/shard_map/ppermute | solution.py:271
  358.7 27.1 %collective-permute-start.70 = (bf16[512,1024]{1,0:T(8,128)(2,1)S(1)}, bf16[512,1024]{1,0:T(8,128)(2,1)S(1)}, u32[]{:S(2)}, u32[]{:S(2)}) collective-permute-start(bf16[512,1024]{1,0:T(8,128)(2,1)S(1)} %get-tuple-element.323.refs_3_), channel_id=1, source_target_pairs={{8,16},{16,8},{9,17},{17,9},{10,18},{18,10},{11,19},{19,11},{12,20... | collective-permute-start | bytes 3145736 | tf_op jit(solution)/shard_map/ppermute | solution.py:273
  361.3 28.8 %collective-permute-start.51 = (bf16[128,1024]{1,0:T(8,128)(2,1)S(1)}, bf16[128,1024]{1,0:T(8,128)(2,1)S(1)}, u32[]{:S(2)}, u32[]{:S(2)}) collective-permute-start(bf16[128,1024]{1,0:T(8,128)(2,1)S(1)} %fusion.52), channel_id=1, source_target_pairs={{0,2},{1,3},{2,0},{3,1},{4,6},{5,7},{6,4},{7,5},{8,10},{9,11},{10,... | collective-permute-start | bytes 786440 | tf_op jit(solution)/shard_map/ppermute | solution.py:49
  364.4 27.3 %collective-permute-start.52 = (bf16[128,1024]{1,0:T(8,128)(2,1)S(1)}, bf16[128,1024]{1,0:T(8,128)(2,1)}, u32[]{:S(2)}, u32[]{:S(2)}) collective-permute-start(bf16[128,1024]{1,0:T(8,128)(2,1)S(1)} %fusion.53), channel_id=1, source_target_pairs={{0,4},{1,5},{2,6},{3,7},{4,0},{5,1},{6,2},{7,3},{8,12},{9,13},{10,... | collective-permute-start | bytes 786440 | tf_op jit(solution)/shard_map/ppermute | solution.py:49
  374.0 31.0 %collective-permute-start.47 = (bf16[2,128,1024]{2,1,0:T(8,128)(2,1)}, bf16[2,128,1024]{2,1,0:T(8,128)(2,1)}, u32[]{:S(2)}, u32[]{:S(2)}) collective-permute-start(bf16[2,128,1024]{2,1,0:T(8,128)(2,1)} %slice.1036), channel_id=1, source_target_pairs={{0,4},{1,5},{2,6},{3,7},{4,0},{5,1},{6,2},{7,3},{8,12},{9,13},{10,... | collective-permute-start | bytes 1572872 | tf_op jit(solution)/shard_map/ppermute | solution.py:49
  391.7 26.4 %collective-permute-start.73 = (bf16[512,1024]{1,0:T(8,128)(2,1)}, bf16[512,1024]{1,0:T(8,128)(2,1)}, u32[]{:S(2)}, u32[]{:S(2)}) collective-permute-start(bf16[512,1024]{1,0:T(8,128)(2,1)} %get-tuple-element.328.refs_0_), channel_id=1, source_target_pairs={{0,4},{4,0},{1,5},{5,1},{2,6},{6,2},{3,7},{7,3},{8,12},{12,8},{9,1... | collective-permute-start | bytes 3145736 | tf_op jit(solution)/shard_map/ppermute | solution.py:276
  396.3 78.4 %all-to-all-start.3 = ((bf16[4,256,1024]{2,1,0:T(8,128)(2,1)}), bf16[4,256,1024]{2,1,0:T(8,128)(2,1)}, u32[]{:S(2)}, u32[]{:S(2)}) async-start(bf16[4,256,1024]{2,1,0:T(8,128)(2,1)} %slice.613), calls=%async_computation.3 | async-start | bytes 4194304 | tf_op jit(solution)/shard_map/all_to_all | solution.py:947
  423.2 26.4 %collective-permute-start.75 = (bf16[512,1024]{1,0:T(8,128)(2,1)}, bf16[512,1024]{1,0:T(8,128)(2,1)}, u32[]{:S(2)}, u32[]{:S(2)}) collective-permute-start(bf16[512,1024]{1,0:T(8,128)(2,1)} %get-tuple-element.332.refs_3_), channel_id=1, source_target_pairs={{8,16},{16,8},{9,17},{17,9},{10,18},{18,10},{11,19},{19,11},{12,20... | collective-permute-start | bytes 3145736 | tf_op jit(solution)/shard_map/ppermute | solution.py:273
  424.9 26.2 %collective-permute-start.76 = (bf16[512,1024]{1,0:T(8,128)(2,1)S(1)}, bf16[512,1024]{1,0:T(8,128)(2,1)}, u32[]{:S(2)}, u32[]{:S(2)}) collective-permute-start(bf16[512,1024]{1,0:T(8,128)(2,1)S(1)} %get-tuple-element.333.refs_0_), channel_id=1, source_target_pairs={{0,4},{4,0},{1,5},{5,1},{2,6},{6,2},{3,7},{7,3},{8,12},{12,8},{9,1... | collective-permute-start | bytes 3145736 | tf_op jit(solution)/shard_map/ppermute | solution.py:276
  433.9 26.9 %collective-permute-start.53 = (bf16[128,2048]{1,0:T(8,128)(2,1)}, bf16[128,2048]{1,0:T(8,128)(2,1)}, u32[]{:S(2)}, u32[]{:S(2)}) collective-permute-start(bf16[128,2048]{1,0:T(8,128)(2,1)} %get-tuple-element.445), channel_id=1, source_target_pairs={{0,2},{1,3},{2,0},{3,1},{4,6},{5,7},{6,4},{7,5},{8,10},{9,11},{10,... | collective-permute-start | bytes 1572872 | tf_op jit(solution)/shard_map/ppermute | solution.py:49
  434.3 26.5 %collective-permute-start.54 = (bf16[128,2048]{1,0:T(8,128)(2,1)}, bf16[128,2048]{1,0:T(8,128)(2,1)}, u32[]{:S(2)}, u32[]{:S(2)}) collective-permute-start(bf16[128,2048]{1,0:T(8,128)(2,1)} %get-tuple-element.445), channel_id=1, source_target_pairs={{0,4},{1,5},{2,6},{3,7},{4,0},{5,1},{6,2},{7,3},{8,12},{9,13},{10,... | collective-permute-start | bytes 1572872 | tf_op jit(solution)/shard_map/ppermute | solution.py:49
  455.1 40.6 %collective-permute-start.77 = (bf16[512,1024]{1,0:T(8,128)(2,1)}, bf16[512,1024]{1,0:T(8,128)(2,1)}, u32[]{:S(2)}, u32[]{:S(2)}) collective-permute-start(bf16[512,1024]{1,0:T(8,128)(2,1)} %get-tuple-element.337.refs_5_), channel_id=1, source_target_pairs={{0,8},{24,16},{8,0},{16,24},{1,9},{25,17},{9,1},{17,25},{2,10},{26... | collective-permute-start | bytes 3145736 | tf_op jit(solution)/shard_map/ppermute | solution.py:271
  487.2 27.6 %all-to-all-start.4 = ((bf16[4,64,1024]{2,1,0:T(8,128)(2,1)}), bf16[4,64,1024]{2,1,0:T(8,128)(2,1)S(1)}, u32[]{:S(2)}, u32[]{:S(2)}) async-start(bf16[4,64,1024]{2,1,0:T(8,128)(2,1)} %bitcast.377), calls=%async_computation.4 | async-start | bytes 1048576 | tf_op jit(solution)/shard_map/all_to_all | solution.py:961
  502.7 28.2 %collective-permute-start.80 = (bf16[512,1024]{1,0:T(8,128)(2,1)}, bf16[512,1024]{1,0:T(8,128)(2,1)}, u32[]{:S(2)}, u32[]{:S(2)}) collective-permute-start(bf16[512,1024]{1,0:T(8,128)(2,1)} %get-tuple-element.344.refs_5_), channel_id=1, source_target_pairs={{0,8},{24,16},{8,0},{16,24},{1,9},{25,17},{9,1},{17,25},{2,10},{26... | collective-permute-start | bytes 3145736 | tf_op jit(solution)/shard_map/ppermute | solution.py:271
  515.6 36.1 %all-to-all-start.5 = ((bf16[4,256,1024]{2,1,0:T(8,128)(2,1)}), bf16[4,256,1024]{2,1,0:T(8,128)(2,1)S(1)}, u32[]{:S(2)}, u32[]{:S(2)}) async-start(bf16[4,256,1024]{2,1,0:T(8,128)(2,1)} %slice.614), calls=%async_computation.5 | async-start | bytes 4194304 | tf_op jit(solution)/shard_map/all_to_all | solution.py:947
  555.6 50.6 %all-to-all-start.6 = ((bf16[4,256,1024]{2,1,0:T(8,128)(2,1)}), bf16[4,256,1024]{2,1,0:T(8,128)(2,1)S(1)}, u32[]{:S(2)}, u32[]{:S(2)}) async-start(bf16[4,256,1024]{2,1,0:T(8,128)(2,1)} %slice.615), calls=%async_computation.6 | async-start | bytes 4194304 | tf_op jit(solution)/shard_map/all_to_all | solution.py:947
  569.3 48.4 %collective-permute-start.86 = (bf16[512,1024]{1,0:T(8,128)(2,1)}, bf16[512,1024]{1,0:T(8,128)(2,1)}, u32[]{:S(2)}, u32[]{:S(2)}) collective-permute-start(bf16[512,1024]{1,0:T(8,128)(2,1)} %get-tuple-element.358.refs_5_), channel_id=1, source_target_pairs={{0,8},{24,16},{8,0},{16,24},{1,9},{25,17},{9,1},{17,25},{2,10},{26... | collective-permute-start | bytes 3145736 | tf_op jit(solution)/shard_map/ppermute | solution.py:271
  571.2 46.4 %collective-permute-start.87 = (bf16[512,1024]{1,0:T(8,128)(2,1)}, bf16[512,1024]{1,0:T(8,128)(2,1)}, u32[]{:S(2)}, u32[]{:S(2)}) collective-permute-start(bf16[512,1024]{1,0:T(8,128)(2,1)} %get-tuple-element.359.refs_3_), channel_id=1, source_target_pairs={{8,16},{16,8},{9,17},{17,9},{10,18},{18,10},{11,19},{19,11},{12,20... | collective-permute-start | bytes 3145736 | tf_op jit(solution)/shard_map/ppermute | solution.py:273
  572.9 44.8 %collective-permute-start.88 = (bf16[512,1024]{1,0:T(8,128)(2,1)}, bf16[512,1024]{1,0:T(8,128)(2,1)}, u32[]{:S(2)}, u32[]{:S(2)}) collective-permute-start(bf16[512,1024]{1,0:T(8,128)(2,1)} %get-tuple-element.360), channel_id=1, source_target_pairs={{0,4},{4,0},{1,5},{5,1},{2,6},{6,2},{3,7},{7,3},{8,12},{12,8},{9,1... | collective-permute-start | bytes 3145736 | tf_op jit(solution)/shard_map/ppermute | solution.py:276
  608.4 28.8 %all-to-all-start.7 = ((bf16[4,128,1024]{2,1,0:T(8,128)(2,1)}), bf16[4,128,1024]{2,1,0:T(8,128)(2,1)}, u32[]{:S(2)}, u32[]{:S(2)}) async-start(bf16[4,128,1024]{2,1,0:T(8,128)(2,1)} %slice.617), calls=%async_computation.7 | async-start | bytes 2097152 | tf_op jit(solution)/shard_map/all_to_all | solution.py:881
  621.7 32.6 %collective-permute-start.89 = (bf16[512,1024]{1,0:T(8,128)(2,1)}, bf16[512,1024]{1,0:T(8,128)(2,1)}, u32[]{:S(2)}, u32[]{:S(2)}) collective-permute-start(bf16[512,1024]{1,0:T(8,128)(2,1)} %get-tuple-element.364.refs_5_), channel_id=1, source_target_pairs={{0,8},{24,16},{8,0},{16,24},{1,9},{25,17},{9,1},{17,25},{2,10},{26... | collective-permute-start | bytes 3145736 | tf_op jit(solution)/shard_map/ppermute | solution.py:271
  624.2 30.2 %collective-permute-start.90 = (bf16[512,1024]{1,0:T(8,128)(2,1)}, bf16[512,1024]{1,0:T(8,128)(2,1)}, u32[]{:S(2)}, u32[]{:S(2)}) collective-permute-start(bf16[512,1024]{1,0:T(8,128)(2,1)} %get-tuple-element.365.refs_3_), channel_id=1, source_target_pairs={{8,16},{16,8},{9,17},{17,9},{10,18},{18,10},{11,19},{19,11},{12,20... | collective-permute-start | bytes 3145736 | tf_op jit(solution)/shard_map/ppermute | solution.py:273
  625.8 28.5 %collective-permute-start.91 = (bf16[512,1024]{1,0:T(8,128)(2,1)}, bf16[512,1024]{1,0:T(8,128)(2,1)}, u32[]{:S(2)}, u32[]{:S(2)}) collective-permute-start(bf16[512,1024]{1,0:T(8,128)(2,1)} %get-tuple-element.366), channel_id=1, source_target_pairs={{0,4},{4,0},{1,5},{5,1},{2,6},{6,2},{3,7},{7,3},{8,12},{12,8},{9,1... | collective-permute-start | bytes 3145736 | tf_op jit(solution)/shard_map/ppermute | solution.py:276
  637.2 40.1 %all-to-all-start.8 = ((bf16[4,64,1024]{2,1,0:T(8,128)(2,1)}), bf16[4,64,1024]{2,1,0:T(8,128)(2,1)}, u32[]{:S(2)}, u32[]{:S(2)}) async-start(bf16[4,64,1024]{2,1,0:T(8,128)(2,1)} %slice.616), calls=%async_computation.8 | async-start | bytes 1048576 | tf_op jit(solution)/shard_map/all_to_all | solution.py:881
  658.3 34.5 %collective-permute-start.92 = (bf16[512,1024]{1,0:T(8,128)(2,1)}, bf16[512,1024]{1,0:T(8,128)(2,1)}, u32[]{:S(2)}, u32[]{:S(2)}) collective-permute-start(bf16[512,1024]{1,0:T(8,128)(2,1)} %get-tuple-element.371.refs_5_), channel_id=1, source_target_pairs={{0,8},{24,16},{8,0},{16,24},{1,9},{25,17},{9,1},{17,25},{2,10},{26... | collective-permute-start | bytes 3145736 | tf_op jit(solution)/shard_map/ppermute | solution.py:271
  683.6 49.8 %all-to-all-start.9 = ((bf16[4,512,384]{2,1,0:T(8,128)(2,1)}), bf16[4,512,384]{2,1,0:T(8,128)(2,1)}, u32[]{:S(2)}, u32[]{:S(2)}) async-start(bf16[4,512,384]{2,1,0:T(8,128)(2,1)} %bitcast.376), calls=%async_computation.9 | async-start | bytes 3145728 | tf_op jit(solution)/shard_map/all_to_all | solution.py:947
  707.0 54.2 %collective-permute-start.62 = (bf16[512,2048]{1,0:T(8,128)(2,1)}, bf16[512,2048]{1,0:T(8,128)(2,1)}, u32[]{:S(2)}, u32[]{:S(2)}) collective-permute-start(bf16[512,2048]{1,0:T(8,128)(2,1)} %convolution_convert_fusion.4), channel_id=1, source_target_pairs={{0,1},{1,0},{2,3},{3,2},{4,5},{5,4},{6,7},{7,6},{8,9},{9,8},{10,11... | collective-permute-start | bytes 6291464 | tf_op jit(solution)/shard_map/ppermute | solution.py:49
  755.5 37.6 %collective-permute-start.101 = (bf16[512,1024]{1,0:T(8,128)(2,1)S(1)}, bf16[512,1024]{1,0:T(8,128)(2,1)S(1)}, u32[]{:S(2)}, u32[]{:S(2)}) collective-permute-start(bf16[512,1024]{1,0:T(8,128)(2,1)S(1)} %get-tuple-element.391.refs_5_), channel_id=1, source_target_pairs={{0,8},{24,16},{8,0},{16,24},{1,9},{25,17},{9,1},{17,25},{2,10},{26... | collective-permute-start | bytes 3145736 | tf_op jit(solution)/shard_map/ppermute | solution.py:271
  758.6 34.5 %collective-permute-start.102 = (bf16[512,1024]{1,0:T(8,128)(2,1)S(1)}, bf16[512,1024]{1,0:T(8,128)(2,1)S(1)}, u32[]{:S(2)}, u32[]{:S(2)}) collective-permute-start(bf16[512,1024]{1,0:T(8,128)(2,1)S(1)} %get-tuple-element.392.refs_3_), channel_id=1, source_target_pairs={{8,16},{16,8},{9,17},{17,9},{10,18},{18,10},{11,19},{19,11},{12,20... | collective-permute-start | bytes 3145736 | tf_op jit(solution)/shard_map/ppermute | solution.py:273
  759.3 33.7 %collective-permute-start.103 = (bf16[512,1024]{1,0:T(8,128)(2,1)S(1)}, bf16[512,1024]{1,0:T(8,128)(2,1)S(1)}, u32[]{:S(2)}, u32[]{:S(2)}) collective-permute-start(bf16[512,1024]{1,0:T(8,128)(2,1)S(1)} %get-tuple-element.393), channel_id=1, source_target_pairs={{0,4},{4,0},{1,5},{5,1},{2,6},{6,2},{3,7},{7,3},{8,12},{12,8},{9,1... | collective-permute-start | bytes 3145736 | tf_op jit(solution)/shard_map/ppermute | solution.py:276
  763.9 29.2 %collective-permute-start.63 = (bf16[2,128,1024]{2,1,0:T(8,128)(2,1)S(1)}, bf16[2,128,1024]{2,1,0:T(8,128)(2,1)S(1)}, u32[]{:S(2)}, u32[]{:S(2)}) collective-permute-start(bf16[2,128,1024]{2,1,0:T(8,128)(2,1)S(1)} %slice.1035), channel_id=1, source_target_pairs={{0,4},{1,5},{2,6},{3,7},{4,0},{5,1},{6,2},{7,3},{8,12},{9,13},{10,... | collective-permute-start | bytes 1572872 | tf_op jit(solution)/shard_map/ppermute | solution.py:49
  764.3 28.8 %collective-permute-start.64 = (bf16[2,128,1024]{2,1,0:T(8,128)(2,1)S(1)}, bf16[2,128,1024]{2,1,0:T(8,128)(2,1)S(1)}, u32[]{:S(2)}, u32[]{:S(2)}) collective-permute-start(bf16[2,128,1024]{2,1,0:T(8,128)(2,1)S(1)} %slice.628), channel_id=1, source_target_pairs={{0,2},{1,3},{2,0},{3,1},{4,6},{5,7},{6,4},{7,5},{8,10},{9,11},{10,... | collective-permute-start | bytes 1572872 | tf_op jit(solution)/shard_map/ppermute | solution.py:49
  797.3 26.2 %collective-permute-start.106 = (bf16[512,1024]{1,0:T(8,128)(2,1)S(1)}, bf16[512,1024]{1,0:T(8,128)(2,1)S(1)}, u32[]{:S(2)}, u32[]{:S(2)}) collective-permute-start(bf16[512,1024]{1,0:T(8,128)(2,1)S(1)} %get-tuple-element.400), channel_id=1, source_target_pairs={{0,4},{4,0},{1,5},{5,1},{2,6},{6,2},{3,7},{7,3},{8,12},{12,8},{9,1... | collective-permute-start | bytes 3145736 | tf_op jit(solution)/shard_map/ppermute | solution.py:276
  799.3 26.2 %collective-permute-start.65 = (bf16[128,1024]{1,0:T(8,128)(2,1)S(1)}, bf16[128,1024]{1,0:T(8,128)(2,1)S(1)}, u32[]{:S(2)}, u32[]{:S(2)}) collective-permute-start(bf16[128,1024]{1,0:T(8,128)(2,1)S(1)} %fusion.54), channel_id=1, source_target_pairs={{0,2},{1,3},{2,0},{3,1},{4,6},{5,7},{6,4},{7,5},{8,10},{9,11},{10,... | collective-permute-start | bytes 786440 | tf_op jit(solution)/shard_map/ppermute | solution.py:49
  799.6 29.5 %collective-permute-start.66 = (bf16[128,1024]{1,0:T(8,128)(2,1)S(1)}, bf16[128,1024]{1,0:T(8,128)(2,1)S(1)}, u32[]{:S(2)}, u32[]{:S(2)}) collective-permute-start(bf16[128,1024]{1,0:T(8,128)(2,1)S(1)} %fusion.55), channel_id=1, source_target_pairs={{0,4},{1,5},{2,6},{3,7},{4,0},{5,1},{6,2},{7,3},{8,12},{9,13},{10,... | collective-permute-start | bytes 786440 | tf_op jit(solution)/shard_map/ppermute | solution.py:49
  823.6 28.7 %collective-permute-start.109 = (bf16[512,1024]{1,0:T(8,128)(2,1)S(1)}, bf16[512,1024]{1,0:T(8,128)(2,1)S(1)}, u32[]{:S(2)}, u32[]{:S(2)}) collective-permute-start(bf16[512,1024]{1,0:T(8,128)(2,1)S(1)} %get-tuple-element.407.refs_0_), channel_id=1, source_target_pairs={{0,4},{4,0},{1,5},{5,1},{2,6},{6,2},{3,7},{7,3},{8,12},{12,8},{9,1... | collective-permute-start | bytes 3145736 | tf_op jit(solution)/shard_map/ppermute | solution.py:276
  (173 other events, 2483.7 us)

commit v6 on v5

--- a/solution.py
+++ b/solution.py
@@ -991,11 +991,9 @@
         gate1 = to_shards(gate_now[:, half_rows:])
         yield []
         (box["gate1"],) = yield [gate1]
+        up_all = to_shards(after(up_partial, *box["now"]))
         yield []
-        up_now = after(up_partial, *box["now"])
-        (box["up0"],) = yield [to_shards(up_now[:, :half_rows])]
-        up_now = after(up_partial, *box["now"])
-        (box["up1"],) = yield [to_shards(up_now[:, half_rows:])]
+        (box["up"],) = yield [up_all]
         return None
 
     def feed_forward_out(last):
@@ -1033,6 +1031,8 @@
         each = shards // steps
 
         def source():
+            if name in box:
+                return box[name], (each, size, units), lambda i: (i, c, 0)
             return (
                 box[name + str(c // 2)],
                 (each, size, units),

time: 915 us -> 947 us (1.035)
  waiting for transfers between devices: 301 us -> 333 us
  starting transfers between devices: 197 us -> 210 us
  Pallas kernels: 162 us -> 150 us
    ppermute x61, waiting for transfers between devices: 106 us -> 129 us  [swap(): return lax.ppermute(value, SLAB, [(i, i ^ flip) for i in range(KVH)])]
    ppermute x17, waiting for transfers between devices: 81.2 us -> 101 us  [stream(): moves['got'] = lax.ppermute(sending, 'line', pairs)]
    ppermute x61, starting transfers between devices: 40 us -> 52.7 us  [swap(): return lax.ppermute(value, SLAB, [(i, i ^ flip) for i in range(KVH)])]
    unnamed x183 -> x169, local copies, waits for them, and re-layouts: 22.4 us -> 25.6 us
    all_to_all x5 -> x4, starting transfers between devices: 20.5 us -> 18.1 us  [to_shards(): return lax.all_to_all(partial, 'wshard', 0, 0, tiled=True)]
  transfers between devices with their start and end apart: 133 -> 132, of which waited for: 48 -> 48; matrix products, arithmetic and copies ran while one was open for 20% -> 18% of each run, Pallas kernels for 17% -> 15%
where the time goes in v6:
time: 947 us; the launch traced here: 934 us
  waiting for transfers between devices  333 us (35%)
  starting transfers between devices  210 us (22%)
  Pallas kernels  150 us (16%)
  local copies, waits for them, and re-layouts  114 us (12%)
  matrix products  81 us (9%)
  other arithmetic  43.1 us (5%)
    ppermute x61, waiting for transfers between devices, swap(): return lax.ppermute(value, SLAB, [(i, i ^ flip) for i in range(KVH)])  129 us
    ppermute x17, waiting for transfers between devices, stream(): moves['got'] = lax.ppermute(sending, 'line', pairs)  101 us
    dot_general x17, matrix products, contract(): lax.dot_general(left, right, (((left_dim,), (right_dim,)), ((), ())), pre...  81 us
    ppermute x17, starting transfers between devices, stream(): moves['got'] = lax.ppermute(sending, 'line', pairs)  63.8 us
    ppermute x61, starting transfers between devices, swap(): return lax.ppermute(value, SLAB, [(i, i ^ flip) for i in range(KVH)])  52.7 us
    ppermute x12, waiting for transfers between devices, pass_on(): return lax.ppermute(block, 'wshard', [(i, i ^ flip) for i in range(shards)])  50 us
    dynamic_update_slice x38, local copies, waits for them, and re-layouts, put(): lax.dynamic_update_slice(total, piece, (index * half,) + (0,) * (block.nd...  42.8 us
    pallas_call x18, Pallas kernels, mix(): pl.pallas_call(functools.partial(mix_kernel, tuple(names) + tuple(results...  38.9 us
  transfers between devices with their start and end apart: 132, of which 48 were waited for; matrix products, arithmetic and copies ran while one was open for 18% of the time, Pallas kernels for 15%

profile of v6, /device:TPU:0, one launch (start us, length us, event | category | flops | bytes accessed | tf_op | source)
XLA Modules:
  0.0 934.3 jit_solution(8673860347625763343)
XLA Ops:
  42.0 7.1 collective-permute-done.8
  54.4 9.3 collective-permute-done.14
  74.0 5.0 all-to-all-start
  79.6 13.2 %collective-permute-done.15 = bf16[128,2048]{1,0:T(8,128)(2,1)S(1)} collective-permute-done((bf16[128,2048]{1,0:T(8,128)(2,1)S(1)}, bf16[128,2048]{1,0:T(8,128)(2,1)S(1)}, u32[]{:S(2)}, u32[]{:S(2)}) %collective-permute-start.15) | collective-permute-done | bytes 524320 | tf_op jit(solution)/shard_map/ppermute | solution.py:49
  101.5 8.9 collective-permute-done.18
  110.4 11.2 %collective-permute-done.17 = bf16[512,1024]{1,0:T(8,128)(2,1)} collective-permute-done((bf16[512,1024]{1,0:T(8,128)(2,1)}, bf16[512,1024]{1,0:T(8,128)(2,1)}, u32[]{:S(2)}, u32[]{:S(2)}) %collective-permute-start.17) | collective-permute-done | bytes 1048608 | tf_op jit(solution)/shard_map/ppermute | solution.py:783
  125.9 22.6 %attend_forward.1 = (bf16[4,64,1024]{2,1,0:T(8,128)(2,1)}, bf16[192,4096]{1,0:T(8,128)(2,1)}, f32[64,4096]{1,0:T(8,128)}, f32[1,4096]{1,0:T(1,128)}) custom-call(s32[64]{0:T(128)} %select_reduce_fusion.sort_ref, s32[64]{0:T(128)} %copy-done.75, s32[2]{0:T(128)} %pad_add_fusion.range_ref, bf16[4,192,1024]{2,1,0:T(8,128)(2,1)} %all-to-all-done.blocks_ref), custom_call_target="tpu_custom_call" | custom-call | flops 30000001024 | bytes 8000000 | tf_op jit(solution)/shard_map/attend_forward/pallas_call | solution.py:673
  157.1 4.8 all-to-all-start.1
  169.5 7.1 all-to-all-done.1
  195.8 18.6 %collective-permute-done.30 = bf16[512,1024]{1,0:T(8,128)(2,1)S(1)} collective-permute-done((bf16[512,1024]{1,0:T(8,128)(2,1)S(1)}, bf16[512,1024]{1,0:T(8,128)(2,1)S(1)}, u32[]{:S(2)}, u32[]{:S(2)}) %collective-permute-start.30) | collective-permute-done | bytes 1048608 | tf_op jit(solution)/shard_map/ppermute | solution.py:783
  214.4 11.6 %collective-permute-done.29 = bf16[2,128,1024]{2,1,0:T(8,128)(2,1)S(1)} collective-permute-done((bf16[2,128,1024]{2,1,0:T(8,128)(2,1)S(1)}, bf16[2,128,1024]{2,1,0:T(8,128)(2,1)S(1)}, u32[]{:S(2)}, u32[]{:S(2)}) %collective-permute-start.29) | collective-permute-done | bytes 524320 | tf_op jit(solution)/shard_map/ppermute | solution.py:49
  228.4 6.8 fusion.7
  241.7 8.9 collective-permute-done.33
  260.2 8.8 fusion.89
  272.9 7.4 convolution_convert_fusion.1.refs_0_.refs_1_
  286.7 6.6 convolution_convert_fusion.2
  293.3 13.6 %collective-permute-done.42.refs_2_ = bf16[512,1024]{1,0:T(8,128)(2,1)S(1)} collective-permute-done((bf16[512,1024]{1,0:T(8,128)(2,1)S(1)}, bf16[512,1024]{1,0:T(8,128)(2,1)S(1)}, u32[]{:S(2)}, u32[]{:S(2)}) %collective-permute-start.42) | collective-permute-done | bytes 1048608 | tf_op jit(solution)/shard_map/ppermute | solution.py:271
  309.9 5.7 convolution_convert_fusion.5
  320.0 6.1 convert_add_fusion.2
  329.8 6.4 convolution_convert_fusion
  351.5 7.0 collective-permute-start.67
  376.7 4.9 collective-permute-done.67.refs_2_
  408.1 19.9 %collective-permute-done.49 = bf16[128,1024]{1,0:T(8,128)(2,1)S(1)} collective-permute-done((bf16[128,1024]{1,0:T(8,128)(2,1)S(1)}, bf16[128,1024]{1,0:T(8,128)(2,1)S(1)}, u32[]{:S(2)}, u32[]{:S(2)}) %collective-permute-start.49) | collective-permute-done | bytes 262176 | tf_op jit(solution)/shard_map/ppermute | solution.py:49
  475.4 5.5 collective-permute-done.73.refs_1_
  486.7 9.0 collective-permute-start.74
  498.8 4.9 all-to-all-start.5
  503.8 5.1 place_blocks.5.refs_2_
  508.8 5.6 collective-permute-done.74.refs_2_
  526.0 4.9 place_blocks.6.refs_2_
  530.9 11.1 %collective-permute-done.77.refs_2_ = bf16[512,1024]{1,0:T(8,128)(2,1)S(1)} collective-permute-done((bf16[512,1024]{1,0:T(8,128)(2,1)S(1)}, bf16[512,1024]{1,0:T(8,128)(2,1)S(1)}, u32[]{:S(2)}, u32[]{:S(2)}) %collective-permute-start.77) | collective-permute-done | bytes 1048608 | tf_op jit(solution)/shard_map/ppermute | solution.py:271
  558.4 8.5 collective-permute-done.80.refs_2_
  579.1 33.0 %attend_backward.1 = bf16[4,192,1024]{2,1,0:T(8,128)(2,1)} custom-call(s32[64]{0:T(128)} %select_reduce_fusion.sort_ref, s32[64]{0:T(128)} %copy-done.75, s32[2]{0:T(128)} %pad_add_fusion.range_ref, bf16[192,4096]{1,0:T(8,128)(2,1)} %get-tuple-element.288.sorted_ref, f32[64,4096]{1,0:T(8,128)} %get-tuple-element.289.float_ref, ...), custom_call_target="tpu_custom_call" | custom-call | flops 35999997952 | bytes 8000000 | tf_op jit(solution)/shard_map/attend_backward/pallas_call | solution.py:699
  628.3 4.8 place_columns.8.refs_2_
  633.1 21.0 %collective-permute-done.86.refs_2_ = bf16[512,1024]{1,0:T(8,128)(2,1)S(1)} collective-permute-done((bf16[512,1024]{1,0:T(8,128)(2,1)S(1)}, bf16[512,1024]{1,0:T(8,128)(2,1)S(1)}, u32[]{:S(2)}, u32[]{:S(2)}) %collective-permute-start.86) | collective-permute-done | bytes 1048608 | tf_op jit(solution)/shard_map/ppermute | solution.py:271
  658.7 6.5 collective-permute-start.89
  682.5 6.0 collective-permute-done.89.refs_2_
  693.6 9.2 collective-permute-start.92
  707.1 4.8 convolution_convert_fusion.6
  738.0 4.6 place_columns.11
  746.2 8.8 collective-permute-done.95.refs_2_
  768.8 4.8 place_columns.12.refs_2_
  773.5 11.1 %collective-permute-done.98.refs_2_ = bf16[512,1024]{1,0:T(8,128)(2,1)S(1)} collective-permute-done((bf16[512,1024]{1,0:T(8,128)(2,1)S(1)}, bf16[512,1024]{1,0:T(8,128)(2,1)S(1)}, u32[]{:S(2)}, u32[]{:S(2)}) %collective-permute-start.98) | collective-permute-done | bytes 1048608 | tf_op jit(solution)/shard_map/ppermute | solution.py:271
  798.6 26.2 %collective-permute-done.63 = bf16[2,128,1024]{2,1,0:T(8,128)(2,1)S(1)} collective-permute-done((bf16[2,128,1024]{2,1,0:T(8,128)(2,1)S(1)}, bf16[2,128,1024]{2,1,0:T(8,128)(2,1)S(1)}, u32[]{:S(2)}, u32[]{:S(2)}) %collective-permute-start.63) | collective-permute-done | bytes 524320 | tf_op jit(solution)/shard_map/ppermute | solution.py:49
  839.3 10.6 %collective-permute-done.104.refs_1_ = bf16[512,1024]{1,0:T(8,128)(2,1)S(1)} collective-permute-done((bf16[512,1024]{1,0:T(8,128)(2,1)S(1)}, bf16[512,1024]{1,0:T(8,128)(2,1)S(1)}, u32[]{:S(2)}, u32[]{:S(2)}) %collective-permute-start.104) | collective-permute-done | bytes 1048608 | tf_op jit(solution)/shard_map/ppermute | solution.py:271
  849.9 6.6 collective-permute-done.106
  872.4 7.6 collective-permute-done.113
  902.4 9.1 collective-permute-done.121
  919.8 11.6 %collective-permute-done.122.refs_1_ = bf16[384,1024]{1,0:T(8,128)(2,1)S(1)} collective-permute-done((bf16[384,1024]{1,0:T(8,128)(2,1)S(1)}, bf16[384,1024]{1,0:T(8,128)(2,1)S(1)}, u32[]{:S(2)}, u32[]{:S(2)}) %collective-permute-start.122) | collective-permute-done | bytes 786464 | tf_op jit(solution)/shard_map/ppermute | solution.py:276
  (620 shorter events, 469.3 us)
Async XLA Ops:
  20.4 28.7 %collective-permute-start.6 = (bf16[128,2048]{1,0:T(8,128)(2,1)}, bf16[128,2048]{1,0:T(8,128)(2,1)S(1)}, u32[]{:S(2)}, u32[]{:S(2)}) collective-permute-start(bf16[128,2048]{1,0:T(8,128)(2,1)} %collective-permute-done), channel_id=1, source_target_pairs={{0,1},{1,0},{2,3},{3,2},{4,5},{5,4},{6,7},{7,6},{8,9},{9,8},{10,11... | collective-permute-start | bytes 1572872 | tf_op jit(solution)/shard_map/ppermute | solution.py:49
  22.4 26.7 %collective-permute-start.7 = (bf16[128,2048]{1,0:T(8,128)(2,1)}, bf16[128,2048]{1,0:T(8,128)(2,1)S(1)}, u32[]{:S(2)}, u32[]{:S(2)}) collective-permute-start(bf16[128,2048]{1,0:T(8,128)(2,1)} %collective-permute-done.1), channel_id=1, source_target_pairs={{0,1},{1,0},{2,3},{3,2},{4,5},{5,4},{6,7},{7,6},{8,9},{9,8},{10,11... | collective-permute-start | bytes 1572872 | tf_op jit(solution)/shard_map/ppermute | solution.py:49
  74.0 47.6 %all-to-all-start = ((bf16[4,192,1024]{2,1,0:T(8,128)(2,1)}), bf16[4,192,1024]{2,1,0:T(8,128)(2,1)}, u32[]{:S(2)}, u32[]{:S(2)}) async-start(bf16[4,192,1024]{2,1,0:T(8,128)(2,1)} %pad_maximum_fusion.1), calls=%async_computation | async-start | bytes 3145728 | tf_op jit(solution)/shard_map/all_to_all | solution.py:857
  95.8 25.9 %collective-permute-start.17 = (bf16[512,1024]{1,0:T(8,128)(2,1)}, bf16[512,1024]{1,0:T(8,128)(2,1)}, u32[]{:S(2)}, u32[]{:S(2)}) collective-permute-start(bf16[512,1024]{1,0:T(8,128)(2,1)} %get-tuple-element.450), channel_id=1, source_target_pairs={{0,2},{1,3},{2,0},{3,1},{4,6},{5,7},{6,4},{7,5},{8,10},{9,11},{10,... | collective-permute-start | bytes 3145736 | tf_op jit(solution)/shard_map/ppermute | solution.py:783
  121.6 27.7 %collective-permute-start.22 = (bf16[128,2048]{1,0:T(8,128)(2,1)S(1)}, bf16[128,2048]{1,0:T(8,128)(2,1)S(1)}, u32[]{:S(2)}, u32[]{:S(2)}) collective-permute-start(bf16[128,2048]{1,0:T(8,128)(2,1)S(1)} %collective-permute-done.15), channel_id=1, source_target_pairs={{0,4},{1,5},{2,6},{3,7},{4,0},{5,1},{6,2},{7,3},{8,12},{9,13},{10,... | collective-permute-start | bytes 1572872 | tf_op jit(solution)/shard_map/ppermute | solution.py:49
  123.1 26.2 %collective-permute-start.23 = (bf16[128,2048]{1,0:T(8,128)(2,1)S(1)}, bf16[128,2048]{1,0:T(8,128)(2,1)S(1)}, u32[]{:S(2)}, u32[]{:S(2)}) collective-permute-start(bf16[128,2048]{1,0:T(8,128)(2,1)S(1)} %collective-permute-done.15), channel_id=1, source_target_pairs={{0,1},{1,0},{2,3},{3,2},{4,5},{5,4},{6,7},{7,6},{8,9},{9,8},{10,11... | collective-permute-start | bytes 1572872 | tf_op jit(solution)/shard_map/ppermute | solution.py:49
  125.4 25.1 %collective-permute-start.21 = (bf16[512,1024]{1,0:T(8,128)(2,1)S(1)}, bf16[512,1024]{1,0:T(8,128)(2,1)S(1)}, u32[]{:S(2)}, u32[]{:S(2)}) collective-permute-start(bf16[512,1024]{1,0:T(8,128)(2,1)S(1)} %get-tuple-element.448), channel_id=1, source_target_pairs={{0,2},{1,3},{2,0},{3,1},{4,6},{5,7},{6,4},{7,5},{8,10},{9,11},{10,... | collective-permute-start | bytes 3145736 | tf_op jit(solution)/shard_map/ppermute | solution.py:783
  153.8 25.4 %collective-permute-start.25 = (bf16[512,1024]{1,0:T(8,128)(2,1)}, bf16[512,1024]{1,0:T(8,128)(2,1)}, u32[]{:S(2)}, u32[]{:S(2)}) collective-permute-start(bf16[512,1024]{1,0:T(8,128)(2,1)} %constant_dynamic-slice_fusion.5), channel_id=1, source_target_pairs={{0,3},{1,2},{2,1},{3,0},{4,7},{5,6},{6,5},{7,4},{8,11},{9,10},{10,... | collective-permute-start | bytes 3145736 | tf_op jit(solution)/shard_map/ppermute | solution.py:783
  189.2 25.2 %collective-permute-start.30 = (bf16[512,1024]{1,0:T(8,128)(2,1)S(1)}, bf16[512,1024]{1,0:T(8,128)(2,1)S(1)}, u32[]{:S(2)}, u32[]{:S(2)}) collective-permute-start(bf16[512,1024]{1,0:T(8,128)(2,1)S(1)} %constant_dynamic-slice_fusion.4), channel_id=1, source_target_pairs={{0,3},{1,2},{2,1},{3,0},{4,7},{5,6},{6,5},{7,4},{8,11},{9,10},{10,... | collective-permute-start | bytes 3145736 | tf_op jit(solution)/shard_map/ppermute | solution.py:783
  193.6 32.4 %collective-permute-start.29 = (bf16[2,128,1024]{2,1,0:T(8,128)(2,1)S(1)}, bf16[2,128,1024]{2,1,0:T(8,128)(2,1)S(1)}, u32[]{:S(2)}, u32[]{:S(2)}) collective-permute-start(bf16[2,128,1024]{2,1,0:T(8,128)(2,1)S(1)} %slice.571), channel_id=1, source_target_pairs={{0,2},{1,3},{2,0},{3,1},{4,6},{5,7},{6,4},{7,5},{8,10},{9,11},{10,... | collective-permute-start | bytes 1572872 | tf_op jit(solution)/shard_map/ppermute | solution.py:49
  280.6 26.4 %collective-permute-start.42 = (bf16[512,1024]{1,0:T(8,128)(2,1)S(1)}, bf16[512,1024]{1,0:T(8,128)(2,1)S(1)}, u32[]{:S(2)}, u32[]{:S(2)}) collective-permute-start(bf16[512,1024]{1,0:T(8,128)(2,1)S(1)} %mix.18), channel_id=1, source_target_pairs={{0,8},{24,16},{1,9},{25,17},{2,10},{26,18},{3,11},{27,19},{4,12},{... | collective-permute-start | bytes 3145736 | tf_op jit(solution)/shard_map/ppermute | solution.py:271
  344.6 27.1 %collective-permute-start.46 = (bf16[512,2048]{1,0:T(8,128)(2,1)}, bf16[512,2048]{1,0:T(8,128)(2,1)}, u32[]{:S(2)}, u32[]{:S(2)}) collective-permute-start(bf16[512,2048]{1,0:T(8,128)(2,1)} %fusion.9), channel_id=1, source_target_pairs={{0,1},{1,0},{2,3},{3,2},{4,5},{5,4},{6,7},{7,6},{8,9},{9,8},{10,11... | collective-permute-start | bytes 6291464 | tf_op jit(solution)/shard_map/ppermute | solution.py:49
  346.1 43.1 %all-to-all-start.2 = ((bf16[4,256,1024]{2,1,0:T(8,128)(2,1)}), bf16[4,256,1024]{2,1,0:T(8,128)(2,1)}, u32[]{:S(2)}, u32[]{:S(2)}) async-start(bf16[4,256,1024]{2,1,0:T(8,128)(2,1)} %slice.710), calls=%async_computation.2 | async-start | bytes 4194304 | tf_op jit(solution)/shard_map/all_to_all | solution.py:947
  350.7 32.5 %collective-permute-start.68 = (bf16[512,1024]{1,0:T(8,128)(2,1)S(1)}, bf16[512,1024]{1,0:T(8,128)(2,1)S(1)}, u32[]{:S(2)}, u32[]{:S(2)}) collective-permute-start(bf16[512,1024]{1,0:T(8,128)(2,1)S(1)} %get-tuple-element.276.refs_3_), channel_id=1, source_target_pairs={{8,16},{16,8},{9,17},{17,9},{10,18},{18,10},{11,19},{19,11},{12,20... | collective-permute-start | bytes 3145736 | tf_op jit(solution)/shard_map/ppermute | solution.py:273
  351.5 30.0 %collective-permute-start.67 = (bf16[512,1024]{1,0:T(8,128)(2,1)}, bf16[512,1024]{1,0:T(8,128)(2,1)S(1)}, u32[]{:S(2)}, u32[]{:S(2)}) collective-permute-start(bf16[512,1024]{1,0:T(8,128)(2,1)} %copy-done.16), channel_id=1, source_target_pairs={{0,8},{24,16},{1,9},{25,17},{2,10},{26,18},{3,11},{27,19},{4,12},{... | collective-permute-start | bytes 3145736 | tf_op jit(solution)/shard_map/ppermute | solution.py:271
  375.2 25.7 %collective-permute-start.47 = (bf16[2,128,1024]{2,1,0:T(8,128)(2,1)}, bf16[2,128,1024]{2,1,0:T(8,128)(2,1)}, u32[]{:S(2)}, u32[]{:S(2)}) collective-permute-start(bf16[2,128,1024]{2,1,0:T(8,128)(2,1)} %slice.1028), channel_id=1, source_target_pairs={{0,4},{1,5},{2,6},{3,7},{4,0},{5,1},{6,2},{7,3},{8,12},{9,13},{10,... | collective-permute-start | bytes 1572872 | tf_op jit(solution)/shard_map/ppermute | solution.py:49
  384.9 46.6 %collective-permute-start.69 = (bf16[512,1024]{1,0:T(8,128)(2,1)}, bf16[512,1024]{1,0:T(8,128)(2,1)}, u32[]{:S(2)}, u32[]{:S(2)}) collective-permute-start(bf16[512,1024]{1,0:T(8,128)(2,1)} %get-tuple-element.318.refs_5_), channel_id=1, source_target_pairs={{0,8},{24,16},{8,0},{16,24},{1,9},{25,17},{9,1},{17,25},{2,10},{26... | collective-permute-start | bytes 3145736 | tf_op jit(solution)/shard_map/ppermute | solution.py:271
  387.6 43.9 %collective-permute-start.70 = (bf16[512,1024]{1,0:T(8,128)(2,1)S(1)}, bf16[512,1024]{1,0:T(8,128)(2,1)}, u32[]{:S(2)}, u32[]{:S(2)}) collective-permute-start(bf16[512,1024]{1,0:T(8,128)(2,1)S(1)} %get-tuple-element.319.refs_3_), channel_id=1, source_target_pairs={{8,16},{16,8},{9,17},{17,9},{10,18},{18,10},{11,19},{19,11},{12,20... | collective-permute-start | bytes 3145736 | tf_op jit(solution)/shard_map/ppermute | solution.py:273
  392.3 65.2 %all-to-all-start.3 = ((bf16[4,256,1024]{2,1,0:T(8,128)(2,1)}), bf16[4,256,1024]{2,1,0:T(8,128)(2,1)}, u32[]{:S(2)}, u32[]{:S(2)}) async-start(bf16[4,256,1024]{2,1,0:T(8,128)(2,1)} %slice.607), calls=%async_computation.3 | async-start | bytes 4194304 | tf_op jit(solution)/shard_map/all_to_all | solution.py:947
  402.5 25.6 %collective-permute-start.49 = (bf16[128,1024]{1,0:T(8,128)(2,1)S(1)}, bf16[128,1024]{1,0:T(8,128)(2,1)S(1)}, u32[]{:S(2)}, u32[]{:S(2)}) collective-permute-start(bf16[128,1024]{1,0:T(8,128)(2,1)S(1)} %fusion.50), channel_id=1, source_target_pairs={{0,2},{1,3},{2,0},{3,1},{4,6},{5,7},{6,4},{7,5},{8,10},{9,11},{10,... | collective-permute-start | bytes 786440 | tf_op jit(solution)/shard_map/ppermute | solution.py:49
  435.6 38.8 %collective-permute-start.71 = (bf16[512,1024]{1,0:T(8,128)(2,1)}, bf16[512,1024]{1,0:T(8,128)(2,1)S(1)}, u32[]{:S(2)}, u32[]{:S(2)}) collective-permute-start(bf16[512,1024]{1,0:T(8,128)(2,1)} %get-tuple-element.322.refs_5_), channel_id=1, source_target_pairs={{0,8},{24,16},{8,0},{16,24},{1,9},{25,17},{9,1},{17,25},{2,10},{26... | collective-permute-start | bytes 3145736 | tf_op jit(solution)/shard_map/ppermute | solution.py:271
  470.0 28.8 %all-to-all-start.4 = ((bf16[4,64,1024]{2,1,0:T(8,128)(2,1)}), bf16[4,64,1024]{2,1,0:T(8,128)(2,1)}, u32[]{:S(2)}, u32[]{:S(2)}) async-start(bf16[4,64,1024]{2,1,0:T(8,128)(2,1)} %bitcast.380), calls=%async_computation.4 | async-start | bytes 1048576 | tf_op jit(solution)/shard_map/all_to_all | solution.py:961
  486.7 27.7 %collective-permute-start.74 = (bf16[512,1024]{1,0:T(8,128)(2,1)S(1)}, bf16[512,1024]{1,0:T(8,128)(2,1)}, u32[]{:S(2)}, u32[]{:S(2)}) collective-permute-start(bf16[512,1024]{1,0:T(8,128)(2,1)S(1)} %get-tuple-element.327.refs_5_), channel_id=1, source_target_pairs={{0,8},{24,16},{8,0},{16,24},{1,9},{25,17},{9,1},{17,25},{2,10},{26... | collective-permute-start | bytes 3145736 | tf_op jit(solution)/shard_map/ppermute | solution.py:271
  498.8 80.2 %all-to-all-start.5 = ((bf16[4,512,1024]{2,1,0:T(8,128)(2,1)}), bf16[4,512,1024]{2,1,0:T(8,128)(2,1)}, u32[]{:S(2)}, u32[]{:S(2)}) async-start(bf16[4,512,1024]{2,1,0:T(8,128)(2,1)} %bitcast.371), calls=%async_computation.5 | async-start | bytes 8388608 | tf_op jit(solution)/shard_map/all_to_all | solution.py:947
  573.0 48.6 %collective-permute-start.83 = (bf16[512,1024]{1,0:T(8,128)(2,1)}, bf16[512,1024]{1,0:T(8,128)(2,1)}, u32[]{:S(2)}, u32[]{:S(2)}) collective-permute-start(bf16[512,1024]{1,0:T(8,128)(2,1)} %get-tuple-element.347.refs_5_), channel_id=1, source_target_pairs={{0,8},{24,16},{8,0},{16,24},{1,9},{25,17},{9,1},{17,25},{2,10},{26... | collective-permute-start | bytes 3145736 | tf_op jit(solution)/shard_map/ppermute | solution.py:271
  575.7 45.9 %collective-permute-start.84 = (bf16[512,1024]{1,0:T(8,128)(2,1)}, bf16[512,1024]{1,0:T(8,128)(2,1)}, u32[]{:S(2)}, u32[]{:S(2)}) collective-permute-start(bf16[512,1024]{1,0:T(8,128)(2,1)} %get-tuple-element.348.refs_3_), channel_id=1, source_target_pairs={{8,16},{16,8},{9,17},{17,9},{10,18},{18,10},{11,19},{19,11},{12,20... | collective-permute-start | bytes 3145736 | tf_op jit(solution)/shard_map/ppermute | solution.py:273
  577.3 44.3 %collective-permute-start.85 = (bf16[512,1024]{1,0:T(8,128)(2,1)}, bf16[512,1024]{1,0:T(8,128)(2,1)}, u32[]{:S(2)}, u32[]{:S(2)}) collective-permute-start(bf16[512,1024]{1,0:T(8,128)(2,1)} %get-tuple-element.349), channel_id=1, source_target_pairs={{0,4},{4,0},{1,5},{5,1},{2,6},{6,2},{3,7},{7,3},{8,12},{12,8},{9,1... | collective-permute-start | bytes 3145736 | tf_op jit(solution)/shard_map/ppermute | solution.py:276
  614.3 54.8 %all-to-all-start.6 = ((bf16[4,128,1024]{2,1,0:T(8,128)(2,1)}), bf16[4,128,1024]{2,1,0:T(8,128)(2,1)}, u32[]{:S(2)}, u32[]{:S(2)}) async-start(bf16[4,128,1024]{2,1,0:T(8,128)(2,1)} %slice.609), calls=%async_computation.6 | async-start | bytes 2097152 | tf_op jit(solution)/shard_map/all_to_all | solution.py:881
  624.4 29.7 %collective-permute-start.86 = (bf16[512,1024]{1,0:T(8,128)(2,1)S(1)}, bf16[512,1024]{1,0:T(8,128)(2,1)S(1)}, u32[]{:S(2)}, u32[]{:S(2)}) collective-permute-start(bf16[512,1024]{1,0:T(8,128)(2,1)S(1)} %get-tuple-element.354.refs_5_), channel_id=1, source_target_pairs={{0,8},{24,16},{8,0},{16,24},{1,9},{25,17},{9,1},{17,25},{2,10},{26... | collective-permute-start | bytes 3145736 | tf_op jit(solution)/shard_map/ppermute | solution.py:271
  627.1 26.9 %collective-permute-start.87 = (bf16[512,1024]{1,0:T(8,128)(2,1)S(1)}, bf16[512,1024]{1,0:T(8,128)(2,1)S(1)}, u32[]{:S(2)}, u32[]{:S(2)}) collective-permute-start(bf16[512,1024]{1,0:T(8,128)(2,1)S(1)} %get-tuple-element.355.refs_3_), channel_id=1, source_target_pairs={{8,16},{16,8},{9,17},{17,9},{10,18},{18,10},{11,19},{19,11},{12,20... | collective-permute-start | bytes 3145736 | tf_op jit(solution)/shard_map/ppermute | solution.py:273
  627.9 26.2 %collective-permute-start.88 = (bf16[512,1024]{1,0:T(8,128)(2,1)S(1)}, bf16[512,1024]{1,0:T(8,128)(2,1)S(1)}, u32[]{:S(2)}, u32[]{:S(2)}) collective-permute-start(bf16[512,1024]{1,0:T(8,128)(2,1)S(1)} %get-tuple-element.356), channel_id=1, source_target_pairs={{0,4},{4,0},{1,5},{5,1},{2,6},{6,2},{3,7},{7,3},{8,12},{12,8},{9,1... | collective-permute-start | bytes 3145736 | tf_op jit(solution)/shard_map/ppermute | solution.py:276
  658.7 29.8 %collective-permute-start.89 = (bf16[512,1024]{1,0:T(8,128)(2,1)}, bf16[512,1024]{1,0:T(8,128)(2,1)}, u32[]{:S(2)}, u32[]{:S(2)}) collective-permute-start(bf16[512,1024]{1,0:T(8,128)(2,1)} %get-tuple-element.360.refs_5_), channel_id=1, source_target_pairs={{0,8},{24,16},{8,0},{16,24},{1,9},{25,17},{9,1},{17,25},{2,10},{26... | collective-permute-start | bytes 3145736 | tf_op jit(solution)/shard_map/ppermute | solution.py:271
  669.1 35.7 %all-to-all-start.7 = ((bf16[4,64,1024]{2,1,0:T(8,128)(2,1)}), bf16[4,64,1024]{2,1,0:T(8,128)(2,1)}, u32[]{:S(2)}, u32[]{:S(2)}) async-start(bf16[4,64,1024]{2,1,0:T(8,128)(2,1)} %slice.608), calls=%async_computation.7 | async-start | bytes 1048576 | tf_op jit(solution)/shard_map/all_to_all | solution.py:881
  693.6 30.3 %collective-permute-start.92 = (bf16[512,1024]{1,0:T(8,128)(2,1)}, bf16[512,1024]{1,0:T(8,128)(2,1)}, u32[]{:S(2)}, u32[]{:S(2)}) collective-permute-start(bf16[512,1024]{1,0:T(8,128)(2,1)} %get-tuple-element.367.refs_5_), channel_id=1, source_target_pairs={{0,8},{24,16},{8,0},{16,24},{1,9},{25,17},{9,1},{17,25},{2,10},{26... | collective-permute-start | bytes 3145736 | tf_op jit(solution)/shard_map/ppermute | solution.py:271
  711.9 30.7 %all-to-all-start.8 = ((bf16[4,512,384]{2,1,0:T(8,128)(2,1)}), bf16[4,512,384]{2,1,0:T(8,128)(2,1)}, u32[]{:S(2)}, u32[]{:S(2)}) async-start(bf16[4,512,384]{2,1,0:T(8,128)(2,1)} %bitcast.379), calls=%async_computation.8 | async-start | bytes 3145728 | tf_op jit(solution)/shard_map/all_to_all | solution.py:947
  723.4 50.1 %collective-permute-start.62 = (bf16[512,2048]{1,0:T(8,128)(2,1)}, bf16[512,2048]{1,0:T(8,128)(2,1)}, u32[]{:S(2)}, u32[]{:S(2)}) collective-permute-start(bf16[512,2048]{1,0:T(8,128)(2,1)} %convolution_convert_fusion.4), channel_id=1, source_target_pairs={{0,1},{1,0},{2,3},{3,2},{4,5},{5,4},{6,7},{7,6},{8,9},{9,8},{10,11... | collective-permute-start | bytes 6291464 | tf_op jit(solution)/shard_map/ppermute | solution.py:49
  728.0 27.0 %collective-permute-start.95 = (bf16[512,1024]{1,0:T(8,128)(2,1)}, bf16[512,1024]{1,0:T(8,128)(2,1)}, u32[]{:S(2)}, u32[]{:S(2)}) collective-permute-start(bf16[512,1024]{1,0:T(8,128)(2,1)} %get-tuple-element.374.refs_5_), channel_id=1, source_target_pairs={{0,8},{24,16},{8,0},{16,24},{1,9},{25,17},{9,1},{17,25},{2,10},{26... | collective-permute-start | bytes 3145736 | tf_op jit(solution)/shard_map/ppermute | solution.py:271
  732.9 25.2 %collective-permute-start.97 = (bf16[512,1024]{1,0:T(8,128)(2,1)}, bf16[512,1024]{1,0:T(8,128)(2,1)}, u32[]{:S(2)}, u32[]{:S(2)}) collective-permute-start(bf16[512,1024]{1,0:T(8,128)(2,1)} %get-tuple-element.376), channel_id=1, source_target_pairs={{0,4},{4,0},{1,5},{5,1},{2,6},{6,2},{3,7},{7,3},{8,12},{12,8},{9,1... | collective-permute-start | bytes 3145736 | tf_op jit(solution)/shard_map/ppermute | solution.py:276
  787.1 40.9 %collective-permute-start.101 = (bf16[512,1024]{1,0:T(8,128)(2,1)S(1)}, bf16[512,1024]{1,0:T(8,128)(2,1)S(1)}, u32[]{:S(2)}, u32[]{:S(2)}) collective-permute-start(bf16[512,1024]{1,0:T(8,128)(2,1)S(1)} %get-tuple-element.387.refs_5_), channel_id=1, source_target_pairs={{0,8},{24,16},{8,0},{16,24},{1,9},{25,17},{9,1},{17,25},{2,10},{26... | collective-permute-start | bytes 3145736 | tf_op jit(solution)/shard_map/ppermute | solution.py:271
  790.3 37.7 %collective-permute-start.102 = (bf16[512,1024]{1,0:T(8,128)(2,1)S(1)}, bf16[512,1024]{1,0:T(8,128)(2,1)S(1)}, u32[]{:S(2)}, u32[]{:S(2)}) collective-permute-start(bf16[512,1024]{1,0:T(8,128)(2,1)S(1)} %get-tuple-element.388.refs_3_), channel_id=1, source_target_pairs={{8,16},{16,8},{9,17},{17,9},{10,18},{18,10},{11,19},{19,11},{12,20... | collective-permute-start | bytes 3145736 | tf_op jit(solution)/shard_map/ppermute | solution.py:273
  791.0 37.0 %collective-permute-start.103 = (bf16[512,1024]{1,0:T(8,128)(2,1)S(1)}, bf16[512,1024]{1,0:T(8,128)(2,1)S(1)}, u32[]{:S(2)}, u32[]{:S(2)}) collective-permute-start(bf16[512,1024]{1,0:T(8,128)(2,1)S(1)} %get-tuple-element.389), channel_id=1, source_target_pairs={{0,4},{4,0},{1,5},{5,1},{2,6},{6,2},{3,7},{7,3},{8,12},{12,8},{9,1... | collective-permute-start | bytes 3145736 | tf_op jit(solution)/shard_map/ppermute | solution.py:276
  795.5 29.3 %collective-permute-start.63 = (bf16[2,128,1024]{2,1,0:T(8,128)(2,1)S(1)}, bf16[2,128,1024]{2,1,0:T(8,128)(2,1)S(1)}, u32[]{:S(2)}, u32[]{:S(2)}) collective-permute-start(bf16[2,128,1024]{2,1,0:T(8,128)(2,1)S(1)} %slice.1027), channel_id=1, source_target_pairs={{0,4},{1,5},{2,6},{3,7},{4,0},{5,1},{6,2},{7,3},{8,12},{9,13},{10,... | collective-permute-start | bytes 1572872 | tf_op jit(solution)/shard_map/ppermute | solution.py:49
  795.9 28.9 %collective-permute-start.64 = (bf16[2,128,1024]{2,1,0:T(8,128)(2,1)S(1)}, bf16[2,128,1024]{2,1,0:T(8,128)(2,1)S(1)}, u32[]{:S(2)}, u32[]{:S(2)}) collective-permute-start(bf16[2,128,1024]{2,1,0:T(8,128)(2,1)S(1)} %slice.620), channel_id=1, source_target_pairs={{0,2},{1,3},{2,0},{3,1},{4,6},{5,7},{6,4},{7,5},{8,10},{9,11},{10,... | collective-permute-start | bytes 1572872 | tf_op jit(solution)/shard_map/ppermute | solution.py:49
  830.4 26.1 %collective-permute-start.106 = (bf16[512,1024]{1,0:T(8,128)(2,1)S(1)}, bf16[512,1024]{1,0:T(8,128)(2,1)S(1)}, u32[]{:S(2)}, u32[]{:S(2)}) collective-permute-start(bf16[512,1024]{1,0:T(8,128)(2,1)S(1)} %get-tuple-element.396), channel_id=1, source_target_pairs={{0,4},{4,0},{1,5},{5,1},{2,6},{6,2},{3,7},{7,3},{8,12},{12,8},{9,1... | collective-permute-start | bytes 3145736 | tf_op jit(solution)/shard_map/ppermute | solution.py:276
  833.0 25.4 %collective-permute-start.65 = (bf16[128,1024]{1,0:T(8,128)(2,1)S(1)}, bf16[128,1024]{1,0:T(8,128)(2,1)S(1)}, u32[]{:S(2)}, u32[]{:S(2)}) collective-permute-start(bf16[128,1024]{1,0:T(8,128)(2,1)S(1)} %fusion.54), channel_id=1, source_target_pairs={{0,2},{1,3},{2,0},{3,1},{4,6},{5,7},{6,4},{7,5},{8,10},{9,11},{10,... | collective-permute-start | bytes 786440 | tf_op jit(solution)/shard_map/ppermute | solution.py:49
  835.9 26.2 %collective-permute-start.66 = (bf16[128,1024]{1,0:T(8,128)(2,1)S(1)}, bf16[128,1024]{1,0:T(8,128)(2,1)S(1)}, u32[]{:S(2)}, u32[]{:S(2)}) collective-permute-start(bf16[128,1024]{1,0:T(8,128)(2,1)S(1)} %fusion.55), channel_id=1, source_target_pairs={{0,4},{1,5},{2,6},{3,7},{4,0},{5,1},{6,2},{7,3},{8,12},{9,13},{10,... | collective-permute-start | bytes 786440 | tf_op jit(solution)/shard_map/ppermute | solution.py:49
  856.6 31.7 %collective-permute-start.109 = (bf16[512,1024]{1,0:T(8,128)(2,1)S(1)}, bf16[512,1024]{1,0:T(8,128)(2,1)S(1)}, u32[]{:S(2)}, u32[]{:S(2)}) collective-permute-start(bf16[512,1024]{1,0:T(8,128)(2,1)S(1)} %get-tuple-element.403.refs_0_), channel_id=1, source_target_pairs={{0,4},{4,0},{1,5},{5,1},{2,6},{6,2},{3,7},{7,3},{8,12},{12,8},{9,1... | collective-permute-start | bytes 3145736 | tf_op jit(solution)/shard_map/ppermute | solution.py:276
  862.1 26.3 %collective-permute-start.107 = (bf16[384,1024]{1,0:T(8,128)(2,1)S(1)}, bf16[384,1024]{1,0:T(8,128)(2,1)S(1)}, u32[]{:S(2)}, u32[]{:S(2)}) collective-permute-start(bf16[384,1024]{1,0:T(8,128)(2,1)S(1)} %get-tuple-element.401.refs_3_), channel_id=1, source_target_pairs={{8,0},{16,24},{9,1},{17,25},{10,2},{18,26},{11,3},{19,27},{12,4},{... | collective-permute-start | bytes 2359304 | tf_op jit(solution)/shard_map/ppermute | solution.py:271
  (165 other events, 2295.5 us)
